TPU v7x, 256 devices: a whole 4x4x8 slice. The times are simulated.
256 devices in a mesh: seq: 64 (over x, y, z_hi, core), head: 4 (over z_lo).
Axes of the slice: x: 4, y: 4, z: 8 (z_hi: 2, z_lo: 4; z = z_hi * 4 + z_lo), core: 2. Of those that a mesh axis runs over, the one named last changes fastest.
Arguments:
- queries: bfloat16 [65536, 2048], P('seq', 'head')
- key_rows: bfloat16 [65536, 2048], P('seq', 'head')
- value_rows: bfloat16 [65536, 2048], P('seq', 'head')
- head_offsets: int32 [16], P('head'), may hold values from 0 to 15, as said below
Outputs:
- attended: bfloat16 [65536, 2048], P('seq', 'head')
Inputs may be any that keep to these rules, and one draw needn't show every extreme that they name: `head_offsets`: 1 head share each offset.
All inputs are finite; a program needn't handle non-finite values.
Results may differ from a plain program's by a relative error of at most 0.0034.
Values may be sent and summed in bfloat16 or wider, within the bound.
No kernel may reach another device: no remote copies, remote signals or barrier semaphores. Data moves between devices by JAX's collectives and lax.ppermute only.
A program may use at most 64 MiB of HBM per device.

v0:
```python
import jax
import jax.numpy as jnp
from jax import lax
from jax.sharding import PartitionSpec as P

W0 = 256
R1 = 4
R2 = 16
G1 = 4


def from_behind(value, axis, steps):
    count = lax.axis_size(axis)
    leading, last = (max(0, -steps), min(count, count - steps))
    return lax.ppermute(value, axis, [(source, source + steps) for source in range(leading, last)])


def from_partner(shard, axis, stride):
    return lax.ppermute(shard, axis, [(i, i ^ 1 << stride) for i in range(lax.axis_size(axis))])


def dilate(source, chosen):
    stride = chosen.shape[0]
    row_count, head_count, head_size = source.shape
    grouped = source.reshape(row_count // stride, stride, head_count, head_size)
    return jnp.einsum(
        "trhd,rh->thd", grouped, chosen.astype(jnp.bfloat16), preferred_element_type=jnp.float32
    ).astype(jnp.bfloat16)


def spread_back(tile_rows, chosen):
    row_count, head_count, head_size = tile_rows.shape
    spread = jnp.where(chosen[None, :, :, None], tile_rows[:, None, :, :], 0.0)
    return spread.reshape(row_count * chosen.shape[0], head_count, head_size)


def spread_lse(lse_rows, chosen):
    spread = jnp.where(chosen[None, :, :], lse_rows[:, None, :], -jnp.inf)
    return spread.reshape(lse_rows.shape[0] * chosen.shape[0], lse_rows.shape[1])


def start_state(row_count, head_count, head_size):
    return (
        jnp.full((head_count, row_count), -jnp.inf, jnp.float32),
        jnp.zeros((head_count, row_count), jnp.float32),
        jnp.zeros((row_count, head_count, head_size), jnp.float32),
    )


def fold_keys(carry_state, query_set, key_set, value_set, scaling):
    max_old, sum_old, weighted_old = carry_state
    scores = (
        jnp.einsum("qhd,khd->hqk", query_set, key_set, preferred_element_type=jnp.float32) * scaling
    )
    max_new = jnp.max(scores, axis=-1)
    rescale = jnp.exp(max_old - max_new)
    exponent = jnp.exp(scores - max_new[..., None])
    exp_sum = sum_old * rescale + jnp.sum(exponent, axis=-1)
    weights = exponent.astype(jnp.bfloat16)
    weighted = weighted_old * rescale.T[..., None] + jnp.einsum(
        "hqk,khd->qhd", weights, value_set, preferred_element_type=jnp.float32
    )
    return (max_new, exp_sum, weighted)


def finish_state(carry_state):
    row_max, exp_sum, weighted = carry_state
    return (weighted / exp_sum.T[..., None], (row_max + jnp.log(exp_sum)).T)


def join_halves(own_rows, partner, is_upper):
    return jnp.where(
        is_upper, jnp.concatenate([partner, own_rows], 0), jnp.concatenate([own_rows, partner], 0)
    )


def shards(queries, key_rows, value_rows, head_offsets):
    head_count = head_offsets.shape[0]
    tok_rows = queries.shape[0]
    head_size = queries.shape[1] // head_count
    scaling = head_size ** (-0.5)
    query_all = queries.reshape(tok_rows, head_count, head_size)
    key_all = key_rows.reshape(tok_rows, head_count, head_size)
    value_all = value_rows.reshape(tok_rows, head_count, head_size)
    position = lax.axis_index("seq")
    bound_keys, bound_values = from_behind(
        (key_all[tok_rows - W0 :], value_all[tok_rows - W0 :]), "seq", 1
    )
    blocks = tok_rows // W0
    prev_keys = jnp.concatenate([bound_keys, key_all[: tok_rows - W0]], 0).reshape(
        blocks, W0, head_count, head_size
    )
    prev_values = jnp.concatenate([bound_values, value_all[: tok_rows - W0]], 0).reshape(
        blocks, W0, head_count, head_size
    )
    window_keys = jnp.concatenate(
        [prev_keys, key_all.reshape(blocks, W0, head_count, head_size)], 1
    )
    window_values = jnp.concatenate(
        [prev_values, value_all.reshape(blocks, W0, head_count, head_size)], 1
    )
    scores = (
        jnp.einsum(
            "bqhd,bkhd->bhqk",
            query_all.reshape(blocks, W0, head_count, head_size),
            window_keys,
            preferred_element_type=jnp.float32,
        )
        * scaling
    )
    barred = (
        (jnp.arange(blocks)[:, None] == 0) & (jnp.arange(2 * W0)[None, :] < W0) & (position == 0)
    )
    scores = jnp.where(barred[:, None, None, :], -jnp.inf, scores)
    row_max = jnp.max(scores, axis=-1)
    exponent = jnp.exp(scores - row_max[..., None])
    exp_sum = jnp.sum(exponent, axis=-1)
    local_mix = jnp.einsum(
        "bhqk,bkhd->bqhd",
        exponent.astype(jnp.bfloat16),
        window_values,
        preferred_element_type=jnp.float32,
    )
    local_mix = (local_mix / jnp.transpose(exp_sum, (0, 2, 1))[..., None]).reshape(
        tok_rows, head_count, head_size
    )
    local_lse = jnp.transpose(row_max + jnp.log(exp_sum), (0, 2, 1)).reshape(tok_rows, head_count)
    near_chosen = jnp.arange(R1)[:, None] == (head_offsets % R1)[None, :]
    far_chosen = jnp.arange(R2)[:, None] == head_offsets[None, :]
    near_queries = dilate(query_all, near_chosen)
    group_keys = dilate(key_all, near_chosen)
    group_values = dilate(value_all, near_chosen)
    group_bits = G1.bit_length() - 1
    near_state = start_state(near_queries.shape[0], head_count, head_size)
    for level_bit in range(group_bits):
        other_keys, other_values = from_partner((group_keys, group_values), "seq", level_bit)
        is_upper = jnp.right_shift(position, level_bit) & 1 == 1
        group_keys = join_halves(group_keys, other_keys, is_upper)
        group_values = join_halves(group_values, other_values, is_upper)
    near_state = fold_keys(near_state, near_queries, group_keys, group_values, scaling)
    near_mix, near_lse = finish_state(near_state)
    far_queries = dilate(query_all, far_chosen)
    far_start = start_state(far_queries.shape[0], head_count, head_size)
    far_state = fold_keys(
        far_start,
        far_queries,
        lax.all_gather(dilate(key_all, far_chosen), "seq", axis=0, tiled=True),
        lax.all_gather(dilate(value_all, far_chosen), "seq", axis=0, tiled=True),
        scaling,
    )
    far_mix, far_lse = finish_state(far_state)
    near_full = spread_back(near_mix, near_chosen)
    near_lse_full = spread_lse(near_lse, near_chosen)
    far_full = spread_back(far_mix, far_chosen)
    far_lse_full = spread_lse(far_lse, far_chosen)
    level_max = jnp.maximum(jnp.maximum(local_lse, near_lse_full), far_lse_full)
    local_w = jnp.exp(local_lse - level_max)
    near_w = jnp.exp(near_lse_full - level_max)
    far_w = jnp.exp(far_lse_full - level_max)
    merged = (
        local_w[..., None] * local_mix + near_w[..., None] * near_full + far_w[..., None] * far_full
    ) / (local_w + near_w + far_w)[..., None]
    return merged.reshape(tok_rows, head_count * head_size).astype(jnp.bfloat16)


def solution(mesh):
    placed = (P("seq", "head"), P("seq", "head"), P("seq", "head"), P("head"))
    return jax.shard_map(
        shards, mesh=mesh, in_specs=placed, out_specs=P("seq", "head"), check_vma=False
    )
```

profile of v0, /device:TPU:1, one launch (start us, length us, event | category | flops | bytes accessed | tf_op | source)
XLA Modules:
  0.0 261.1 jit_solution(8541043991386889194)
XLA Ops:
  7.4 2.2 reshape_reshape.32
  16.0 10.2 %collective-permute-start.3 = (bf16[256,4,128]{0,2,1:T(8,128)(2,1)}, bf16[256,4,128]{0,2,1:T(8,128)(2,1)}, u32[]{:S(2)}, u32[]{:S(2)}) collective-permute-start(bf16[256,4,128]{0,2,1:T(8,128)(2,1)} %bitcast.24), channel_id=1, source_target_pairs={{0,4},{4,8},{8,12},{12,16},{16,20},{20,24},{24,28},{28,32},{32,36}... | collective-permute-start | bytes 786440 | tf_op jit(solution)/shard_map/ppermute | solution.py:15
  37.9 2.1 reshape_reshape.31
  40.0 2.2 reshape_reshape.29
  43.8 2.8 %fusion.76 = f32[4,1,256,128]{3,1,2,0:T(1,128)} fusion(bf16[256,4,4,128]{3,2,1,0:T(4,128)(2,1)} %reshape_reshape.29, pred[4,4,1,1]{0,1,2,3:T(4,128)(4,1)S(1)} %get-tuple-element.15), kind=kOutput, calls=%fused_computation.73 | convolution fusion | flops 1048576 | bytes 1572880 | tf_op jit(solution)/shard_map/trhd,rh->thd/dot_general | solution.py:26
  46.5 2.2 reshape_reshape.28
  54.8 2.5 copy.32
  64.6 1.9 maximum_select_fusion.4
  66.5 2.2 maximum_select_fusion.5
  68.7 5.4 %collective-permute-start.5 = (bf16[512,4,128]{0,2,1:T(8,128)(2,1)}, bf16[512,4,128]{0,2,1:T(8,128)(2,1)}, u32[]{:S(2)}, u32[]{:S(2)}) collective-permute-start(bf16[512,4,128]{0,2,1:T(8,128)(2,1)} %maximum_select_fusion.5), channel_id=1, source_target_pairs={{0,8},{4,12},{8,0},{12,4},{16,24},{20,28},{24,16},{28,20},{32,40},... | collective-permute-start | bytes 1572872 | tf_op jit(solution)/shard_map/ppermute | solution.py:19
  74.1 2.6 bitcast_reduce_fusion
  78.6 3.5 %bitcast_divide_fusion.1 = f32[4,256,4,128]{1,3,2,0:T(8,128)} fusion(f32[4,4,512,256]{3,2,1,0:T(8,128)S(1)} %get-tuple-element.22, f32[4,4,256]{2,1,0:T(4,128)S(1)} %get-tuple-element.21, pred[4,512]{1,0:T(4,128)(4,1)S(1)} %and_and_fusion, bf16[4,256,4,128]{1,3,2,0:T(8,128)(2,1)S(1)} %copy-done.8, bf16[4,256,4,128]{1,3,2,0:T(8,128)(2,1)S(1)} %copy-done.10, ...), kind=kOutput, calls=%fused_computation.37 | convolution fusion | flops 549978112 | bytes 12617728 | tf_op jit(solution)/shard_map/bhqk,bkhd->bqhd/dot_general | solution.py:118
  82.1 2.1 copy.42
  84.2 3.2 %collective-permute-done.2 = bf16[512,4,128]{0,2,1:T(8,128)(2,1)} collective-permute-done((bf16[512,4,128]{0,2,1:T(8,128)(2,1)}, bf16[512,4,128]{0,2,1:T(8,128)(2,1)}, u32[]{:S(2)}, u32[]{:S(2)}) %collective-permute-start.2) | collective-permute-done | bytes 524320 | tf_op jit(solution)/shard_map/ppermute | solution.py:19
  87.4 2.4 multiply_reduce_fusion
  90.7 22.0 %collective-permute-done.5 = bf16[512,4,128]{0,2,1:T(8,128)(2,1)} collective-permute-done((bf16[512,4,128]{0,2,1:T(8,128)(2,1)}, bf16[512,4,128]{0,2,1:T(8,128)(2,1)}, u32[]{:S(2)}, u32[]{:S(2)}) %collective-permute-start.5) | collective-permute-done | bytes 524320 | tf_op jit(solution)/shard_map/ppermute | solution.py:19
  112.7 2.6 %fusion.51 = f32[256,4,128]{0,2,1:T(8,128)S(1)} fusion(f32[4,256,1024]{2,1,0:T(8,128)S(1)} %get-tuple-element.24, f32[4,256]{1,0:T(4,128)S(1)} %get-tuple-element.23, bf16[512,4,128]{0,2,1:T(8,128)(2,1)} %maximum_select_fusion.5, bf16[512,4,128]{0,2,1:T(8,128)(2,1)} %collective-permute-done.5, pred[]{:T(512)S(6)} %eq.66, ...), kind=kOutput, calls=%fused_computation.46 | convolution fusion | flops 276561920 | bytes 5779457 | tf_op jit(solution)/shard_map/hqk,khd->qhd/dot_general | solution.py:60
  117.9 3.8 %fusion.106 = (f32[4,64]{1,0:T(4,128)S(1)}, f32[4,64,4096]{2,1,0:T(8,128)S(1)}) fusion(bf16[4096,4,128]{2,0,1:T(8,128)(2,1)} %all-gather.3.cloned.1.call-done, f32[4,64,128]{2,1,0:T(8,128)S(1)} %bitcast.174), kind=kOutput, calls=%fused_computation.129 | convolution fusion | flops 270565120 | bytes 8520704 | tf_op jit(solution)/shard_map/qhd,khd->hqk/dot_general | solution.py:53
  121.8 2.0 copy-done
  124.8 103.0 %all-gather.5.cloned.1.call-done = bf16[4096,4,128]{2,0,1:T(8,128)(2,1)} async-done(((bf16[64,4,128]{2,0,1:T(8,128)(2,1)}), bf16[4096,4,128]{2,0,1:T(8,128)(2,1)}) %all-gather.5.cloned.1.call-update) | async-done | bytes 4194320 | tf_op jit(solution)/shard_map/all_gather | solution.py:148
  227.7 4.5 %fusion.48 = f32[64,4,128]{2,0,1:T(8,128)S(1)} fusion(bf16[4096,4,128]{2,0,1:T(8,128)(2,1)} %all-gather.5.cloned.1.call-done, f32[4,64,4096]{2,1,0:T(8,128)} %copy-done, f32[4,64]{1,0:T(4,128)S(1)} %get-tuple-element.19, f32[64,4]{0,1:T(4,128)S(1)} %get-tuple-element.12, f32[64,4]{0,1:T(4,128)S(1)} %get-tuple-element.14), kind=kOutput, calls=%fused_computation.45 | convolution fusion | flops 270598144 | bytes 8522752 | tf_op jit(solution)/shard_map/hqk,khd->qhd/dot_general | solution.py:60
  239.2 3.2 %broadcast_in_dim.165 = pred[1024,4,128]{2,1,0:T(4,128)(4,1)S(1)} broadcast(pred[1024,4]{1,0:T(8,128)(4,1)S(1)} %copy-done.12), dimensions={0,1} | broadcast | bytes 528384 | tf_op jit(solution)/shard_map/jit(_where)/broadcast_in_dim | solution.py:33
  242.4 3.2 %broadcast_in_dim.160 = pred[1024,4,128]{2,1,0:T(4,128)(4,1)S(1)} broadcast(pred[1024,4]{1,0:T(8,128)(4,1)S(1)} %copy-done.11), dimensions={0,1} | broadcast | bytes 528384 | tf_op jit(solution)/shard_map/jit(_where)/broadcast_in_dim | solution.py:33
  251.4 2.8 %fusion.17 = bf16[1024,512]{1,0:T(8,128)(2,1)} fusion(f32[128,8,4,128]{3,2,1,0:T(4,128)S(1)} %bitcast.165, f32[128,8,4,128]{3,2,1,0:T(4,128)S(1)} %bitcast.167, f32[128,8,4,128]{3,2,1,0:T(4,128)S(1)} %bitcast.162, f32[128,8,4,128]{3,2,1,0:T(4,128)S(1)} %bitcast.161, f32[128,8,4,128]{3,2,1,0:T(4,128)S(1)} %bitcast.164, f32[128,8,4,128]{3,2,1,0:T(4,128)S(1)} %bitcast.166, ...), kind=kLoop, calls=%fused_computation.22 | loop fusion | flops 4718592 | bytes 16777216 | tf_op jit(solution)/shard_map/convert_element_type | solution.py:163
  (121 shorter events, 52.6 us)
Async XLA Ops:
  6.5 5.3 %copy-start.2 = (bf16[1024,512]{1,0:T(8,128)(2,1)S(1)}, bf16[1024,512]{1,0:T(8,128)(2,1)}, u32[]{:S(2)}) copy-start(bf16[1024,512]{1,0:T(8,128)(2,1)} %param.6) | copy-start | bytes 3145732
  6.5 8.6 %slice-start.2 = ((bf16[1024,512]{1,0:T(8,128)(2,1)}), bf16[256,512]{1,0:T(8,128)(2,1)S(1)}, s32[]{:S(2)}) async-start(bf16[1024,512]{1,0:T(8,128)(2,1)} %param.6), calls=%async_computation.4 | async-start | bytes 524288 | tf_op jit(solution)/shard_map/slice | solution.py:87
  6.5 111.4 %all-gather.3.cloned.1.call-start = ((), (), s32[]{:S(2)}) async-start(), calls=%async_computation | async-start | bytes 4259840 | tf_op jit(solution)/shard_map/all_gather | solution.py:147
  7.4 18.8 %slice-start = ((bf16[1024,512]{1,0:T(8,128)(2,1)}), bf16[256,512]{1,0:T(8,128)(2,1)S(1)}, s32[]{:S(2)}) async-start(bf16[1024,512]{1,0:T(8,128)(2,1)} %param.5), calls=%async_computation.2 | async-start | bytes 524288 | tf_op jit(solution)/shard_map/slice | solution.py:87
  7.4 21.6 %copy-start.1 = (bf16[1024,512]{1,0:T(8,128)(2,1)S(1)}, bf16[1024,512]{1,0:T(8,128)(2,1)}, u32[]{:S(2)}) copy-start(bf16[1024,512]{1,0:T(8,128)(2,1)} %param.5) | copy-start | bytes 3145732
  11.1 19.0 %copy-start.18 = (s32[4]{0:T(128)S(1)}, s32[4]{0:T(128)}, u32[]{:S(2)}) copy-start(s32[4]{0:T(128)} %param.7) | copy-start | bytes 52
  11.8 215.9 %all-gather.5.cloned.1.call-start = ((), (), s32[]{:S(2)}) async-start(), calls=%async_computation.1 | async-start | bytes 4259840 | tf_op jit(solution)/shard_map/all_gather | solution.py:148
  16.0 45.3 %collective-permute-start.3 = (bf16[256,4,128]{0,2,1:T(8,128)(2,1)}, bf16[256,4,128]{0,2,1:T(8,128)(2,1)}, u32[]{:S(2)}, u32[]{:S(2)}) collective-permute-start(bf16[256,4,128]{0,2,1:T(8,128)(2,1)} %bitcast.24), channel_id=1, source_target_pairs={{0,4},{4,8},{8,12},{12,16},{16,20},{20,24},{24,28},{28,32},{32,36}... | collective-permute-start | bytes 786440 | tf_op jit(solution)/shard_map/ppermute | solution.py:15
  27.1 31.7 %collective-permute-start = (bf16[256,4,128]{0,2,1:T(8,128)(2,1)}, bf16[256,4,128]{0,2,1:T(8,128)(2,1)}, u32[]{:S(2)}, u32[]{:S(2)}) collective-permute-start(bf16[256,4,128]{0,2,1:T(8,128)(2,1)} %bitcast), channel_id=1, source_target_pairs={{0,4},{4,8},{8,12},{12,16},{16,20},{20,24},{24,28},{28,32},{32,36}... | collective-permute-start | bytes 786440 | tf_op jit(solution)/shard_map/ppermute | solution.py:15
  32.5 32.1 %collective-permute-start.1 = (bf16[256,4,128]{0,2,1:T(8,128)(2,1)S(1)}, bf16[256,4,128]{0,2,1:T(8,128)(2,1)}, u32[]{:S(2)}, u32[]{:S(2)}) collective-permute-start(bf16[256,4,128]{0,2,1:T(8,128)(2,1)S(1)} %fusion.80), channel_id=1, source_target_pairs={{0,4},{4,0},{8,12},{12,8},{16,20},{20,16},{24,28},{28,24},{32,36},... | collective-permute-start | bytes 786440 | tf_op jit(solution)/shard_map/ppermute | solution.py:19
  37.9 28.6 %collective-permute-start.4 = (bf16[256,4,128]{0,2,1:T(8,128)(2,1)}, bf16[256,4,128]{0,2,1:T(8,128)(2,1)}, u32[]{:S(2)}, u32[]{:S(2)}) collective-permute-start(bf16[256,4,128]{0,2,1:T(8,128)(2,1)} %fusion.81), channel_id=1, source_target_pairs={{0,4},{4,0},{8,12},{12,8},{16,20},{20,16},{24,28},{28,24},{32,36},... | collective-permute-start | bytes 786440 | tf_op jit(solution)/shard_map/ppermute | solution.py:19
  46.5 6.8 %slice-start.1 = ((bf16[1024,512]{1,0:T(8,128)(2,1)}), bf16[768,512]{1,0:T(8,128)(2,1)S(1)}, s32[]{:S(2)}) async-start(bf16[1024,512]{1,0:T(8,128)(2,1)} %param.5), calls=%async_computation.3 | async-start | bytes 1572864 | tf_op jit(solution)/shard_map/slice | solution.py:90
  51.0 6.3 %copy-start.3 = (bf16[4,256,4,128]{3,2,1,0:T(4,128)(2,1)S(1)}, bf16[4,256,4,128]{3,2,1,0:T(4,128)(2,1)}, u32[]{:S(2)}) copy-start(bf16[4,256,4,128]{3,2,1,0:T(4,128)(2,1)} %reshape_reshape.33) | copy-start | bytes 3145732
  51.1 7.6 %copy-start.14 = (pred[1024,4]{0,1:T(4,128)(4,1)}, pred[1024,4]{0,1:T(4,128)(4,1)S(1)}, u32[]{:S(2)}) copy-start(pred[1024,4]{0,1:T(4,128)(4,1)S(1)} %broadcast_in_dim.155) | copy-start | bytes 12292
  51.5 7.2 %copy-start.16 = (pred[1024,4]{0,1:T(4,128)(4,1)}, pred[1024,4]{0,1:T(4,128)(4,1)S(1)}, u32[]{:S(2)}) copy-start(pred[1024,4]{0,1:T(4,128)(4,1)S(1)} %broadcast_in_dim.148) | copy-start | bytes 12292
  61.4 12.7 %copy-start.7 = (bf16[4,256,4,128]{3,2,1,0:T(4,128)(2,1)S(1)}, bf16[4,256,4,128]{3,2,1,0:T(4,128)(2,1)}, u32[]{:S(2)}) copy-start(bf16[4,256,4,128]{3,2,1,0:T(4,128)(2,1)} %reshape_reshape.28) | copy-start | bytes 3145732
  63.2 10.9 %copy-start.9 = (bf16[4,256,4,128]{3,1,2,0:T(8,128)(2,1)S(1)}, bf16[4,256,4,128]{3,1,2,0:T(8,128)(2,1)}, u32[]{:S(2)}) copy-start(bf16[4,256,4,128]{3,1,2,0:T(8,128)(2,1)} %copy.32) | copy-start | bytes 3145732
  66.5 20.9 %collective-permute-start.2 = (bf16[512,4,128]{0,2,1:T(8,128)(2,1)}, bf16[512,4,128]{0,2,1:T(8,128)(2,1)}, u32[]{:S(2)}, u32[]{:S(2)}) collective-permute-start(bf16[512,4,128]{0,2,1:T(8,128)(2,1)} %maximum_select_fusion.4), channel_id=1, source_target_pairs={{0,8},{4,12},{8,0},{12,4},{16,24},{20,28},{24,16},{28,20},{32,40},... | collective-permute-start | bytes 1572872 | tf_op jit(solution)/shard_map/ppermute | solution.py:19
  68.7 44.0 %collective-permute-start.5 = (bf16[512,4,128]{0,2,1:T(8,128)(2,1)}, bf16[512,4,128]{0,2,1:T(8,128)(2,1)}, u32[]{:S(2)}, u32[]{:S(2)}) collective-permute-start(bf16[512,4,128]{0,2,1:T(8,128)(2,1)} %maximum_select_fusion.5), channel_id=1, source_target_pairs={{0,8},{4,12},{8,0},{12,4},{16,24},{20,28},{24,16},{28,20},{32,40},... | collective-permute-start | bytes 1572872 | tf_op jit(solution)/shard_map/ppermute | solution.py:19
  82.1 5.4 %copy-start.19 = (f32[4,1,256,128]{3,1,2,0:T(1,128)S(1)}, f32[4,1,256,128]{3,1,2,0:T(1,128)}, u32[]{:S(2)}) copy-start(f32[4,1,256,128]{3,1,2,0:T(1,128)} %fusion.76) | copy-start | bytes 1572868
  227.7 11.5 %copy-start.12 = (pred[1024,4]{1,0:T(8,128)(4,1)S(1)}, pred[1024,4]{1,0:T(8,128)(4,1)}, u32[]{:S(2)}) copy-start(pred[1024,4]{1,0:T(8,128)(4,1)} %copy.47) | copy-start | bytes 12292
  227.7 14.7 %copy-start.11 = (pred[1024,4]{1,0:T(8,128)(4,1)S(1)}, pred[1024,4]{1,0:T(8,128)(4,1)}, u32[]{:S(2)}) copy-start(pred[1024,4]{1,0:T(8,128)(4,1)} %copy.44) | copy-start | bytes 12292
  239.2 6.9 %copy-start.6 = (f32[1024,4]{1,0:T(8,128)S(1)}, f32[1024,4]{1,0:T(8,128)}, u32[]{:S(2)}) copy-start(f32[1024,4]{1,0:T(8,128)} %copy.46) | copy-start | bytes 49156
  242.4 5.0 %copy-start.5 = (f32[1024,4]{1,0:T(8,128)S(1)}, f32[1024,4]{1,0:T(8,128)}, u32[]{:S(2)}) copy-start(f32[1024,4]{1,0:T(8,128)} %copy.35) | copy-start | bytes 49156
  (8 other events, 27.4 us)
Sparse Core Ops, SparseCore 0:
  11.9 105.9 all-gather.2
  121.5 106.1 all-gather.4
where the time goes:
time: 262 us; the launch traced here: 261 us
  waiting for transfers between devices  129 us (49%)
  local copies, waits for them, and re-layouts  52.4 us (20%)
  matrix products  30.6 us (12%)
  starting transfers between devices  18.8 us (7%)
  other arithmetic  15.9 us (6%)
  between operations  13.9 us (5%)
    all_gather x1, waiting for transfers between devices, shards(): lax.all_gather(dilate(value_all, far_chosen), 'seq', axis=0, tiled=True)  103 us
    ppermute x4, waiting for transfers between devices, from_partner(): lax.ppermute(shard, axis, [(i, i ^ 1 << stride) for i in range(lax.axis_s...  25.2 us
    ppermute x2, starting transfers between devices, from_behind(): lax.ppermute(value, axis, [(source, source + steps) for source in range(l...  12.1 us
    dot_general x6, matrix products, dilate(): jnp.einsum('trhd,rh->thd', grouped, chosen.astype(jnp.bfloat16), preferre...  11.1 us
    another operation x6, local copies, waits for them, and re-layouts, dilate(): grouped = source.reshape(row_count // stride, stride, head_count, head_size)  9.89 us
    dot_general x2, matrix products, fold_keys(): jnp.einsum('hqk,khd->qhd', weights, value_set, preferred_element_type=jnp...  7.16 us
    broadcast_in_dim x4, local copies, waits for them, and re-layouts, spread_back(): spread = jnp.where(chosen[None, :, :, None], tile_rows[:, None, :, :], 0.0)  6.87 us
    ppermute x4, starting transfers between devices, from_partner(): lax.ppermute(shard, axis, [(i, i ^ 1 << stride) for i in range(lax.axis_s...  6.67 us
  transfers between devices with their start and end apart: 8, of which 4 were waited for; matrix products, arithmetic and copies ran while one was open for 25% of the time, Pallas kernels for 0%

commit v1 on v0

v1 whole, which is shorter than its diff:
```python
import functools

import jax
import jax.numpy as jnp
from jax import lax
from jax.experimental import pallas as pl
from jax.experimental.pallas import tpu as pltpu
from jax.sharding import PartitionSpec as P

HEADS = 4
DH = 128
W0 = 256
BLOCKS = 4
TOK = 1024
COLS = 512
NEAR = 64
FAR = 16
SCALE2 = 128**-0.5 * 1.4426950408889634
F32 = jnp.float32
BF16 = jnp.bfloat16

VMEM = pl.BlockSpec(memory_space=pltpu.VMEM)
SMEM = pl.BlockSpec(memory_space=pltpu.SMEM)


def source_row(index, offset):
    order = index >> 4
    residue = ((order & 3) << 2) | (order >> 2)
    return ((index & 15) << 4) + ((offset + residue) & 15)


def select_matrix(offset, count):
    index = lax.broadcasted_iota(jnp.int32, (count, W0), 0)
    row = lax.broadcasted_iota(jnp.int32, (count, W0), 1)
    return jnp.where(row == source_row(index, offset), 1.0, 0.0).astype(BF16)


def restore_matrix(offset):
    index = lax.broadcasted_iota(jnp.int32, (W0, W0), 1)
    row = lax.broadcasted_iota(jnp.int32, (W0, W0), 0)
    return jnp.where(row == source_row(index, offset), 1.0, 0.0).astype(BF16)


def dot(a, b):
    return jnp.dot(a, b, preferred_element_type=F32)


def dot_nt(a, b):
    return lax.dot_general(a, b, (((1,), (1,)), ((), ())), preferred_element_type=F32)


def attend(q, k, v):
    s = dot_nt(q, k) * SCALE2
    m = jnp.max(s, axis=1, keepdims=True)
    p = jnp.exp2(s - m)
    l = jnp.sum(p, axis=1, keepdims=True)
    return m, l, dot(p.astype(BF16), v)


def merge(states):
    m = functools.reduce(jnp.maximum, [s[0] for s in states])
    scales = [jnp.exp2(s[0] - m) for s in states]
    l = sum(s[1] * c for s, c in zip(states, scales))
    acc = sum(s[2] * c for s, c in zip(states, scales))
    return m, l, acc


def head_cols(h):
    return slice(h * DH, (h + 1) * DH)


def value_cols(h):
    return slice(COLS + h * DH, COLS + (h + 1) * DH)


def extract_kernel(off, q, k, v, kv_far, kv_rest, pack, q_near, q_far):
    rest = NEAR - FAR
    for h in range(HEADS):
        sel = select_matrix(off[h], NEAR)
        c, d = head_cols(h), value_cols(h)
        for b in range(BLOCKS):
            rows = slice(b * W0, (b + 1) * W0)
            picked = dot(sel, jnp.concatenate([k[rows, c], v[rows, c]], 1)).astype(BF16)
            f, r = slice(b * FAR, (b + 1) * FAR), slice(b * rest, (b + 1) * rest)
            g = slice(NEAR + b * rest, NEAR + (b + 1) * rest)
            kv_far[f, c] = picked[:FAR, :DH]
            kv_far[f, d] = picked[:FAR, DH:]
            kv_rest[r, c] = picked[FAR:, :DH]
            kv_rest[r, d] = picked[FAR:, DH:]
            pack[f, c] = picked[:FAR, :DH]
            pack[f, d] = picked[:FAR, DH:]
            pack[g, c] = picked[FAR:, :DH]
            pack[g, d] = picked[FAR:, DH:]
        for b in range(0, BLOCKS, 2):
            pair = jnp.concatenate(
                [q[b * W0 : (b + 1) * W0, c], q[(b + 1) * W0 : (b + 2) * W0, c]], 1
            )
            picked = dot(sel, pair).astype(BF16)
            for i in range(2):
                part = picked[:, i * DH : (i + 1) * DH]
                q_near[(b + i) * NEAR : (b + i + 1) * NEAR, c] = part
                q_far[(b + i) * FAR : (b + i + 1) * FAR, c] = part[:FAR]
    pack[W0:, :COLS] = k[TOK - W0 :, :]
    pack[W0:, COLS:] = v[TOK - W0 :, :]


def extract(off, q, k, v):
    return pl.pallas_call(
        extract_kernel,
        out_shape=[
            jax.ShapeDtypeStruct((FAR * BLOCKS, 2 * COLS), BF16),
            jax.ShapeDtypeStruct(((NEAR - FAR) * BLOCKS, 2 * COLS), BF16),
            jax.ShapeDtypeStruct((2 * W0, 2 * COLS), BF16),
            jax.ShapeDtypeStruct((NEAR * BLOCKS, COLS), BF16),
            jax.ShapeDtypeStruct((FAR * BLOCKS, COLS), BF16),
        ],
        in_specs=[SMEM, VMEM, VMEM, VMEM],
        out_specs=[VMEM] * 5,
        compiler_params=pltpu.CompilerParams(vmem_limit_bytes=40 << 20),
        cost_estimate=pl.CostEstimate(
            flops=400_000_000, bytes_accessed=6_000_000, transcendentals=0
        ),
        name="extract",
    )(off, q, k, v)


def local_kernel(off, q, k, v, acc, ml):
    for h in range(HEADS):
        perm = select_matrix(off[h], W0)
        c = head_cols(h)
        for b in range(BLOCKS):
            rows = slice(b * W0, (b + 1) * W0)
            keys = slice(max(b - 1, 0) * W0, (b + 1) * W0)
            qp = dot(perm, q[rows, c]).astype(BF16)
            m, l, o = attend(qp, k[keys, c], v[keys, c])
            acc[rows, c] = o
            ml[rows, h : h + 1] = m
            ml[rows, HEADS + h : HEADS + h + 1] = l


def local(off, q, k, v):
    return pl.pallas_call(
        local_kernel,
        out_shape=[
            jax.ShapeDtypeStruct((TOK, COLS), F32),
            jax.ShapeDtypeStruct((TOK, DH), F32),
        ],
        in_specs=[SMEM, VMEM, VMEM, VMEM],
        out_specs=[VMEM] * 2,
        compiler_params=pltpu.CompilerParams(vmem_limit_bytes=40 << 20),
        cost_estimate=pl.CostEstimate(
            flops=2_000_000_000, bytes_accessed=6_000_000, transcendentals=2_000_000
        ),
        name="local",
    )(off, q, k, v)


def near_kernel(q, far, rest, pack, far_z, far_zc, acc, ml):
    for h in range(HEADS):
        c, d = head_cols(h), value_cols(h)
        k = jnp.concatenate([far[:, c], rest[:, c], pack[:W0, c], far_z[:, c], far_zc[FAR * BLOCKS :, c]], 0)
        v = jnp.concatenate([far[:, d], rest[:, d], pack[:W0, d], far_z[:, d], far_zc[FAR * BLOCKS :, d]], 0)
        m, l, o = attend(q[:, c], k, v)
        acc[:, c] = o
        ml[:, h : h + 1] = m
        ml[:, HEADS + h : HEADS + h + 1] = l


def near(*args):
    return pl.pallas_call(
        near_kernel,
        out_shape=[
            jax.ShapeDtypeStruct((NEAR * BLOCKS, COLS), F32),
            jax.ShapeDtypeStruct((NEAR * BLOCKS, DH), F32),
        ],
        in_specs=[VMEM] * 6,
        out_specs=[VMEM] * 2,
        compiler_params=pltpu.CompilerParams(vmem_limit_bytes=40 << 20),
        cost_estimate=pl.CostEstimate(
            flops=600_000_000, bytes_accessed=3_000_000, transcendentals=600_000
        ),
        name="near",
    )(*args)


def far_kernel(*refs):
    q, kv, out = refs[:4], refs[4:12], refs[12:]
    n = FAR * BLOCKS
    for part in out:
        part[:, COLS:] = jnp.zeros((n, DH), BF16)
    for h in range(HEADS):
        c, d = head_cols(h), value_cols(h)
        qh = jnp.concatenate([x[:, c] for x in q], 0)
        k = jnp.concatenate([x[:, c] for x in kv], 0)
        v = jnp.concatenate([x[:, d] for x in kv], 0)
        m, l, o = attend(qh, k, v)
        o = (o / l).astype(BF16)
        lse = m + jnp.log2(l)
        first = lse.astype(BF16)
        left = lse - first.astype(F32)
        second = left.astype(BF16)
        third = (left - second.astype(F32)).astype(BF16)
        for i, part in enumerate(out):
            rows = slice(i * n, (i + 1) * n)
            part[:, c] = o[rows]
            for e, piece in enumerate((first, second, third)):
                col = COLS + e * HEADS + h
                part[:, col : col + 1] = piece[rows]


def far(*args):
    return pl.pallas_call(
        far_kernel,
        out_shape=[jax.ShapeDtypeStruct((FAR * BLOCKS, COLS + DH), BF16)] * 4,
        in_specs=[VMEM] * 12,
        out_specs=[VMEM] * 4,
        compiler_params=pltpu.CompilerParams(vmem_limit_bytes=40 << 20),
        cost_estimate=pl.CostEstimate(
            flops=1_000_000_000, bytes_accessed=3_000_000, transcendentals=1_000_000
        ),
        name="far",
    )(*args)


def final_kernel(
    off, where, q, acc0, ml0, q_near, acc1, ml1, rest_z, rest_zc, pack, halo, f0, f1, f2, f3, out
):
    from_core = where[0] == 1
    has_halo = where[1] == 1
    for h in range(HEADS):
        c, d = head_cols(h), value_cols(h)
        lc = slice(HEADS + h, HEADS + h + 1)
        mc = slice(h, h + 1)
        k = jnp.concatenate([rest_z[:, c], rest_zc[:, c]], 0)
        v = jnp.concatenate([rest_z[:, d], rest_zc[:, d]], 0)
        near_state = merge([(ml1[:, mc], ml1[:, lc], acc1[:, c]), attend(q_near[:, c], k, v)])
        restore = restore_matrix(off[h])
        for b in range(BLOCKS):
            rows = slice(b * W0, (b + 1) * W0)
            m, l, acc = ml0[rows, mc], ml0[rows, lc], acc0[rows, c]
            if b == 0:
                hk = jnp.where(from_core, pack[W0:, c], halo[:, c])
                hv = jnp.where(from_core, pack[W0:, d], halo[:, d])
                qp = dot(select_matrix(off[h], W0), q[rows, c]).astype(BF16)
                s = jnp.where(has_halo, dot_nt(qp, hk) * SCALE2, -jnp.inf)
                m_new = jnp.maximum(m, jnp.max(s, axis=1, keepdims=True))
                p = jnp.exp2(s - m_new)
                scale = jnp.exp2(m - m_new)
                l = l * scale + jnp.sum(p, axis=1, keepdims=True)
                acc = acc * scale + dot(p.astype(BF16), hv)
                m = m_new
            near_rows = slice(b * NEAR, (b + 1) * NEAR)
            far_rows = slice(b * FAR, (b + 1) * FAR)
            m1, l1, a1 = merge(
                [(m[:NEAR], l[:NEAR], acc[:NEAR]), tuple(x[near_rows] for x in near_state)]
            )
            parts = [(m1[:FAR], l1[:FAR], a1[:FAR])]
            for f in (f0, f1, f2, f3):
                lse = sum(
                    f[far_rows, COLS + e * HEADS + h : COLS + e * HEADS + h + 1].astype(F32)
                    for e in range(3)
                )
                parts.append((lse, jnp.ones_like(lse), f[far_rows, c].astype(F32)))
            m2, l2, a2 = merge(parts)
            mixed = jnp.concatenate(
                [a2 / l2, a1[FAR:] / l1[FAR:], acc[NEAR:] / l[NEAR:]], 0
            ).astype(BF16)
            out[rows, c] = dot(restore, mixed).astype(BF16)


def final(*args):
    return pl.pallas_call(
        final_kernel,
        out_shape=jax.ShapeDtypeStruct((TOK, COLS), BF16),
        in_specs=[SMEM, SMEM] + [VMEM] * 14,
        out_specs=VMEM,
        compiler_params=pltpu.CompilerParams(vmem_limit_bytes=40 << 20),
        cost_estimate=pl.CostEstimate(
            flops=1_000_000_000, bytes_accessed=6_000_000, transcendentals=1_000_000
        ),
        name="final",
    )(*args)


def place(x, y, z, core):
    return ((x % 4 * 4 + y % 4) * 2 + z % 2) * 2 + core


def moves(dx=0, dy=0, dz=0, dcore=0):
    return [
        (place(x, y, z, core), place(x + dx, y + dy, z + dz, (core + dcore) % 2))
        for x in range(4)
        for y in range(4)
        for z in range(2)
        for core in range(2)
    ]


def send(value, **shift):
    return lax.ppermute(value, "seq", moves(**shift))


def shards(q, k, v, off):
    position = lax.axis_index("seq")
    where = jnp.stack([position & 1, jnp.minimum(position, 1)]).astype(jnp.int32)
    kv_far, kv_rest, pack, q_near, q_far = extract(off, q, k, v)
    pack_c = send(pack, dcore=1)
    far_z = send(kv_far, dz=1)
    rest_z = send(kv_rest, dz=1)
    halo = lax.ppermute(pack[W0:], "seq", [(s, s + 1) for s in range(1, 63, 2)])
    qs = [q_far] + [send(q_far, dy=s) for s in (1, -1, 2)]
    own = jnp.concatenate([kv_far, far_z], 0)
    gathered = [own] + [send(own, dx=s) for s in (1, -1, 2)]
    crossed = [send(x, dcore=1) for x in gathered]
    acc0, ml0 = local(off, q, k, v)
    far_zc = crossed[0]
    acc1, ml1 = near(q_near, kv_far, kv_rest, pack_c, far_z, far_zc)
    parts = far(*qs, *gathered, *crossed)
    back = [parts[0]] + [send(p, dy=-s) for p, s in zip(parts[1:], (1, -1, 2))]
    rest_zc = send(rest_z, dcore=1)
    return final(
        off, where, q, acc0, ml0, q_near, acc1, ml1, rest_z, rest_zc, pack_c, halo, *back
    )


def solution(mesh):
    placed = (P("seq", "head"), P("seq", "head"), P("seq", "head"), P("head"))
    return jax.shard_map(
        shards, mesh=mesh, in_specs=placed, out_specs=P("seq", "head"), check_vma=False
    )
```

time: 262 us -> 90 us (0.34)
  waiting for transfers between devices: 129 us -> 7.76 us
  local copies, waits for them, and re-layouts: 52.4 us -> 10 us
  matrix products: 30.6 us -> 0 us
  starting transfers between devices: 18.8 us -> 47 us
  Pallas kernels: 0 us -> 24.6 us
  other arithmetic: 15.9 us -> 0.07 us
  between operations: 13.9 us -> 0.22 us
    all_gather x2 -> x0, waiting for transfers between devices: 104 us -> none  [the longest x1 103 us: shards(): lax.all_gather(dilate(value_all, far_chosen), 'seq', axis=0, tiled=True)]
    dot_general x12 -> x0, matrix products: 30.6 us -> none  [the longest x6 11.1 us: dilate(): jnp.einsum('trhd,rh->thd', grouped, chosen.astype(jnp.bfloat16), preferre...]
    ppermute x6 -> x18, starting transfers between devices: 18.8 us -> 47 us  [the longest x17 41.2 us: send(): return lax.ppermute(value, 'seq', moves(**shift))]
    pallas_call x0 -> x5, Pallas kernels: none -> 24.6 us  [the longest x1 10 us: final(): pl.pallas_call(final_kernel, out_shape=jax.ShapeDtypeStruct((TOK, COLS),...]
    another operation x11 -> x0, local copies, waits for them, and re-layouts: 18.2 us -> none  [the longest x6 9.89 us: dilate(): grouped = source.reshape(row_count // stride, stride, head_count, head_size)]
    ppermute x6 -> x18, waiting for transfers between devices: 25.2 us -> 7.76 us  [the longest x17 7.76 us: send(): return lax.ppermute(value, 'seq', moves(**shift))]
    broadcast_in_dim x14 -> x0, local copies, waits for them, and re-layouts: 10.5 us -> none  [the longest x4 6.87 us: spread_back(): spread = jnp.where(chosen[None, :, :, None], tile_rows[:, None, :, :], 0.0)]
    exp x3 -> x0, local copies, waits for them, and re-layouts: 5.26 us -> none  [the longest x1 1.77 us: shards(): near_w = jnp.exp(near_lse_full - level_max)]
  transfers between devices with their start and end apart: 8 -> 18, of which waited for: 4 -> 5; matrix products, arithmetic and copies ran while one was open for 25% -> 2% of each run, Pallas kernels for 0% -> 14%
where the time goes in v1:
time: 90 us; the launch traced here: 89.7 us
  starting transfers between devices  47 us (52%)
  Pallas kernels  24.6 us (27%)
  local copies, waits for them, and re-layouts  10 us (11%)
  waiting for transfers between devices  7.76 us (9%)
    ppermute x17, starting transfers between devices, send(): return lax.ppermute(value, 'seq', moves(**shift))  41.2 us
    pallas_call x1, Pallas kernels, final(): pl.pallas_call(final_kernel, out_shape=jax.ShapeDtypeStruct((TOK, COLS),...  10 us
    unnamed x49, local copies, waits for them, and re-layouts  8.12 us
    ppermute x17, waiting for transfers between devices, send(): return lax.ppermute(value, 'seq', moves(**shift))  7.76 us
    pallas_call x1, Pallas kernels, local(): pl.pallas_call(local_kernel, out_shape=[jax.ShapeDtypeStruct((TOK, COLS),...  7.01 us
    ppermute x1, starting transfers between devices, shards(): halo = lax.ppermute(pack[W0:], 'seq', [(s, s + 1) for s in range(1, 63, 2)])  5.77 us
    pallas_call x1, Pallas kernels, far(): pl.pallas_call(far_kernel, out_shape=[jax.ShapeDtypeStruct((FAR * BLOCKS,...  3.72 us
    pallas_call x1, Pallas kernels, extract(): pl.pallas_call(extract_kernel, out_shape=[jax.ShapeDtypeStruct((FAR * BLO...  2.16 us
  transfers between devices with their start and end apart: 18, of which 5 were waited for; matrix products, arithmetic and copies ran while one was open for 2% of the time, Pallas kernels for 14%

profile of v1, /device:TPU:1, one launch (start us, length us, event | category | flops | bytes accessed | tf_op | source)
XLA Modules:
  0.0 89.7 jit_solution(10543453958968081756)
XLA Ops:
  0.0 1.2 %copy-done = bf16[1024,512]{1,0:T(8,128)(2,1)S(1)} copy-done((bf16[1024,512]{1,0:T(8,128)(2,1)S(1)}, bf16[1024,512]{1,0:T(8,128)(2,1)}, u32[]{:S(2)}) %copy-start) | copy-done | bytes 1048600
  1.2 1.2 %copy-done.2 = bf16[1024,512]{1,0:T(8,128)(2,1)S(1)} copy-done((bf16[1024,512]{1,0:T(8,128)(2,1)S(1)}, bf16[1024,512]{1,0:T(8,128)(2,1)}, u32[]{:S(2)}) %copy-start.2) | copy-done | bytes 1048600
  2.5 1.2 %copy-done.4 = bf16[1024,512]{1,0:T(8,128)(2,1)S(1)} copy-done((bf16[1024,512]{1,0:T(8,128)(2,1)S(1)}, bf16[1024,512]{1,0:T(8,128)(2,1)}, u32[]{:S(2)}) %copy-start.4) | copy-done | bytes 1048600
  4.3 2.2 %extract.1 = (bf16[64,1024]{1,0:T(8,128)(2,1)S(1)}, bf16[192,1024]{1,0:T(8,128)(2,1)S(1)}, bf16[512,1024]{1,0:T(8,128)(2,1)}, bf16[256,512]{1,0:T(8,128)(2,1)S(1)}, bf16[64,512]{1,0:T(8,128)(2,1)S(1)}) custom-call(s32[4]{0:T(128)S(1)} %copy-done.14, bf16[1024,512]{1,0:T(8,128)(2,1)S(1)} %copy-done, bf16[1024,512]{1,0:T(8,128)(2,1)S(1)} %copy-done.2, ...), custom_call_target="tpu_custom_call" | custom-call | flops 400000000 | bytes 6000000 | tf_op jit(solution)/shard_map/extract/pallas_call | solution.py:108
  6.5 7.7 %collective-permute-start.1 = (bf16[64,1024]{1,0:T(8,128)(2,1)S(1)}, bf16[64,1024]{1,0:T(8,128)(2,1)S(1)}, u32[]{:S(2)}, u32[]{:S(2)}) collective-permute-start(bf16[64,1024]{1,0:T(8,128)(2,1)S(1)} %get-tuple-element.21.far), channel_id=1, source_target_pairs={{0,8},{4,12},{8,0},{12,4},{16,24},{20,28},{24,16},{28,20},{32,40},... | collective-permute-start | bytes 393224 | tf_op jit(solution)/shard_map/ppermute | solution.py:300
  14.2 1.0 %collective-permute-start = (bf16[512,1024]{1,0:T(8,128)(2,1)}, bf16[512,1024]{1,0:T(8,128)(2,1)S(1)}, u32[]{:S(2)}, u32[]{:S(2)}) collective-permute-start(bf16[512,1024]{1,0:T(8,128)(2,1)} %get-tuple-element.23), channel_id=1, source_target_pairs={{0,4},{4,0},{8,12},{12,8},{16,20},{20,16},{24,28},{28,24},{32,36},... | collective-permute-start | bytes 3145736 | tf_op jit(solution)/shard_map/ppermute | solution.py:300
  15.2 1.7 %collective-permute-done.1.far_z = bf16[64,1024]{1,0:T(8,128)(2,1)S(1)} collective-permute-done((bf16[64,1024]{1,0:T(8,128)(2,1)S(1)}, bf16[64,1024]{1,0:T(8,128)(2,1)S(1)}, u32[]{:S(2)}, u32[]{:S(2)}) %collective-permute-start.1) | collective-permute-done | bytes 131104 | tf_op jit(solution)/shard_map/ppermute | solution.py:300
  17.6 3.3 %collective-permute-start.11 = (bf16[128,1024]{1,0:T(8,128)(2,1)S(1)}, bf16[128,1024]{1,0:T(8,128)(2,1)}, u32[]{:S(2)}, u32[]{:S(2)}) collective-permute-start(bf16[128,1024]{1,0:T(8,128)(2,1)S(1)} %constant_dynamic-update-slice_fusion.refs_4_), channel_id=1, source_target_pairs={{0,128},{4,132},{8,136},{12,140},{16,144},{20,148},{24,152},{28,15... | collective-permute-start | bytes 786440 | tf_op jit(solution)/shard_map/ppermute | solution.py:300
  20.9 2.9 %collective-permute-start.8 = (bf16[64,512]{1,0:T(8,128)(2,1)S(1)}, bf16[64,512]{1,0:T(8,128)(2,1)S(1)}, u32[]{:S(2)}, u32[]{:S(2)}) collective-permute-start(bf16[64,512]{1,0:T(8,128)(2,1)S(1)} %get-tuple-element.26.refs_0_), channel_id=1, source_target_pairs={{0,32},{4,36},{8,40},{12,44},{16,48},{20,52},{24,56},{28,60},{32,0... | collective-permute-start | bytes 196616 | tf_op jit(solution)/shard_map/ppermute | solution.py:300
  26.5 4.7 %collective-permute-start.3 = (bf16[192,1024]{1,0:T(8,128)(2,1)S(1)}, bf16[192,1024]{1,0:T(8,128)(2,1)}, u32[]{:S(2)}, u32[]{:S(2)}) collective-permute-start(bf16[192,1024]{1,0:T(8,128)(2,1)S(1)} %get-tuple-element.22.rest), channel_id=1, source_target_pairs={{0,8},{4,12},{8,0},{12,4},{16,24},{20,28},{24,16},{28,20},{32,40},... | collective-permute-start | bytes 1179656 | tf_op jit(solution)/shard_map/ppermute | solution.py:300
  31.8 1.3 %collective-permute-start.6 = (bf16[64,512]{1,0:T(8,128)(2,1)S(1)}, bf16[64,512]{1,0:T(8,128)(2,1)S(1)}, u32[]{:S(2)}, u32[]{:S(2)}) collective-permute-start(bf16[64,512]{1,0:T(8,128)(2,1)S(1)} %get-tuple-element.26.refs_0_), channel_id=1, source_target_pairs={{0,16},{4,20},{8,24},{12,28},{16,32},{20,36},{24,40},{28,44},{32,4... | collective-permute-start | bytes 196616 | tf_op jit(solution)/shard_map/ppermute | solution.py:300
  33.1 3.1 %collective-permute-done.6.refs_1_ = bf16[64,512]{1,0:T(8,128)(2,1)S(1)} collective-permute-done((bf16[64,512]{1,0:T(8,128)(2,1)S(1)}, bf16[64,512]{1,0:T(8,128)(2,1)S(1)}, u32[]{:S(2)}, u32[]{:S(2)}) %collective-permute-start.6) | collective-permute-done | bytes 65568 | tf_op jit(solution)/shard_map/ppermute | solution.py:300
  37.3 6.6 %collective-permute-start.2 = (bf16[128,1024]{1,0:T(8,128)(2,1)S(1)}, bf16[128,1024]{1,0:T(8,128)(2,1)S(1)}, u32[]{:S(2)}, u32[]{:S(2)}) collective-permute-start(bf16[128,1024]{1,0:T(8,128)(2,1)S(1)} %constant_dynamic-update-slice_fusion.refs_4_), channel_id=1, source_target_pairs={{0,4},{4,0},{8,12},{12,8},{16,20},{20,16},{24,28},{28,24},{32,36},... | collective-permute-start | bytes 786440 | tf_op jit(solution)/shard_map/ppermute | solution.py:300
  44.0 7.0 %collective-permute-start.13 = (bf16[128,1024]{1,0:T(8,128)(2,1)}, bf16[128,1024]{1,0:T(8,128)(2,1)}, u32[]{:S(2)}, u32[]{:S(2)}) collective-permute-start(bf16[128,1024]{1,0:T(8,128)(2,1)} %collective-permute-done.10.refs_6_), channel_id=1, source_target_pairs={{0,4},{4,0},{8,12},{12,8},{16,20},{20,16},{24,28},{28,24},{32,36},... | collective-permute-start | bytes 786440 | tf_op jit(solution)/shard_map/ppermute | solution.py:300
  51.1 1.9 %slice.3 = bf16[256,1024]{1,0:T(8,128)(2,1)} slice(bf16[512,1024]{1,0:T(8,128)(2,1)} %get-tuple-element.23), slice={[256:512], [0:1024]} | slice | bytes 1048576 | tf_op jit(solution)/shard_map/slice | solution.py:310
  53.0 5.8 %collective-permute-start.5 = (bf16[256,1024]{1,0:T(8,128)(2,1)}, bf16[256,1024]{1,0:T(8,128)(2,1)}, u32[]{:S(2)}, u32[]{:S(2)}) collective-permute-start(bf16[256,1024]{1,0:T(8,128)(2,1)} %slice.3), channel_id=1, source_target_pairs={{4,8},{12,16},{20,24},{28,32},{36,40},{44,48},{52,56},{60,64},{68,... | collective-permute-start | bytes 1572872 | tf_op jit(solution)/shard_map/ppermute | solution.py:310
  58.8 1.2 %copy-done.5 = bf16[1024,512]{1,0:T(8,128)(2,1)S(1)} copy-done((bf16[1024,512]{1,0:T(8,128)(2,1)S(1)}, bf16[1024,512]{1,0:T(8,128)(2,1)}, u32[]{:S(2)}) %copy-start.5) | copy-done | bytes 1048600
  60.1 7.0 %local.1 = (f32[1024,512]{1,0:T(8,128)S(1)}, f32[1024,128]{1,0:T(8,128)S(1)}) custom-call(s32[4]{0:T(128)S(1)} %copy-done.15, bf16[1024,512]{1,0:T(8,128)(2,1)S(1)} %copy-done.1, bf16[1024,512]{1,0:T(8,128)(2,1)S(1)} %copy-done.3, bf16[1024,512]{1,0:T(8,128)(2,1)S(1)} %copy-done.5), custom_call_target="tpu_custom_call" | custom-call | flops 2000000000 | bytes 6000000 | tf_op jit(solution)/shard_map/local/pallas_call | solution.py:142
  67.2 3.7 %far.1 = (bf16[64,640]{1,0:T(8,128)(2,1)S(1)}, bf16[64,640]{1,0:T(8,128)(2,1)S(1)}, bf16[64,640]{1,0:T(8,128)(2,1)S(1)}, bf16[64,640]{1,0:T(8,128)(2,1)S(1)}) custom-call(bf16[64,512]{1,0:T(8,128)(2,1)S(1)} %copy-done.17, bf16[64,512]{1,0:T(8,128)(2,1)S(1)} %copy-done.23, bf16[64,512]{1,0:T(8,128)(2,1)S(1)} %copy-done.21, bf16[64,512]{1,0:T(8,128)(2,1)S(1)} %copy-done.19, ...), custom_call_target="tpu_custom_call" | custom-call | flops 1000000000 | bytes 3000000 | tf_op jit(solution)/shard_map/far/pallas_call | solution.py:212
  70.9 2.8 %collective-permute-start.15 = (bf16[64,640]{1,0:T(8,128)(2,1)S(1)}, bf16[64,640]{1,0:T(8,128)(2,1)S(1)}, u32[]{:S(2)}, u32[]{:S(2)}) collective-permute-start(bf16[64,640]{1,0:T(8,128)(2,1)S(1)} %get-tuple-element.28), channel_id=1, source_target_pairs={{0,48},{4,52},{8,56},{12,60},{16,0},{20,4},{24,8},{28,12},{32,16},... | collective-permute-start | bytes 245768 | tf_op jit(solution)/shard_map/ppermute | solution.py:300
  73.7 1.6 %collective-permute-start.17 = (bf16[64,640]{1,0:T(8,128)(2,1)S(1)}, bf16[64,640]{1,0:T(8,128)(2,1)S(1)}, u32[]{:S(2)}, u32[]{:S(2)}) collective-permute-start(bf16[64,640]{1,0:T(8,128)(2,1)S(1)} %get-tuple-element.30), channel_id=1, source_target_pairs={{0,32},{4,36},{8,40},{12,44},{16,48},{20,52},{24,56},{28,60},{32,0... | collective-permute-start | bytes 245768 | tf_op jit(solution)/shard_map/ppermute | solution.py:300
  75.4 1.8 %near.1 = (f32[256,512]{1,0:T(8,128)S(1)}, f32[256,128]{1,0:T(8,128)S(1)}) custom-call(bf16[256,512]{1,0:T(8,128)(2,1)S(1)} %get-tuple-element.20.q.q_near, bf16[64,1024]{1,0:T(8,128)(2,1)S(1)} %get-tuple-element.21.far, bf16[192,1024]{1,0:T(8,128)(2,1)S(1)} %copy-done.9, bf16[512,1024]{1,0:T(8,128)(2,1)S(1)} %collective-permute-done.pack, ...), custom_call_target="tpu_custom_call" | custom-call | flops 600000000 | bytes 3000000 | tf_op jit(solution)/shard_map/near/pallas_call | solution.py:170
  77.2 2.0 %collective-permute-done.16.f2 = bf16[64,640]{1,0:T(8,128)(2,1)S(1)} collective-permute-done((bf16[64,640]{1,0:T(8,128)(2,1)S(1)}, bf16[64,640]{1,0:T(8,128)(2,1)S(1)}, u32[]{:S(2)}, u32[]{:S(2)}) %collective-permute-start.16) | collective-permute-done | bytes 81952 | tf_op jit(solution)/shard_map/ppermute | solution.py:300
  79.7 10.0 %final.1 = bf16[1024,512]{1,0:T(8,128)(2,1)} custom-call(s32[4]{0:T(128)S(1)} %copy-done.15, s32[2]{0:T(128)S(1)} %pad_add_fusion.where, bf16[1024,512]{1,0:T(8,128)(2,1)S(1)} %copy-done.1, f32[1024,512]{1,0:T(8,128)S(1)} %get-tuple-element.18.acc0, f32[1024,128]{1,0:T(8,128)S(1)} %get-tuple-element.19.ml0, bf16[256,512]{1,0:T(8,128)(2,1)S(1)} %get-tuple-element.20.q.q_near, ...), custom_call_target="tpu_custom_call" | custom-call | flops 1000000000 | bytes 6000000 | tf_op jit(solution)/shard_map/final/pallas_call | solution.py:272
  (69 shorter events, 6.6 us)
Async XLA Ops:
  4.3 54.4 %copy-start.1 = (bf16[1024,512]{1,0:T(8,128)(2,1)S(1)}, bf16[1024,512]{1,0:T(8,128)(2,1)}, u32[]{:S(2)}) copy-start(bf16[1024,512]{1,0:T(8,128)(2,1)} %q.5) | copy-start | bytes 3145732
  4.3 54.4 %copy-start.3 = (bf16[1024,512]{1,0:T(8,128)(2,1)S(1)}, bf16[1024,512]{1,0:T(8,128)(2,1)}, u32[]{:S(2)}) copy-start(bf16[1024,512]{1,0:T(8,128)(2,1)} %k.3) | copy-start | bytes 3145732
  4.3 54.4 %copy-start.15 = (s32[4]{0:T(128)S(1)}, s32[4]{0:T(128)}, u32[]{:S(2)}) copy-start(s32[4]{0:T(128)} %off.5) | copy-start | bytes 52
  6.5 20.0 %copy-start.8 = (bf16[192,1024]{1,0:T(8,128)(2,1)}, bf16[192,1024]{1,0:T(8,128)(2,1)S(1)}, u32[]{:S(2)}) copy-start(bf16[192,1024]{1,0:T(8,128)(2,1)S(1)} %get-tuple-element.22.rest) | copy-start | bytes 1179652
  6.5 30.8 %copy-start.16 = (bf16[64,512]{1,0:T(8,128)(2,1)}, bf16[64,512]{1,0:T(8,128)(2,1)S(1)}, u32[]{:S(2)}) copy-start(bf16[64,512]{1,0:T(8,128)(2,1)S(1)} %get-tuple-element.26.refs_0_) | copy-start | bytes 196612
  6.5 10.4 %collective-permute-start.1 = (bf16[64,1024]{1,0:T(8,128)(2,1)S(1)}, bf16[64,1024]{1,0:T(8,128)(2,1)S(1)}, u32[]{:S(2)}, u32[]{:S(2)}) collective-permute-start(bf16[64,1024]{1,0:T(8,128)(2,1)S(1)} %get-tuple-element.21.far), channel_id=1, source_target_pairs={{0,8},{4,12},{8,0},{12,4},{16,24},{20,28},{24,16},{28,20},{32,40},... | collective-permute-start | bytes 393224 | tf_op jit(solution)/shard_map/ppermute | solution.py:300
  14.2 59.5 %collective-permute-start = (bf16[512,1024]{1,0:T(8,128)(2,1)}, bf16[512,1024]{1,0:T(8,128)(2,1)S(1)}, u32[]{:S(2)}, u32[]{:S(2)}) collective-permute-start(bf16[512,1024]{1,0:T(8,128)(2,1)} %get-tuple-element.23), channel_id=1, source_target_pairs={{0,4},{4,0},{8,12},{12,8},{16,20},{20,16},{24,28},{28,24},{32,36},... | collective-permute-start | bytes 3145736 | tf_op jit(solution)/shard_map/ppermute | solution.py:300
  17.6 41.2 %copy-start.12 = (bf16[128,1024]{1,0:T(8,128)(2,1)}, bf16[128,1024]{1,0:T(8,128)(2,1)S(1)}, u32[]{:S(2)}) copy-start(bf16[128,1024]{1,0:T(8,128)(2,1)S(1)} %constant_dynamic-update-slice_fusion.refs_4_) | copy-start | bytes 786436
  17.6 19.7 %collective-permute-start.11 = (bf16[128,1024]{1,0:T(8,128)(2,1)S(1)}, bf16[128,1024]{1,0:T(8,128)(2,1)}, u32[]{:S(2)}, u32[]{:S(2)}) collective-permute-start(bf16[128,1024]{1,0:T(8,128)(2,1)S(1)} %constant_dynamic-update-slice_fusion.refs_4_), channel_id=1, source_target_pairs={{0,128},{4,132},{8,136},{12,140},{16,144},{20,148},{24,152},{28,15... | collective-permute-start | bytes 786440 | tf_op jit(solution)/shard_map/ppermute | solution.py:300
  20.9 5.0 %collective-permute-start.8 = (bf16[64,512]{1,0:T(8,128)(2,1)S(1)}, bf16[64,512]{1,0:T(8,128)(2,1)S(1)}, u32[]{:S(2)}, u32[]{:S(2)}) collective-permute-start(bf16[64,512]{1,0:T(8,128)(2,1)S(1)} %get-tuple-element.26.refs_0_), channel_id=1, source_target_pairs={{0,32},{4,36},{8,40},{12,44},{16,48},{20,52},{24,56},{28,60},{32,0... | collective-permute-start | bytes 196616 | tf_op jit(solution)/shard_map/ppermute | solution.py:300
  23.8 20.1 %collective-permute-start.10 = (bf16[128,1024]{1,0:T(8,128)(2,1)S(1)}, bf16[128,1024]{1,0:T(8,128)(2,1)}, u32[]{:S(2)}, u32[]{:S(2)}) collective-permute-start(bf16[128,1024]{1,0:T(8,128)(2,1)S(1)} %constant_dynamic-update-slice_fusion.refs_4_), channel_id=1, source_target_pairs={{0,192},{4,196},{8,200},{12,204},{16,208},{20,212},{24,216},{28,22... | collective-permute-start | bytes 786440 | tf_op jit(solution)/shard_map/ppermute | solution.py:300
  24.6 6.5 %collective-permute-start.7 = (bf16[64,512]{1,0:T(8,128)(2,1)S(1)}, bf16[64,512]{1,0:T(8,128)(2,1)S(1)}, u32[]{:S(2)}, u32[]{:S(2)}) collective-permute-start(bf16[64,512]{1,0:T(8,128)(2,1)S(1)} %get-tuple-element.26.refs_0_), channel_id=1, source_target_pairs={{0,48},{4,52},{8,56},{12,60},{16,0},{20,4},{24,8},{28,12},{32,16},... | collective-permute-start | bytes 196616 | tf_op jit(solution)/shard_map/ppermute | solution.py:300
  26.5 26.5 %collective-permute-start.3 = (bf16[192,1024]{1,0:T(8,128)(2,1)S(1)}, bf16[192,1024]{1,0:T(8,128)(2,1)}, u32[]{:S(2)}, u32[]{:S(2)}) collective-permute-start(bf16[192,1024]{1,0:T(8,128)(2,1)S(1)} %get-tuple-element.22.rest), channel_id=1, source_target_pairs={{0,8},{4,12},{8,0},{12,4},{16,24},{20,28},{24,16},{28,20},{32,40},... | collective-permute-start | bytes 1179656 | tf_op jit(solution)/shard_map/ppermute | solution.py:300
  31.8 4.4 %collective-permute-start.6 = (bf16[64,512]{1,0:T(8,128)(2,1)S(1)}, bf16[64,512]{1,0:T(8,128)(2,1)S(1)}, u32[]{:S(2)}, u32[]{:S(2)}) collective-permute-start(bf16[64,512]{1,0:T(8,128)(2,1)S(1)} %get-tuple-element.26.refs_0_), channel_id=1, source_target_pairs={{0,16},{4,20},{8,24},{12,28},{16,32},{20,36},{24,40},{28,44},{32,4... | collective-permute-start | bytes 196616 | tf_op jit(solution)/shard_map/ppermute | solution.py:300
  36.8 7.2 %collective-permute-start.9 = (bf16[128,1024]{1,0:T(8,128)(2,1)S(1)}, bf16[128,1024]{1,0:T(8,128)(2,1)}, u32[]{:S(2)}, u32[]{:S(2)}) collective-permute-start(bf16[128,1024]{1,0:T(8,128)(2,1)S(1)} %constant_dynamic-update-slice_fusion.refs_4_), channel_id=1, source_target_pairs={{0,64},{4,68},{8,72},{12,76},{16,80},{20,84},{24,88},{28,92},{32,9... | collective-permute-start | bytes 786440 | tf_op jit(solution)/shard_map/ppermute | solution.py:300
  37.3 13.7 %collective-permute-start.2 = (bf16[128,1024]{1,0:T(8,128)(2,1)S(1)}, bf16[128,1024]{1,0:T(8,128)(2,1)S(1)}, u32[]{:S(2)}, u32[]{:S(2)}) collective-permute-start(bf16[128,1024]{1,0:T(8,128)(2,1)S(1)} %constant_dynamic-update-slice_fusion.refs_4_), channel_id=1, source_target_pairs={{0,4},{4,0},{8,12},{12,8},{16,20},{20,16},{24,28},{28,24},{32,36},... | collective-permute-start | bytes 786440 | tf_op jit(solution)/shard_map/ppermute | solution.py:300
  43.9 14.9 %collective-permute-start.14 = (bf16[128,1024]{1,0:T(8,128)(2,1)}, bf16[128,1024]{1,0:T(8,128)(2,1)}, u32[]{:S(2)}, u32[]{:S(2)}) collective-permute-start(bf16[128,1024]{1,0:T(8,128)(2,1)} %collective-permute-done.11.refs_7_), channel_id=1, source_target_pairs={{0,4},{4,0},{8,12},{12,8},{16,20},{20,16},{24,28},{28,24},{32,36},... | collective-permute-start | bytes 786440 | tf_op jit(solution)/shard_map/ppermute | solution.py:300
  44.0 23.1 %collective-permute-start.13 = (bf16[128,1024]{1,0:T(8,128)(2,1)}, bf16[128,1024]{1,0:T(8,128)(2,1)}, u32[]{:S(2)}, u32[]{:S(2)}) collective-permute-start(bf16[128,1024]{1,0:T(8,128)(2,1)} %collective-permute-done.10.refs_6_), channel_id=1, source_target_pairs={{0,4},{4,0},{8,12},{12,8},{16,20},{20,16},{24,28},{28,24},{32,36},... | collective-permute-start | bytes 786440 | tf_op jit(solution)/shard_map/ppermute | solution.py:300
  51.0 16.1 %collective-permute-start.12 = (bf16[128,1024]{1,0:T(8,128)(2,1)}, bf16[128,1024]{1,0:T(8,128)(2,1)}, u32[]{:S(2)}, u32[]{:S(2)}) collective-permute-start(bf16[128,1024]{1,0:T(8,128)(2,1)} %collective-permute-done.9.refs_5_), channel_id=1, source_target_pairs={{0,4},{4,0},{8,12},{12,8},{16,20},{20,16},{24,28},{28,24},{32,36},... | collective-permute-start | bytes 786440 | tf_op jit(solution)/shard_map/ppermute | solution.py:300
  53.0 24.2 %collective-permute-start.5 = (bf16[256,1024]{1,0:T(8,128)(2,1)}, bf16[256,1024]{1,0:T(8,128)(2,1)}, u32[]{:S(2)}, u32[]{:S(2)}) collective-permute-start(bf16[256,1024]{1,0:T(8,128)(2,1)} %slice.3), channel_id=1, source_target_pairs={{4,8},{12,16},{20,24},{28,32},{36,40},{44,48},{52,56},{60,64},{68,... | collective-permute-start | bytes 1572872 | tf_op jit(solution)/shard_map/ppermute | solution.py:310
  58.8 20.9 %collective-permute-start.4 = (bf16[192,1024]{1,0:T(8,128)(2,1)}, bf16[192,1024]{1,0:T(8,128)(2,1)S(1)}, u32[]{:S(2)}, u32[]{:S(2)}) collective-permute-start(bf16[192,1024]{1,0:T(8,128)(2,1)} %collective-permute-done.3.rest_z), channel_id=1, source_target_pairs={{0,4},{4,0},{8,12},{12,8},{16,20},{20,16},{24,28},{28,24},{32,36},... | collective-permute-start | bytes 1179656 | tf_op jit(solution)/shard_map/ppermute | solution.py:300
  70.9 6.3 %collective-permute-start.15 = (bf16[64,640]{1,0:T(8,128)(2,1)S(1)}, bf16[64,640]{1,0:T(8,128)(2,1)S(1)}, u32[]{:S(2)}, u32[]{:S(2)}) collective-permute-start(bf16[64,640]{1,0:T(8,128)(2,1)S(1)} %get-tuple-element.28), channel_id=1, source_target_pairs={{0,48},{4,52},{8,56},{12,60},{16,0},{20,4},{24,8},{28,12},{32,16},... | collective-permute-start | bytes 245768 | tf_op jit(solution)/shard_map/ppermute | solution.py:300
  73.7 5.5 %collective-permute-start.16 = (bf16[64,640]{1,0:T(8,128)(2,1)S(1)}, bf16[64,640]{1,0:T(8,128)(2,1)S(1)}, u32[]{:S(2)}, u32[]{:S(2)}) collective-permute-start(bf16[64,640]{1,0:T(8,128)(2,1)S(1)} %get-tuple-element.29), channel_id=1, source_target_pairs={{0,16},{4,20},{8,24},{12,28},{16,32},{20,36},{24,40},{28,44},{32,4... | collective-permute-start | bytes 245768 | tf_op jit(solution)/shard_map/ppermute | solution.py:300
  73.7 6.0 %collective-permute-start.17 = (bf16[64,640]{1,0:T(8,128)(2,1)S(1)}, bf16[64,640]{1,0:T(8,128)(2,1)S(1)}, u32[]{:S(2)}, u32[]{:S(2)}) collective-permute-start(bf16[64,640]{1,0:T(8,128)(2,1)S(1)} %get-tuple-element.30), channel_id=1, source_target_pairs={{0,32},{4,36},{8,40},{12,44},{16,48},{20,52},{24,56},{28,60},{32,0... | collective-permute-start | bytes 245768 | tf_op jit(solution)/shard_map/ppermute | solution.py:300
  (18 other events, 69.5 us)

commit v2 on v1

v2 whole, which is shorter than its diff:
```python
import functools

import jax
import jax.numpy as jnp
from jax import lax
from jax.experimental import pallas as pl
from jax.experimental.pallas import tpu as pltpu
from jax.sharding import PartitionSpec as P

HEADS = 4
DH = 128
W0 = 256
BLOCKS = 4
TOK = 1024
COLS = 512
NEAR = 64
FAR = 16
REST = NEAR - FAR
OTHER = W0 - NEAR
NROWS = NEAR * BLOCKS
FROWS = FAR * BLOCKS
KEPT = OTHER + NROWS
SENT = COLS + 3 * DH
SCALE2 = 128**-0.5 * 1.4426950408889634
F32 = jnp.float32
BF16 = jnp.bfloat16

VMEM = pl.BlockSpec(memory_space=pltpu.VMEM)
HBM = pl.BlockSpec(memory_space=pltpu.HBM)


def out_of(*shape, dtype=BF16):
    return jax.ShapeDtypeStruct(shape, dtype)


def params(mib):
    return pltpu.CompilerParams(vmem_limit_bytes=mib << 20)


def cost(us):
    return pl.CostEstimate(flops=int(us * 1e9), bytes_accessed=1000, transcendentals=0)


def source_row(index, offset):
    order = index >> 4
    residue = ((order & 3) << 2) + (((order >> 2) + 1) & 3)
    return ((index & 15) << 4) + ((offset + residue) & 15)


def select_matrix(offset, start, count):
    index = lax.broadcasted_iota(jnp.int32, (count, W0), 0) + start
    row = lax.broadcasted_iota(jnp.int32, (count, W0), 1)
    return jnp.where(row == source_row(index, offset), 1.0, 0.0).astype(BF16)


def restore_matrix(offset, start, count):
    index = lax.broadcasted_iota(jnp.int32, (W0, count), 1) + start
    row = lax.broadcasted_iota(jnp.int32, (W0, count), 0)
    return jnp.where(row == source_row(index, offset), 1.0, 0.0).astype(BF16)


def dot(a, b):
    return jnp.dot(a, b, preferred_element_type=F32)


def dot_nt(a, b):
    return lax.dot_general(a, b, (((1,), (1,)), ((), ())), preferred_element_type=F32)


def wide(column):
    return jnp.broadcast_to(column, (column.shape[0], DH))


def attend(q, k, v):
    s = dot_nt(q, k) * SCALE2
    m = jnp.max(s, axis=1, keepdims=True)
    p = jnp.exp2(s - m)
    l = jnp.sum(p, axis=1, keepdims=True)
    return wide(m), wide(l), dot(p.astype(BF16), v)


def merge(states):
    m = functools.reduce(jnp.maximum, [s[0] for s in states])
    scales = [jnp.exp2(s[0] - m) for s in states]
    l = sum(s[1] * c for s, c in zip(states, scales))
    acc = sum(s[2] * c for s, c in zip(states, scales))
    return m, l, acc


def head_cols(h):
    return slice(h * DH, (h + 1) * DH)


def value_cols(h):
    return slice(COLS + h * DH, COLS + (h + 1) * DH)


def block_rows(b):
    return slice(b * W0, (b + 1) * W0)


def offset_rows(offs, h, width):
    row = offs[h : h + 1, :]
    return jnp.concatenate([row] * (width // DH), 1) if width > DH else row[:, :width]


def extract_kernel(
    off_hbm, k_hbm, v_hbm, offs, kv_far, kv_rest, halo, pack, off, k, v, off_sem, sems
):
    off_copy = pltpu.make_async_copy(off_hbm, off, off_sem)
    off_copy.start()
    copies = {}
    for b in range(BLOCKS):
        for i, (src, dst) in enumerate(((k_hbm, k), (v_hbm, v))):
            copies[i, b] = pltpu.make_async_copy(
                src.at[block_rows(b), :], dst.at[block_rows(b), :], sems.at[i, b]
            )
            copies[i, b].start()
    off_copy.wait()
    sels = []
    for h in range(HEADS):
        offs[h : h + 1, :] = jnp.full((1, DH), off[h], jnp.int32)
        sels.append(select_matrix(off[h], OTHER, NEAR))
    for b in range(BLOCKS):
        rows = block_rows(b)
        copies[0, b].wait()
        copies[1, b].wait()
        f, r = slice(b * FAR, (b + 1) * FAR), slice(b * REST, (b + 1) * REST)
        g = slice(FROWS + b * REST, FROWS + (b + 1) * REST)
        for h in range(HEADS):
            c, d = head_cols(h), value_cols(h)
            picked = dot(sels[h], jnp.concatenate([k[rows, c], v[rows, c]], 1)).astype(BF16)
            for cols, part in ((c, picked[:, :DH]), (d, picked[:, DH:])):
                kv_far[f, cols] = part[:FAR]
                pack[f, cols] = part[:FAR]
                kv_rest[r, cols] = part[FAR:]
                pack[g, cols] = part[FAR:]
    last = block_rows(BLOCKS - 1)
    for out, rows in ((halo, slice(0, W0)), (pack, slice(NROWS, NROWS + W0))):
        out[rows, :COLS] = k[last, :]
        out[rows, COLS:] = v[last, :]


def extract(*args):
    return pl.pallas_call(
        extract_kernel,
        out_shape=[
            out_of(8, DH, dtype=jnp.int32),
            out_of(FROWS, 2 * COLS),
            out_of(REST * BLOCKS, 2 * COLS),
            out_of(W0, 2 * COLS),
            out_of(NROWS + W0, 2 * COLS),
        ],
        in_specs=[HBM] * 3,
        out_specs=[VMEM] * 5,
        scratch_shapes=[
            pltpu.SMEM((HEADS,), jnp.int32),
            pltpu.VMEM((TOK, COLS), BF16),
            pltpu.VMEM((TOK, COLS), BF16),
            pltpu.SemaphoreType.DMA,
            pltpu.SemaphoreType.DMA((2, BLOCKS)),
        ],
        compiler_params=params(59),
        cost_estimate=cost(0),
        name="extract",
    )(*args)


def queries_kernel(offs, q_hbm, qp, qn, qf, res, q, sems):
    copies = []
    for b in range(BLOCKS):
        copies.append(
            pltpu.make_async_copy(q_hbm.at[block_rows(b), :], q.at[block_rows(b), :], sems.at[b])
        )
        copies[-1].start()
    sels = []
    for h in range(HEADS):
        offset = offset_rows(offs, h, W0)
        sels.append(select_matrix(offset, 0, W0))
        res[block_rows(h), :] = restore_matrix(offset, 0, W0)
    for b in range(0, BLOCKS, 2):
        copies[b].wait()
        copies[b + 1].wait()
        for h in range(HEADS):
            c = head_cols(h)
            pair = jnp.concatenate([q[block_rows(b), c], q[block_rows(b + 1), c]], 1)
            moved = dot(sels[h], pair).astype(BF16)
            for i in range(2):
                part = moved[:, i * DH : (i + 1) * DH]
                qp[block_rows(b + i), c] = part
                qn[(b + i) * NEAR : (b + i + 1) * NEAR, c] = part[OTHER:]
                qf[(b + i) * FAR : (b + i + 1) * FAR, c] = part[OTHER : OTHER + FAR]


def permute_queries(*args):
    return pl.pallas_call(
        queries_kernel,
        out_shape=[
            out_of(TOK, COLS),
            out_of(NROWS, COLS),
            out_of(FROWS, COLS),
            out_of(HEADS * W0, W0),
        ],
        in_specs=[VMEM, HBM],
        out_specs=[VMEM] * 4,
        scratch_shapes=[pltpu.VMEM((TOK, COLS), BF16), pltpu.SemaphoreType.DMA((BLOCKS,))],
        compiler_params=params(16),
        cost_estimate=cost(3),
        name="queries",
    )(*args)


def own_kernel(kv_far, far_z, own):
    own[:FROWS, :] = kv_far[...]
    own[FROWS:, :] = far_z[...]


def join_far(*args):
    return pl.pallas_call(
        own_kernel,
        out_shape=out_of(2 * FROWS, 2 * COLS),
        in_specs=[VMEM] * 2,
        out_specs=VMEM,
        compiler_params=params(8),
        cost_estimate=cost(0),
        name="own",
    )(*args)


def local_kernel(res, q, k, v, done, km, kl, ka):
    for h in range(HEADS):
        c = head_cols(h)
        qs = [q[block_rows(b), c] for b in range(BLOCKS)]
        scores = [[] for _ in range(BLOCKS)]
        for j in range(BLOCKS):
            users = qs[j : j + 2]
            s = dot_nt(jnp.concatenate(users, 0), k[block_rows(j), c]) * SCALE2
            for i in range(len(users)):
                scores[j + i].append(s[i * W0 : (i + 1) * W0])
        ms, ls, ps = [], [], []
        for b in range(BLOCKS):
            m = functools.reduce(
                jnp.maximum, [jnp.max(s, axis=1, keepdims=True) for s in scores[b]]
            )
            p = [jnp.exp2(s - m) for s in scores[b]]
            ms.append(m)
            ls.append(sum(jnp.sum(x, axis=1, keepdims=True) for x in p))
            ps.append([x.astype(BF16) for x in p])
        accs = [None] * BLOCKS
        for j in range(BLOCKS):
            users = [ps[j][-1]] + ([ps[j + 1][0]] if j + 1 < BLOCKS else [])
            o = dot(jnp.concatenate(users, 0), v[block_rows(j), c])
            for i in range(len(users)):
                part = o[i * W0 : (i + 1) * W0]
                accs[j + i] = part if accs[j + i] is None else accs[j + i] + part
        km[:W0, c], kl[:W0, c], ka[:W0, c] = wide(ms[0]), wide(ls[0]), accs[0]
        rest = []
        for b in range(1, BLOCKS):
            near = slice(OTHER + b * NEAR, OTHER + (b + 1) * NEAR)
            km[near, c] = wide(ms[b][OTHER:])
            kl[near, c] = wide(ls[b][OTHER:])
            ka[near, c] = accs[b][OTHER:]
            rest.append((accs[b][:OTHER] * (1.0 / ls[b][:OTHER])).astype(BF16))
        restore = res[block_rows(h), :OTHER]
        pair = dot(restore, jnp.concatenate(rest[:2], 1)).astype(BF16)
        done[0:W0, c] = pair[:, :DH]
        done[W0 : 2 * W0, c] = pair[:, DH:]
        done[2 * W0 :, c] = dot(restore, rest[2]).astype(BF16)


def local(*args):
    state = out_of(KEPT, COLS, dtype=F32)
    return pl.pallas_call(
        local_kernel,
        out_shape=[
            out_of(TOK - W0, COLS),
            state,
            state,
            state,
        ],
        in_specs=[VMEM] * 4,
        out_specs=[VMEM] * 4,
        compiler_params=params(16),
        cost_estimate=cost(1),
        name="local",
    )(*args)


def halo_kernel(res, q, km, kl, ka, pack, halo, done, hm, hl, ha):
    position = lax.axis_index("seq")
    from_core = (position & 1) == 1
    has_halo = position > 0
    for h in range(HEADS):
        c, d = head_cols(h), value_cols(h)
        hk = jnp.where(from_core, pack[NROWS:, c], halo[:, c])
        hv = jnp.where(from_core, pack[NROWS:, d], halo[:, d])
        m = km[:W0, c]
        s = jnp.where(has_halo, dot_nt(q[:W0, c], hk) * SCALE2, -jnp.inf)
        m_new = jnp.maximum(m, wide(jnp.max(s, axis=1, keepdims=True)))
        p = jnp.exp2(s - jnp.concatenate([m_new, m_new], 1))
        scale = jnp.exp2(m - m_new)
        l = kl[:W0, c] * scale + wide(jnp.sum(p, axis=1, keepdims=True))
        acc = ka[:W0, c] * scale + dot(p.astype(BF16), hv)
        hm[:, c], hl[:, c], ha[:, c] = m_new[OTHER:], l[OTHER:], acc[OTHER:]
        rest = (acc[:OTHER] * (1.0 / l[:OTHER])).astype(BF16)
        done[:, c] = dot(res[block_rows(h), :OTHER], rest).astype(BF16)


def halo_fold(*args):
    state = out_of(NEAR, COLS, dtype=F32)
    return pl.pallas_call(
        halo_kernel,
        out_shape=[out_of(W0, COLS), state, state, state],
        in_specs=[VMEM] * 7,
        out_specs=[VMEM] * 4,
        compiler_params=params(16),
        cost_estimate=cost(0),
        name="halo",
    )(*args)


def near_kernel(q, far, rest, pack, m, l, acc):
    for h in range(HEADS):
        c, d = head_cols(h), value_cols(h)
        k, v = (
            jnp.concatenate([far[:, cols], rest[:, cols], pack[:NROWS, cols]], 0)
            for cols in (c, d)
        )
        m[:, c], l[:, c], acc[:, c] = attend(q[:, c], k, v)


def near(*args):
    return pl.pallas_call(
        near_kernel,
        out_shape=[out_of(NROWS, COLS, dtype=F32)] * 3,
        in_specs=[VMEM] * 4,
        out_specs=[VMEM] * 3,
        compiler_params=params(16),
        cost_estimate=cost(0),
        name="near",
    )(*args)


def far_kernel(*refs):
    q, kv, out = refs[:4], refs[4:12], refs[12:]
    for part in out:
        part[:, COLS:] = jnp.zeros((FROWS, 3 * DH), BF16)
    for h in range(HEADS):
        c, d = head_cols(h), value_cols(h)
        qh = jnp.concatenate([x[:, c] for x in q], 0)
        k = jnp.concatenate([x[:, c] for x in kv], 0)
        v = jnp.concatenate([x[:, d] for x in kv], 0)
        m, l, o = attend(qh, k, v)
        o = (o * (1.0 / l)).astype(BF16)
        lse = (m + jnp.log2(l))[:, :1]
        first = lse.astype(BF16)
        left = lse - first.astype(F32)
        second = left.astype(BF16)
        third = (left - second.astype(F32)).astype(BF16)
        for i, part in enumerate(out):
            rows = slice(i * FROWS, (i + 1) * FROWS)
            part[:, c] = o[rows]
            for e, piece in enumerate((first, second, third)):
                col = COLS + e * DH + h
                part[:, col : col + 1] = piece[rows]


def far(*args):
    return pl.pallas_call(
        far_kernel,
        out_shape=[out_of(FROWS, SENT)] * 4,
        in_specs=[VMEM] * 12,
        out_specs=[VMEM] * 4,
        compiler_params=params(16),
        cost_estimate=cost(0),
        name="far",
    )(*args)


def join_kernel(
    far_z, res, q, km, kl, ka, hm, hl, ha, nm, nl, na, far_zc, rest_z, rest_zc, done0, done, f0, f1, f2, f3, out
):
    fars = (f0, f1, f2, f3)
    lses = [
        sum(f[:, COLS + e * DH : COLS + (e + 1) * DH].astype(F32) for e in range(3)) for f in fars
    ]
    for h in range(HEADS):
        c, d = head_cols(h), value_cols(h)
        k, v = (
            jnp.concatenate(
                [far_z[:, cols], far_zc[FROWS:, cols], rest_z[:, cols], rest_zc[:, cols]], 0
            )
            for cols in (c, d)
        )
        state = tuple(
            jnp.concatenate([x[:, c], y[W0:, c]], 0) for x, y in ((hm, km), (hl, kl), (ha, ka))
        )
        m, l, acc = merge([state, (nm[:, c], nl[:, c], na[:, c]), attend(q[:, c], k, v)])
        parts = [(wide(x[:, h : h + 1]), f[:, c].astype(F32)) for x, f in zip(lses, fars)]
        restored = []
        for b in range(BLOCKS):
            rows = slice(b * NEAR, (b + 1) * NEAR)
            mb, lb, ab = m[rows], l[rows], acc[rows]
            fr = slice(b * FAR, (b + 1) * FAR)
            _, lf, af = merge(
                [(mb[:FAR], lb[:FAR], ab[:FAR])] + [(x[fr], 1.0, o[fr]) for x, o in parts]
            )
            restored.append(
                (
                    jnp.concatenate([af, ab[FAR:]], 0)
                    * (1.0 / jnp.concatenate([lf, lb[FAR:]], 0))
                ).astype(BF16)
            )
        placed = dot(res[block_rows(h), OTHER:], jnp.concatenate(restored, 1)).astype(BF16)
        out[:W0, c] = done0[:, c] + placed[:, :DH]
        for b in range(1, BLOCKS):
            rows = slice((b - 1) * W0, b * W0)
            out[block_rows(b), c] = done[rows, c] + placed[:, b * DH : (b + 1) * DH]


def join(*args):
    return pl.pallas_call(
        join_kernel,
        out_shape=out_of(TOK, COLS),
        in_specs=[VMEM] * 21,
        out_specs=VMEM,
        compiler_params=params(16),
        cost_estimate=cost(0),
        name="join",
    )(*args)


def place(x, y, z, core):
    return ((x % 4 * 4 + y % 4) * 2 + z % 2) * 2 + core


def moves(dx=0, dy=0, dz=0, dcore=0):
    return [
        (place(x, y, z, core), place(x + dx, y + dy, z + dz, (core + dcore) % 2))
        for x in range(4)
        for y in range(4)
        for z in range(2)
        for core in range(2)
    ]


def send(value, **shift):
    return lax.ppermute(value, "seq", moves(**shift))


def shards(q, k, v, off):
    offs, kv_far, kv_rest, halo, pack = extract(off, k, v)
    far_z = send(kv_far, dz=1)
    pack_c = send(pack, dcore=1)
    qp, qn, qf, res = permute_queries(offs, q)
    halo = lax.ppermute(halo, "seq", [(s, s + 1) for s in range(1, 63, 2)])
    qf, pack_c = lax.optimization_barrier((qf, pack_c))
    qs = [send(qf, dy=s) for s in (1, -1, 2)]
    far_z, qs = lax.optimization_barrier((far_z, qs))
    own = join_far(kv_far, far_z)
    own, kv_rest = lax.optimization_barrier((own, kv_rest))
    gathered = [own] + [send(own, dx=s) for s in (1, -1, 2)]
    rest_z = send(kv_rest, dz=1)
    done, km, kl, ka = local(res, qp, k, v)
    near_state = near(qn, kv_far, kv_rest, pack_c)
    done0, *halo_state = halo_fold(res, qp, km, kl, ka, pack_c, halo)
    gathered, near_state, done0 = lax.optimization_barrier((gathered, near_state, done0))
    crossed = [send(x, dcore=1) for x in gathered]
    parts = far(qf, *qs, *gathered, *crossed)
    back = [parts[0]] + [send(p, dy=-s) for p, s in zip(parts[1:], (1, -1, 2))]
    rest_z, *back = lax.optimization_barrier((rest_z, *back))
    rest_zc = send(rest_z, dcore=1)
    return join(
        far_z, res, qn, km, kl, ka, *halo_state, *near_state, crossed[0], rest_z, rest_zc,
        done0, done, *back,
    )


def solution(mesh):
    placed = (P("seq", "head"), P("seq", "head"), P("seq", "head"), P("head"))
    return jax.shard_map(
        shards, mesh=mesh, in_specs=placed, out_specs=P("seq", "head"), check_vma=False
    )
```

time: 90 us -> 64.4 us (0.72)
  starting transfers between devices: 47 us -> 33.5 us
  local copies, waits for them, and re-layouts: 10 us -> 0.03 us
  Pallas kernels: 24.6 us -> 16.5 us
  waiting for transfers between devices: 7.76 us -> 14.1 us
    ppermute x17, starting transfers between devices: 41.2 us -> 31.2 us  [send(): return lax.ppermute(value, 'seq', moves(**shift))]
    pallas_call x5 -> x8, Pallas kernels: 24.6 us -> 16.5 us  [the longest x1 3.82 us: local(): pl.pallas_call(local_kernel, out_shape=[out_of(TOK - W0, COLS), state, st...]
    unnamed x49 -> x12, local copies, waits for them, and re-layouts: 8.12 us -> 0.03 us
    ppermute x17, waiting for transfers between devices: 7.76 us -> 14.1 us  [send(): return lax.ppermute(value, 'seq', moves(**shift))]
    ppermute x1, starting transfers between devices: 5.77 us -> 2.37 us  [shards(): halo = lax.ppermute(halo, 'seq', [(s, s + 1) for s in range(1, 63, 2)])]
    slice x1 -> x0, local copies, waits for them, and re-layouts: 1.92 us -> none  [shards(): halo = lax.ppermute(pack[W0:], 'seq', [(s, s + 1) for s in range(1, 63, 2)])]
  transfers between devices with their start and end apart: 18 -> 18, of which waited for: 5 -> 9; matrix products, arithmetic and copies ran while one was open for 2% -> 0% of each run, Pallas kernels for 14% -> 15%
where the time goes in v2:
time: 64.4 us; the launch traced here: 64.3 us
  starting transfers between devices  33.5 us (52%)
  Pallas kernels  16.5 us (26%)
  waiting for transfers between devices  14.1 us (22%)
    ppermute x17, starting transfers between devices, send(): return lax.ppermute(value, 'seq', moves(**shift))  31.2 us
    ppermute x17, waiting for transfers between devices, send(): return lax.ppermute(value, 'seq', moves(**shift))  14.1 us
    pallas_call x1, Pallas kernels, local(): pl.pallas_call(local_kernel, out_shape=[out_of(TOK - W0, COLS), state, st...  3.82 us
    pallas_call x1, Pallas kernels, join(): pl.pallas_call(join_kernel, out_shape=out_of(TOK, COLS), in_specs=[VMEM]...  3.31 us
    pallas_call x1, Pallas kernels, extract(): pl.pallas_call(extract_kernel, out_shape=[out_of(8, DH, dtype=jnp.int32),...  3.29 us
    ppermute x1, starting transfers between devices, shards(): halo = lax.ppermute(halo, 'seq', [(s, s + 1) for s in range(1, 63, 2)])  2.37 us
    pallas_call x1, Pallas kernels, far(): pl.pallas_call(far_kernel, out_shape=[out_of(FROWS, SENT)] * 4, in_specs=...  2.31 us
    pallas_call x1, Pallas kernels, halo_fold(): pl.pallas_call(halo_kernel, out_shape=[out_of(W0, COLS), state, state, st...  1.4 us
  transfers between devices with their start and end apart: 18, of which 9 were waited for; matrix products, arithmetic and copies ran while one was open for 0% of the time, Pallas kernels for 15%

profile of v2, /device:TPU:1, one launch (start us, length us, event | category | flops | bytes accessed | tf_op | source)
XLA Modules:
  0.0 64.3 jit_solution(5327098662901923419)
XLA Ops:
  0.0 3.3 %extract.1 = (s32[8,128]{1,0:T(8,128)}, bf16[64,1024]{1,0:T(8,128)(2,1)}, bf16[192,1024]{1,0:T(8,128)(2,1)}, bf16[256,1024]{1,0:T(8,128)(2,1)}, bf16[512,1024]{1,0:T(8,128)(2,1)}) custom-call(s32[4]{0:T(128)} %off_hbm.1, bf16[1024,512]{1,0:T(8,128)(2,1)} %k.1, bf16[1024,512]{1,0:T(8,128)(2,1)} %v.1), custom_call_target="tpu_custom_call" | custom-call | bytes 1000 | tf_op jit(solution)/shard_map/extract/pallas_call | solution.py:145
  3.3 3.3 %collective-permute-start.1 = (bf16[512,1024]{1,0:T(8,128)(2,1)}, bf16[512,1024]{1,0:T(8,128)(2,1)S(1)}, u32[]{:S(2)}, u32[]{:S(2)}) collective-permute-start(bf16[512,1024]{1,0:T(8,128)(2,1)} %get-tuple-element.53), channel_id=1, source_target_pairs={{0,4},{4,0},{8,12},{12,8},{16,20},{20,16},{24,28},{28,24},{32,36},... | collective-permute-start | bytes 3145736 | tf_op jit(solution)/shard_map/ppermute | solution.py:448
  6.6 5.2 %collective-permute-start = (bf16[64,1024]{1,0:T(8,128)(2,1)}, bf16[64,1024]{1,0:T(8,128)(2,1)S(1)}, u32[]{:S(2)}, u32[]{:S(2)}) collective-permute-start(bf16[64,1024]{1,0:T(8,128)(2,1)} %get-tuple-element.50.kv_far.far), channel_id=1, source_target_pairs={{0,8},{4,12},{8,0},{12,4},{16,24},{20,28},{24,16},{28,20},{32,40},... | collective-permute-start | bytes 393224 | tf_op jit(solution)/shard_map/ppermute | solution.py:448
  11.8 2.4 %collective-permute-start.5 = (bf16[256,1024]{1,0:T(8,128)(2,1)}, bf16[256,1024]{1,0:T(8,128)(2,1)S(1)}, u32[]{:S(2)}, u32[]{:S(2)}) collective-permute-start(bf16[256,1024]{1,0:T(8,128)(2,1)} %get-tuple-element.63), channel_id=1, source_target_pairs={{4,8},{12,16},{20,24},{28,32},{36,40},{44,48},{52,56},{60,64},{68,... | collective-permute-start | bytes 1572872 | tf_op jit(solution)/shard_map/ppermute | solution.py:456
  14.3 1.0 %queries.1 = (bf16[1024,512]{1,0:T(8,128)(2,1)S(1)}, bf16[256,512]{1,0:T(8,128)(2,1)S(1)}, bf16[64,512]{1,0:T(8,128)(2,1)S(1)}, bf16[1024,256]{1,0:T(8,128)(2,1)S(1)}) custom-call(s32[8,128]{1,0:T(8,128)S(1)} %copy-done.5, bf16[1024,512]{1,0:T(8,128)(2,1)S(1)} %copy-done.4), custom_call_target="tpu_custom_call" | custom-call | flops 3000000000 | bytes 1000 | tf_op jit(solution)/shard_map/queries/pallas_call | solution.py:196
  15.3 0.9 %collective-permute-start.2 = (bf16[64,512]{1,0:T(8,128)(2,1)S(1)}, bf16[64,512]{1,0:T(8,128)(2,1)S(1)}, u32[]{:S(2)}, u32[]{:S(2)}) collective-permute-start(bf16[64,512]{1,0:T(8,128)(2,1)S(1)} %get-tuple-element.54.refs_0_), channel_id=1, source_target_pairs={{0,16},{4,20},{8,24},{12,28},{16,32},{20,36},{24,40},{28,44},{32,4... | collective-permute-start | bytes 196616 | tf_op jit(solution)/shard_map/ppermute | solution.py:448
  16.2 1.8 %collective-permute-start.3 = (bf16[64,512]{1,0:T(8,128)(2,1)S(1)}, bf16[64,512]{1,0:T(8,128)(2,1)S(1)}, u32[]{:S(2)}, u32[]{:S(2)}) collective-permute-start(bf16[64,512]{1,0:T(8,128)(2,1)S(1)} %get-tuple-element.54.refs_0_), channel_id=1, source_target_pairs={{0,48},{4,52},{8,56},{12,60},{16,0},{20,4},{24,8},{28,12},{32,16},... | collective-permute-start | bytes 196616 | tf_op jit(solution)/shard_map/ppermute | solution.py:448
  18.1 1.2 %collective-permute-start.4 = (bf16[64,512]{1,0:T(8,128)(2,1)S(1)}, bf16[64,512]{1,0:T(8,128)(2,1)S(1)}, u32[]{:S(2)}, u32[]{:S(2)}) collective-permute-start(bf16[64,512]{1,0:T(8,128)(2,1)S(1)} %get-tuple-element.54.refs_0_), channel_id=1, source_target_pairs={{0,32},{4,36},{8,40},{12,44},{16,48},{20,52},{24,56},{28,60},{32,0... | collective-permute-start | bytes 196616 | tf_op jit(solution)/shard_map/ppermute | solution.py:448
  19.3 0.6 collective-permute-done.2.refs_1_
  20.0 3.6 %collective-permute-done.4.refs_3_ = bf16[64,512]{1,0:T(8,128)(2,1)S(1)} collective-permute-done((bf16[64,512]{1,0:T(8,128)(2,1)S(1)}, bf16[64,512]{1,0:T(8,128)(2,1)S(1)}, u32[]{:S(2)}, u32[]{:S(2)}) %collective-permute-start.4) | collective-permute-done | bytes 65568 | tf_op jit(solution)/shard_map/ppermute | solution.py:448
  24.1 2.2 %collective-permute-start.7 = (bf16[128,1024]{1,0:T(8,128)(2,1)S(1)}, bf16[128,1024]{1,0:T(8,128)(2,1)S(1)}, u32[]{:S(2)}, u32[]{:S(2)}) collective-permute-start(bf16[128,1024]{1,0:T(8,128)(2,1)S(1)} %own.1.refs_4_), channel_id=1, source_target_pairs={{0,192},{4,196},{8,200},{12,204},{16,208},{20,212},{24,216},{28,22... | collective-permute-start | bytes 786440 | tf_op jit(solution)/shard_map/ppermute | solution.py:448
  26.3 0.8 %collective-permute-start.8 = (bf16[128,1024]{1,0:T(8,128)(2,1)S(1)}, bf16[128,1024]{1,0:T(8,128)(2,1)S(1)}, u32[]{:S(2)}, u32[]{:S(2)}) collective-permute-start(bf16[128,1024]{1,0:T(8,128)(2,1)S(1)} %own.1.refs_4_), channel_id=1, source_target_pairs={{0,128},{4,132},{8,136},{12,140},{16,144},{20,148},{24,152},{28,15... | collective-permute-start | bytes 786440 | tf_op jit(solution)/shard_map/ppermute | solution.py:448
  27.1 6.4 %collective-permute-start.10 = (bf16[192,1024]{1,0:T(8,128)(2,1)S(1)}, bf16[192,1024]{1,0:T(8,128)(2,1)S(1)}, u32[]{:S(2)}, u32[]{:S(2)}) collective-permute-start(bf16[192,1024]{1,0:T(8,128)(2,1)S(1)} %copy-done.3), channel_id=1, source_target_pairs={{0,8},{4,12},{8,0},{12,4},{16,24},{20,28},{24,16},{28,20},{32,40},... | collective-permute-start | bytes 1179656 | tf_op jit(solution)/shard_map/ppermute | solution.py:448
  33.5 3.8 %local.1 = (bf16[768,512]{1,0:T(8,128)(2,1)S(1)}, f32[448,512]{1,0:T(8,128)S(1)}, f32[448,512]{1,0:T(8,128)S(1)}, f32[448,512]{1,0:T(8,128)S(1)}) custom-call(bf16[1024,256]{1,0:T(8,128)(2,1)S(1)} %get-tuple-element.56.res, bf16[1024,512]{1,0:T(8,128)(2,1)S(1)} %get-tuple-element.58.q, bf16[1024,512]{1,0:T(8,128)(2,1)S(1)} %copy-done, ...), custom_call_target="tpu_custom_call" | custom-call | flops 1000000000 | bytes 1000 | tf_op jit(solution)/shard_map/local/pallas_call | solution.py:273
  37.3 1.4 %halo.1 = (bf16[256,512]{1,0:T(8,128)(2,1)S(1)}, f32[64,512]{1,0:T(8,128)S(1)}, f32[64,512]{1,0:T(8,128)S(1)}, f32[64,512]{1,0:T(8,128)S(1)}) custom-call(bf16[1024,256]{1,0:T(8,128)(2,1)S(1)} %get-tuple-element.56.res, bf16[1024,512]{1,0:T(8,128)(2,1)S(1)} %get-tuple-element.58.q, f32[448,512]{1,0:T(8,128)S(1)} %get-tuple-element.59.km, ...), custom_call_target="tpu_custom_call" | custom-call | bytes 1000 | tf_op jit(solution)/shard_map/halo/pallas_call | solution.py:311
  38.7 1.4 %near.1 = (f32[256,512]{1,0:T(8,128)S(1)}, f32[256,512]{1,0:T(8,128)S(1)}, f32[256,512]{1,0:T(8,128)S(1)}) custom-call(bf16[256,512]{1,0:T(8,128)(2,1)S(1)} %get-tuple-element.57.q, bf16[64,1024]{1,0:T(8,128)(2,1)S(1)} %copy-done.2, bf16[192,1024]{1,0:T(8,128)(2,1)S(1)} %copy-done.3, bf16[512,1024]{1,0:T(8,128)(2,1)S(1)} %collective-permute-done.1.pack), custom_call_target="tpu_custom_call" | custom-call | bytes 1000 | tf_op jit(solution)/shard_map/near/pallas_call | solution.py:333
  42.9 2.3 %far.1 = (bf16[64,896]{1,0:T(8,128)(2,1)S(1)}, bf16[64,896]{1,0:T(8,128)(2,1)S(1)}, bf16[64,896]{1,0:T(8,128)(2,1)S(1)}, bf16[64,896]{1,0:T(8,128)(2,1)S(1)}) custom-call(bf16[64,512]{1,0:T(8,128)(2,1)S(1)} %get-tuple-element.54.refs_0_, bf16[64,512]{1,0:T(8,128)(2,1)S(1)} %collective-permute-done.2.refs_1_, ...), custom_call_target="tpu_custom_call" | custom-call | bytes 1000 | tf_op jit(solution)/shard_map/far/pallas_call | solution.py:369
  45.2 5.2 %collective-permute-start.14 = (bf16[64,896]{1,0:T(8,128)(2,1)S(1)}, bf16[64,896]{1,0:T(8,128)(2,1)S(1)}, u32[]{:S(2)}, u32[]{:S(2)}) collective-permute-start(bf16[64,896]{1,0:T(8,128)(2,1)S(1)} %get-tuple-element.85), channel_id=1, source_target_pairs={{0,48},{4,52},{8,56},{12,60},{16,0},{20,4},{24,8},{28,12},{32,16},... | collective-permute-start | bytes 344072 | tf_op jit(solution)/shard_map/ppermute | solution.py:448
  50.4 1.3 %collective-permute-start.16 = (bf16[64,896]{1,0:T(8,128)(2,1)S(1)}, bf16[64,896]{1,0:T(8,128)(2,1)S(1)}, u32[]{:S(2)}, u32[]{:S(2)}) collective-permute-start(bf16[64,896]{1,0:T(8,128)(2,1)S(1)} %get-tuple-element.87), channel_id=1, source_target_pairs={{0,32},{4,36},{8,40},{12,44},{16,48},{20,52},{24,56},{28,60},{32,0... | collective-permute-start | bytes 344072 | tf_op jit(solution)/shard_map/ppermute | solution.py:448
  51.7 0.9 %collective-permute-done.14.f1 = bf16[64,896]{1,0:T(8,128)(2,1)S(1)} collective-permute-done((bf16[64,896]{1,0:T(8,128)(2,1)S(1)}, bf16[64,896]{1,0:T(8,128)(2,1)S(1)}, u32[]{:S(2)}, u32[]{:S(2)}) %collective-permute-start.14) | collective-permute-done | bytes 114720 | tf_op jit(solution)/shard_map/ppermute | solution.py:448
  52.6 6.0 %collective-permute-done.15.f2 = bf16[64,896]{1,0:T(8,128)(2,1)S(1)} collective-permute-done((bf16[64,896]{1,0:T(8,128)(2,1)S(1)}, bf16[64,896]{1,0:T(8,128)(2,1)S(1)}, u32[]{:S(2)}, u32[]{:S(2)}) %collective-permute-start.15) | collective-permute-done | bytes 114720 | tf_op jit(solution)/shard_map/ppermute | solution.py:448
  58.6 1.1 %collective-permute-start.17 = (bf16[192,1024]{1,0:T(8,128)(2,1)S(1)}, bf16[192,1024]{1,0:T(8,128)(2,1)S(1)}, u32[]{:S(2)}, u32[]{:S(2)}) collective-permute-start(bf16[192,1024]{1,0:T(8,128)(2,1)S(1)} %collective-permute-done.10.rest_z), channel_id=1, source_target_pairs={{0,4},{4,0},{8,12},{12,8},{16,20},{20,16},{24,28},{28,24},{32,36},... | collective-permute-start | bytes 1179656 | tf_op jit(solution)/shard_map/ppermute | solution.py:448
  59.7 1.3 %collective-permute-done.17.rest_zc = bf16[192,1024]{1,0:T(8,128)(2,1)S(1)} collective-permute-done((bf16[192,1024]{1,0:T(8,128)(2,1)S(1)}, bf16[192,1024]{1,0:T(8,128)(2,1)S(1)}, u32[]{:S(2)}, u32[]{:S(2)}) %collective-permute-start.17) | collective-permute-done | bytes 393248 | tf_op jit(solution)/shard_map/ppermute | solution.py:448
  61.0 3.3 %join.1 = bf16[1024,512]{1,0:T(8,128)(2,1)} custom-call(bf16[64,1024]{1,0:T(8,128)(2,1)S(1)} %collective-permute-done.far_z, bf16[1024,256]{1,0:T(8,128)(2,1)S(1)} %get-tuple-element.56.res, bf16[256,512]{1,0:T(8,128)(2,1)S(1)} %get-tuple-element.57.q, f32[448,512]{1,0:T(8,128)S(1)} %get-tuple-element.59.km, f32[448,512]{1,0:T(8,128)S(1)} %get-tuple-element.60.kl, ...), custom_call_target="tpu_custom_call" | custom-call | bytes 1000 | tf_op jit(solution)/shard_map/join/pallas_call | solution.py:422
  (32 shorter events, 3.4 us)
Async XLA Ops:
  0.0 14.2 %copy-start.4 = (bf16[1024,512]{1,0:T(8,128)(2,1)S(1)}, bf16[1024,512]{1,0:T(8,128)(2,1)}, u32[]{:S(2)}) copy-start(bf16[1024,512]{1,0:T(8,128)(2,1)} %q_hbm.1) | copy-start | bytes 3145732
  3.3 10.9 %copy-start.5 = (s32[8,128]{1,0:T(8,128)S(1)}, s32[8,128]{1,0:T(8,128)}, u32[]{:S(2)}) copy-start(s32[8,128]{1,0:T(8,128)} %get-tuple-element.51.offs) | copy-start | bytes 12292
  3.3 12.0 %collective-permute-start.1 = (bf16[512,1024]{1,0:T(8,128)(2,1)}, bf16[512,1024]{1,0:T(8,128)(2,1)S(1)}, u32[]{:S(2)}, u32[]{:S(2)}) collective-permute-start(bf16[512,1024]{1,0:T(8,128)(2,1)} %get-tuple-element.53), channel_id=1, source_target_pairs={{0,4},{4,0},{8,12},{12,8},{16,20},{20,16},{24,28},{28,24},{32,36},... | collective-permute-start | bytes 3145736 | tf_op jit(solution)/shard_map/ppermute | solution.py:448
  6.6 12.7 %collective-permute-start = (bf16[64,1024]{1,0:T(8,128)(2,1)}, bf16[64,1024]{1,0:T(8,128)(2,1)S(1)}, u32[]{:S(2)}, u32[]{:S(2)}) collective-permute-start(bf16[64,1024]{1,0:T(8,128)(2,1)} %get-tuple-element.50.kv_far.far), channel_id=1, source_target_pairs={{0,8},{4,12},{8,0},{12,4},{16,24},{20,28},{24,16},{28,20},{32,40},... | collective-permute-start | bytes 393224 | tf_op jit(solution)/shard_map/ppermute | solution.py:448
  11.8 25.5 %collective-permute-start.5 = (bf16[256,1024]{1,0:T(8,128)(2,1)}, bf16[256,1024]{1,0:T(8,128)(2,1)S(1)}, u32[]{:S(2)}, u32[]{:S(2)}) collective-permute-start(bf16[256,1024]{1,0:T(8,128)(2,1)} %get-tuple-element.63), channel_id=1, source_target_pairs={{4,8},{12,16},{20,24},{28,32},{36,40},{44,48},{52,56},{60,64},{68,... | collective-permute-start | bytes 1572872 | tf_op jit(solution)/shard_map/ppermute | solution.py:456
  14.2 9.3 %copy-start.2 = (bf16[64,1024]{1,0:T(8,128)(2,1)S(1)}, bf16[64,1024]{1,0:T(8,128)(2,1)}, u32[]{:S(2)}) copy-start(bf16[64,1024]{1,0:T(8,128)(2,1)} %get-tuple-element.50.kv_far.far) | copy-start | bytes 393220
  14.2 19.3 %copy-start = (bf16[1024,512]{1,0:T(8,128)(2,1)S(1)}, bf16[1024,512]{1,0:T(8,128)(2,1)}, u32[]{:S(2)}) copy-start(bf16[1024,512]{1,0:T(8,128)(2,1)} %k.1) | copy-start | bytes 3145732
  14.3 19.2 %copy-start.1 = (bf16[1024,512]{1,0:T(8,128)(2,1)S(1)}, bf16[1024,512]{1,0:T(8,128)(2,1)}, u32[]{:S(2)}) copy-start(bf16[1024,512]{1,0:T(8,128)(2,1)} %v.1) | copy-start | bytes 3145732
  15.3 11.8 %copy-start.3 = (bf16[192,1024]{1,0:T(8,128)(2,1)S(1)}, bf16[192,1024]{1,0:T(8,128)(2,1)}, u32[]{:S(2)}) copy-start(bf16[192,1024]{1,0:T(8,128)(2,1)} %get-tuple-element.69.rest) | copy-start | bytes 1179652
  15.3 4.6 %collective-permute-start.2 = (bf16[64,512]{1,0:T(8,128)(2,1)S(1)}, bf16[64,512]{1,0:T(8,128)(2,1)S(1)}, u32[]{:S(2)}, u32[]{:S(2)}) collective-permute-start(bf16[64,512]{1,0:T(8,128)(2,1)S(1)} %get-tuple-element.54.refs_0_), channel_id=1, source_target_pairs={{0,16},{4,20},{8,24},{12,28},{16,32},{20,36},{24,40},{28,44},{32,4... | collective-permute-start | bytes 196616 | tf_op jit(solution)/shard_map/ppermute | solution.py:448
  16.2 3.7 %collective-permute-start.3 = (bf16[64,512]{1,0:T(8,128)(2,1)S(1)}, bf16[64,512]{1,0:T(8,128)(2,1)S(1)}, u32[]{:S(2)}, u32[]{:S(2)}) collective-permute-start(bf16[64,512]{1,0:T(8,128)(2,1)S(1)} %get-tuple-element.54.refs_0_), channel_id=1, source_target_pairs={{0,48},{4,52},{8,56},{12,60},{16,0},{20,4},{24,8},{28,12},{32,16},... | collective-permute-start | bytes 196616 | tf_op jit(solution)/shard_map/ppermute | solution.py:448
  18.1 5.5 %collective-permute-start.4 = (bf16[64,512]{1,0:T(8,128)(2,1)S(1)}, bf16[64,512]{1,0:T(8,128)(2,1)S(1)}, u32[]{:S(2)}, u32[]{:S(2)}) collective-permute-start(bf16[64,512]{1,0:T(8,128)(2,1)S(1)} %get-tuple-element.54.refs_0_), channel_id=1, source_target_pairs={{0,32},{4,36},{8,40},{12,44},{16,48},{20,52},{24,56},{28,60},{32,0... | collective-permute-start | bytes 196616 | tf_op jit(solution)/shard_map/ppermute | solution.py:448
  23.6 16.6 %collective-permute-start.6 = (bf16[128,1024]{1,0:T(8,128)(2,1)S(1)}, bf16[128,1024]{1,0:T(8,128)(2,1)S(1)}, u32[]{:S(2)}, u32[]{:S(2)}) collective-permute-start(bf16[128,1024]{1,0:T(8,128)(2,1)S(1)} %own.1.refs_4_), channel_id=1, source_target_pairs={{0,64},{4,68},{8,72},{12,76},{16,80},{20,84},{24,88},{28,92},{32,9... | collective-permute-start | bytes 786440 | tf_op jit(solution)/shard_map/ppermute | solution.py:448
  24.1 16.0 %collective-permute-start.7 = (bf16[128,1024]{1,0:T(8,128)(2,1)S(1)}, bf16[128,1024]{1,0:T(8,128)(2,1)S(1)}, u32[]{:S(2)}, u32[]{:S(2)}) collective-permute-start(bf16[128,1024]{1,0:T(8,128)(2,1)S(1)} %own.1.refs_4_), channel_id=1, source_target_pairs={{0,192},{4,196},{8,200},{12,204},{16,208},{20,212},{24,216},{28,22... | collective-permute-start | bytes 786440 | tf_op jit(solution)/shard_map/ppermute | solution.py:448
  26.3 13.8 %collective-permute-start.8 = (bf16[128,1024]{1,0:T(8,128)(2,1)S(1)}, bf16[128,1024]{1,0:T(8,128)(2,1)S(1)}, u32[]{:S(2)}, u32[]{:S(2)}) collective-permute-start(bf16[128,1024]{1,0:T(8,128)(2,1)S(1)} %own.1.refs_4_), channel_id=1, source_target_pairs={{0,128},{4,132},{8,136},{12,140},{16,144},{20,148},{24,152},{28,15... | collective-permute-start | bytes 786440 | tf_op jit(solution)/shard_map/ppermute | solution.py:448
  27.1 24.6 %collective-permute-start.10 = (bf16[192,1024]{1,0:T(8,128)(2,1)S(1)}, bf16[192,1024]{1,0:T(8,128)(2,1)S(1)}, u32[]{:S(2)}, u32[]{:S(2)}) collective-permute-start(bf16[192,1024]{1,0:T(8,128)(2,1)S(1)} %copy-done.3), channel_id=1, source_target_pairs={{0,8},{4,12},{8,0},{12,4},{16,24},{20,28},{24,16},{28,20},{32,40},... | collective-permute-start | bytes 1179656 | tf_op jit(solution)/shard_map/ppermute | solution.py:448
  40.1 1.6 %collective-permute-start.9 = (bf16[128,1024]{1,0:T(8,128)(2,1)S(1)}, bf16[128,1024]{1,0:T(8,128)(2,1)S(1)}, u32[]{:S(2)}, u32[]{:S(2)}) collective-permute-start(bf16[128,1024]{1,0:T(8,128)(2,1)S(1)} %own.1.refs_4_), channel_id=1, source_target_pairs={{0,4},{4,0},{8,12},{12,8},{16,20},{20,16},{24,28},{28,24},{32,36},... | collective-permute-start | bytes 786440 | tf_op jit(solution)/shard_map/ppermute | solution.py:448
  40.2 1.9 %collective-permute-start.11 = (bf16[128,1024]{1,0:T(8,128)(2,1)S(1)}, bf16[128,1024]{1,0:T(8,128)(2,1)S(1)}, u32[]{:S(2)}, u32[]{:S(2)}) collective-permute-start(bf16[128,1024]{1,0:T(8,128)(2,1)S(1)} %collective-permute-done.6.refs_5_), channel_id=1, source_target_pairs={{0,4},{4,0},{8,12},{12,8},{16,20},{20,16},{24,28},{28,24},{32,36},... | collective-permute-start | bytes 786440 | tf_op jit(solution)/shard_map/ppermute | solution.py:448
  40.7 1.8 %collective-permute-start.12 = (bf16[128,1024]{1,0:T(8,128)(2,1)S(1)}, bf16[128,1024]{1,0:T(8,128)(2,1)S(1)}, u32[]{:S(2)}, u32[]{:S(2)}) collective-permute-start(bf16[128,1024]{1,0:T(8,128)(2,1)S(1)} %collective-permute-done.7.refs_6_), channel_id=1, source_target_pairs={{0,4},{4,0},{8,12},{12,8},{16,20},{20,16},{24,28},{28,24},{32,36},... | collective-permute-start | bytes 786440 | tf_op jit(solution)/shard_map/ppermute | solution.py:448
  40.8 2.0 %collective-permute-start.13 = (bf16[128,1024]{1,0:T(8,128)(2,1)S(1)}, bf16[128,1024]{1,0:T(8,128)(2,1)S(1)}, u32[]{:S(2)}, u32[]{:S(2)}) collective-permute-start(bf16[128,1024]{1,0:T(8,128)(2,1)S(1)} %collective-permute-done.8.refs_7_), channel_id=1, source_target_pairs={{0,4},{4,0},{8,12},{12,8},{16,20},{20,16},{24,28},{28,24},{32,36},... | collective-permute-start | bytes 786440 | tf_op jit(solution)/shard_map/ppermute | solution.py:448
  45.2 7.4 %collective-permute-start.14 = (bf16[64,896]{1,0:T(8,128)(2,1)S(1)}, bf16[64,896]{1,0:T(8,128)(2,1)S(1)}, u32[]{:S(2)}, u32[]{:S(2)}) collective-permute-start(bf16[64,896]{1,0:T(8,128)(2,1)S(1)} %get-tuple-element.85), channel_id=1, source_target_pairs={{0,48},{4,52},{8,56},{12,60},{16,0},{20,4},{24,8},{28,12},{32,16},... | collective-permute-start | bytes 344072 | tf_op jit(solution)/shard_map/ppermute | solution.py:448
  50.4 8.1 %collective-permute-start.15 = (bf16[64,896]{1,0:T(8,128)(2,1)S(1)}, bf16[64,896]{1,0:T(8,128)(2,1)S(1)}, u32[]{:S(2)}, u32[]{:S(2)}) collective-permute-start(bf16[64,896]{1,0:T(8,128)(2,1)S(1)} %get-tuple-element.86), channel_id=1, source_target_pairs={{0,16},{4,20},{8,24},{12,28},{16,32},{20,36},{24,40},{28,44},{32,4... | collective-permute-start | bytes 344072 | tf_op jit(solution)/shard_map/ppermute | solution.py:448
  50.4 8.1 %collective-permute-start.16 = (bf16[64,896]{1,0:T(8,128)(2,1)S(1)}, bf16[64,896]{1,0:T(8,128)(2,1)S(1)}, u32[]{:S(2)}, u32[]{:S(2)}) collective-permute-start(bf16[64,896]{1,0:T(8,128)(2,1)S(1)} %get-tuple-element.87), channel_id=1, source_target_pairs={{0,32},{4,36},{8,40},{12,44},{16,48},{20,52},{24,56},{28,60},{32,0... | collective-permute-start | bytes 344072 | tf_op jit(solution)/shard_map/ppermute | solution.py:448
  58.6 2.5 %collective-permute-start.17 = (bf16[192,1024]{1,0:T(8,128)(2,1)S(1)}, bf16[192,1024]{1,0:T(8,128)(2,1)S(1)}, u32[]{:S(2)}, u32[]{:S(2)}) collective-permute-start(bf16[192,1024]{1,0:T(8,128)(2,1)S(1)} %collective-permute-done.10.rest_z), channel_id=1, source_target_pairs={{0,4},{4,0},{8,12},{12,8},{16,20},{20,16},{24,28},{28,24},{32,36},... | collective-permute-start | bytes 1179656 | tf_op jit(solution)/shard_map/ppermute | solution.py:448

commit v3 on v2

--- a/solution.py
+++ b/solution.py
@@ -11,6 +11,8 @@
 DH = 128
 W0 = 256
 BLOCKS = 4
+R1 = 4
+R2 = 16
 TOK = 1024
 COLS = 512
 NEAR = 64
@@ -105,40 +107,43 @@
 
 
 def extract_kernel(
-    off_hbm, k_hbm, v_hbm, offs, kv_far, kv_rest, halo, pack, off, k, v, off_sem, sems
+    off_hbm, k_hbm, v_hbm, offs, kv_far, kv_rest, kv_near, halo, off, k, v, k32, v32, off_sem, sems
 ):
     off_copy = pltpu.make_async_copy(off_hbm, off, off_sem)
     off_copy.start()
     copies = {}
-    for b in range(BLOCKS):
+    for b in reversed(range(BLOCKS)):
         for i, (src, dst) in enumerate(((k_hbm, k), (v_hbm, v))):
             copies[i, b] = pltpu.make_async_copy(
                 src.at[block_rows(b), :], dst.at[block_rows(b), :], sems.at[i, b]
             )
             copies[i, b].start()
     off_copy.wait()
-    sels = []
     for h in range(HEADS):
         offs[h : h + 1, :] = jnp.full((1, DH), off[h], jnp.int32)
-        sels.append(select_matrix(off[h], OTHER, NEAR))
-    for b in range(BLOCKS):
+    for b in reversed(range(BLOCKS)):
         rows = block_rows(b)
-        copies[0, b].wait()
-        copies[1, b].wait()
-        f, r = slice(b * FAR, (b + 1) * FAR), slice(b * REST, (b + 1) * REST)
-        g = slice(FROWS + b * REST, FROWS + (b + 1) * REST)
-        for h in range(HEADS):
-            c, d = head_cols(h), value_cols(h)
-            picked = dot(sels[h], jnp.concatenate([k[rows, c], v[rows, c]], 1)).astype(BF16)
-            for cols, part in ((c, picked[:, :DH]), (d, picked[:, DH:])):
-                kv_far[f, cols] = part[:FAR]
-                pack[f, cols] = part[:FAR]
-                kv_rest[r, cols] = part[FAR:]
-                pack[g, cols] = part[FAR:]
-    last = block_rows(BLOCKS - 1)
-    for out, rows in ((halo, slice(0, W0)), (pack, slice(NROWS, NROWS + W0))):
-        out[rows, :COLS] = k[last, :]
-        out[rows, COLS:] = v[last, :]
+        for i, (src, dst) in enumerate(((k, k32), (v, v32))):
+            copies[i, b].wait()
+            if b == BLOCKS - 1:
+                copies[i, BLOCKS] = pltpu.make_async_copy(
+                    src.at[rows, :], halo.at[:, i * COLS : (i + 1) * COLS], sems.at[i, BLOCKS]
+                )
+                copies[i, BLOCKS].start()
+            for h in range(HEADS):
+                dst[h, rows, :] = src[rows, head_cols(h)].astype(F32)
+    for h in range(HEADS):
+        for a in range(R2 // R1):
+            start = (off[h] + R1 * a) & (R2 - 1)
+            for src, cols in ((k32, head_cols(h)), (v32, value_cols(h))):
+                part = src[h, pl.ds(start, FROWS, stride=R2), :].astype(BF16)
+                kv_near[a * FROWS : (a + 1) * FROWS, cols] = part
+                if a == 0:
+                    kv_far[:, cols] = part
+                else:
+                    kv_rest[(a - 1) * FROWS : a * FROWS, cols] = part
+    for i in range(2):
+        copies[i, BLOCKS].wait()
 
 
 def extract(*args):
@@ -148,17 +153,19 @@
             out_of(8, DH, dtype=jnp.int32),
             out_of(FROWS, 2 * COLS),
             out_of(REST * BLOCKS, 2 * COLS),
+            out_of(NROWS, 2 * COLS),
             out_of(W0, 2 * COLS),
-            out_of(NROWS + W0, 2 * COLS),
         ],
         in_specs=[HBM] * 3,
-        out_specs=[VMEM] * 5,
+        out_specs=[VMEM] * 4 + [HBM],
         scratch_shapes=[
             pltpu.SMEM((HEADS,), jnp.int32),
             pltpu.VMEM((TOK, COLS), BF16),
             pltpu.VMEM((TOK, COLS), BF16),
+            pltpu.VMEM((HEADS, TOK, DH), F32),
+            pltpu.VMEM((HEADS, TOK, DH), F32),
             pltpu.SemaphoreType.DMA,
-            pltpu.SemaphoreType.DMA((2, BLOCKS)),
+            pltpu.SemaphoreType.DMA((2, BLOCKS + 1)),
         ],
         compiler_params=params(59),
         cost_estimate=cost(0),
@@ -205,7 +212,7 @@
         out_specs=[VMEM] * 4,
         scratch_shapes=[pltpu.VMEM((TOK, COLS), BF16), pltpu.SemaphoreType.DMA((BLOCKS,))],
         compiler_params=params(16),
-        cost_estimate=cost(3),
+        cost_estimate=cost(12),
         name="queries",
     )(*args)
 
@@ -286,14 +293,14 @@
     )(*args)
 
 
-def halo_kernel(res, q, km, kl, ka, pack, halo, done, hm, hl, ha):
+def halo_kernel(res, q, km, kl, ka, halo_c, halo, done, hm, hl, ha):
     position = lax.axis_index("seq")
     from_core = (position & 1) == 1
     has_halo = position > 0
     for h in range(HEADS):
         c, d = head_cols(h), value_cols(h)
-        hk = jnp.where(from_core, pack[NROWS:, c], halo[:, c])
-        hv = jnp.where(from_core, pack[NROWS:, d], halo[:, d])
+        hk = jnp.where(from_core, halo_c[:, c], halo[:, c])
+        hv = jnp.where(from_core, halo_c[:, d], halo[:, d])
         m = km[:W0, c]
         s = jnp.where(has_halo, dot_nt(q[:W0, c], hk) * SCALE2, -jnp.inf)
         m_new = jnp.maximum(m, wide(jnp.max(s, axis=1, keepdims=True)))
@@ -319,25 +326,51 @@
     )(*args)
 
 
-def near_kernel(q, far, rest, pack, m, l, acc):
+def near_kernel(q, km, kl, ka, hm, hl, ha, near, near_c, far_z, m, l, acc):
     for h in range(HEADS):
         c, d = head_cols(h), value_cols(h)
         k, v = (
-            jnp.concatenate([far[:, cols], rest[:, cols], pack[:NROWS, cols]], 0)
+            jnp.concatenate([near[:, cols], near_c[:, cols], far_z[:, cols]], 0)
             for cols in (c, d)
         )
-        m[:, c], l[:, c], acc[:, c] = attend(q[:, c], k, v)
+        state = tuple(
+            jnp.concatenate([x[:, c], y[W0:, c]], 0) for x, y in ((hm, km), (hl, kl), (ha, ka))
+        )
+        m[:, c], l[:, c], acc[:, c] = merge([state, attend(q[:, c], k, v)])
 
 
 def near(*args):
     return pl.pallas_call(
         near_kernel,
         out_shape=[out_of(NROWS, COLS, dtype=F32)] * 3,
-        in_specs=[VMEM] * 4,
+        in_specs=[VMEM] * 10,
         out_specs=[VMEM] * 3,
         compiler_params=params(16),
         cost_estimate=cost(0),
         name="near",
+    )(*args)
+
+
+def across_kernel(q, nm, nl, na, far_zc, rest_z, m, l, acc):
+    for h in range(HEADS):
+        c, d = head_cols(h), value_cols(h)
+        k, v = (
+            jnp.concatenate([far_zc[FROWS:, cols], rest_z[:, cols]], 0) for cols in (c, d)
+        )
+        m[:, c], l[:, c], acc[:, c] = merge(
+            [(nm[:, c], nl[:, c], na[:, c]), attend(q[:, c], k, v)]
+        )
+
+
+def across(*args):
+    return pl.pallas_call(
+        across_kernel,
+        out_shape=[out_of(NROWS, COLS, dtype=F32)] * 3,
+        in_specs=[VMEM] * 6,
+        out_specs=[VMEM] * 3,
+        compiler_params=params(16),
+        cost_estimate=cost(0),
+        name="across",
     )(*args)
 
 
@@ -377,33 +410,48 @@
     )(*args)
 
 
-def join_kernel(
-    far_z, res, q, km, kl, ka, hm, hl, ha, nm, nl, na, far_zc, rest_z, rest_zc, done0, done, f0, f1, f2, f3, out
-):
+def fold_kernel(f0, f1, f2, f3, m, l, acc):
     fars = (f0, f1, f2, f3)
     lses = [
         sum(f[:, COLS + e * DH : COLS + (e + 1) * DH].astype(F32) for e in range(3)) for f in fars
     ]
     for h in range(HEADS):
+        c = head_cols(h)
+        m[:, c], l[:, c], acc[:, c] = merge(
+            [
+                (wide(x[:, h : h + 1]), jnp.ones((FROWS, DH), F32), f[:, c].astype(F32))
+                for x, f in zip(lses, fars)
+            ]
+        )
+
+
+def fold(*args):
+    return pl.pallas_call(
+        fold_kernel,
+        out_shape=[out_of(FROWS, COLS, dtype=F32)] * 3,
+        in_specs=[VMEM] * 4,
+        out_specs=[VMEM] * 3,
+        compiler_params=params(8),
+        cost_estimate=cost(5),
+        name="fold",
+    )(*args)
+
+
+def join_kernel(
+    far_z, res, q, nm, nl, na, rest_zc, done0, done, fm, fl, fa, out, block, sems
+):
+    restored = []
+    for h in range(HEADS):
         c, d = head_cols(h), value_cols(h)
-        k, v = (
-            jnp.concatenate(
-                [far_z[:, cols], far_zc[FROWS:, cols], rest_z[:, cols], rest_zc[:, cols]], 0
-            )
-            for cols in (c, d)
-        )
-        state = tuple(
-            jnp.concatenate([x[:, c], y[W0:, c]], 0) for x, y in ((hm, km), (hl, kl), (ha, ka))
-        )
-        m, l, acc = merge([state, (nm[:, c], nl[:, c], na[:, c]), attend(q[:, c], k, v)])
-        parts = [(wide(x[:, h : h + 1]), f[:, c].astype(F32)) for x, f in zip(lses, fars)]
-        restored = []
+        m, l, acc = merge(
+            [(nm[:, c], nl[:, c], na[:, c]), attend(q[:, c], rest_zc[:, c], rest_zc[:, d])]
+        )
         for b in range(BLOCKS):
             rows = slice(b * NEAR, (b + 1) * NEAR)
             mb, lb, ab = m[rows], l[rows], acc[rows]
             fr = slice(b * FAR, (b + 1) * FAR)
             _, lf, af = merge(
-                [(mb[:FAR], lb[:FAR], ab[:FAR])] + [(x[fr], 1.0, o[fr]) for x, o in parts]
+                [(mb[:FAR], lb[:FAR], ab[:FAR]), (fm[fr, c], fl[fr, c], fa[fr, c])]
             )
             restored.append(
                 (
@@ -411,19 +459,32 @@
                     * (1.0 / jnp.concatenate([lf, lb[FAR:]], 0))
                 ).astype(BF16)
             )
-        placed = dot(res[block_rows(h), OTHER:], jnp.concatenate(restored, 1)).astype(BF16)
-        out[:W0, c] = done0[:, c] + placed[:, :DH]
-        for b in range(1, BLOCKS):
-            rows = slice((b - 1) * W0, b * W0)
-            out[block_rows(b), c] = done[rows, c] + placed[:, b * DH : (b + 1) * DH]
+    copies = []
+    for b in range(0, BLOCKS, 2):
+        for h in range(HEADS):
+            c = head_cols(h)
+            pair = jnp.concatenate(restored[h * BLOCKS + b : h * BLOCKS + b + 2], 1)
+            placed = dot(res[block_rows(h), OTHER:], pair).astype(BF16)
+            for i in range(2):
+                rest = done0[:, c] if b + i == 0 else done[block_rows(b + i - 1), c]
+                block[block_rows(b + i), c] = rest + placed[:, i * DH : (i + 1) * DH]
+        for i in range(2):
+            rows = block_rows(b + i)
+            copies.append(
+                pltpu.make_async_copy(block.at[rows, :], out.at[rows, :], sems.at[b + i])
+            )
+            copies[-1].start()
+    for copy in copies:
+        copy.wait()
 
 
 def join(*args):
     return pl.pallas_call(
         join_kernel,
         out_shape=out_of(TOK, COLS),
-        in_specs=[VMEM] * 21,
-        out_specs=VMEM,
+        in_specs=[VMEM] * 12,
+        out_specs=HBM,
+        scratch_shapes=[pltpu.VMEM((TOK, COLS), BF16), pltpu.SemaphoreType.DMA((BLOCKS,))],
         compiler_params=params(16),
         cost_estimate=cost(0),
         name="join",
@@ -449,31 +510,35 @@
 
 
 def shards(q, k, v, off):
-    offs, kv_far, kv_rest, halo, pack = extract(off, k, v)
+    offs, kv_far, kv_rest, kv_near, halo = extract(off, k, v)
     far_z = send(kv_far, dz=1)
-    pack_c = send(pack, dcore=1)
+    near_c = send(kv_near, dcore=1)
+    halo_c = send(halo, dcore=1)
     qp, qn, qf, res = permute_queries(offs, q)
+    halo, near_c = lax.optimization_barrier((halo, near_c))
     halo = lax.ppermute(halo, "seq", [(s, s + 1) for s in range(1, 63, 2)])
-    qf, pack_c = lax.optimization_barrier((qf, pack_c))
-    qs = [send(qf, dy=s) for s in (1, -1, 2)]
-    far_z, qs = lax.optimization_barrier((far_z, qs))
+    qf, halo_c = lax.optimization_barrier((qf, halo_c))
+    qs = [send(qf, dy=s) for s in (2, 1, -1)]
+    far_z, *qs = lax.optimization_barrier((far_z, *qs))
     own = join_far(kv_far, far_z)
-    own, kv_rest = lax.optimization_barrier((own, kv_rest))
-    gathered = [own] + [send(own, dx=s) for s in (1, -1, 2)]
+    kv_rest, _ = lax.optimization_barrier((kv_rest, own))
+    gathered = [send(own, dx=s) for s in (2, 1, -1)]
     rest_z = send(kv_rest, dz=1)
-    done, km, kl, ka = local(res, qp, k, v)
-    near_state = near(qn, kv_far, kv_rest, pack_c)
-    done0, *halo_state = halo_fold(res, qp, km, kl, ka, pack_c, halo)
-    gathered, near_state, done0 = lax.optimization_barrier((gathered, near_state, done0))
+    done, *kept = local(res, qp, k, v)
+    done0, *halo_state = halo_fold(res, qp, *kept, halo_c, halo)
+    own, _ = lax.optimization_barrier((own, done0))
+    own_c = send(own, dcore=1)
+    gathered, _ = lax.optimization_barrier((gathered, done0))
     crossed = [send(x, dcore=1) for x in gathered]
-    parts = far(qf, *qs, *gathered, *crossed)
-    back = [parts[0]] + [send(p, dy=-s) for p, s in zip(parts[1:], (1, -1, 2))]
-    rest_z, *back = lax.optimization_barrier((rest_z, *back))
+    parts = far(qf, *qs, own, *gathered, own_c, *crossed)
+    back = [parts[0]] + [send(p, dy=-s) for p, s in zip(parts[1:], (2, 1, -1))]
+    folded = fold(*back)
+    qn, _ = lax.optimization_barrier((qn, parts[0]))
+    state = near(qn, *kept, *halo_state, kv_near, near_c, far_z)
+    rest_z, _ = lax.optimization_barrier((rest_z, state[0]))
     rest_zc = send(rest_z, dcore=1)
-    return join(
-        far_z, res, qn, km, kl, ka, *halo_state, *near_state, crossed[0], rest_z, rest_zc,
-        done0, done, *back,
-    )
+    state = across(qn, *state, own_c, rest_z)
+    return join(far_z, res, qn, *state, rest_zc, done0, done, *folded)
 
 
 def solution(mesh):

time: 64.4 us -> 59.1 us (0.918)
  waiting for transfers between devices: 14.1 us -> 5.33 us
  starting transfers between devices: 33.5 us -> 35.9 us
    ppermute x17 -> x18, waiting for transfers between devices: 14.1 us -> 5.33 us  [send(): return lax.ppermute(value, 'seq', moves(**shift))]
    ppermute x17 -> x18, starting transfers between devices: 31.2 us -> 32.4 us  [send(): return lax.ppermute(value, 'seq', moves(**shift))]
    pallas_call x1, Pallas kernels: 3.31 us -> 2.13 us  [join(): pl.pallas_call(join_kernel, out_shape=out_of(TOK, COLS), in_specs=[VMEM]...]
    ppermute x1, starting transfers between devices: 2.37 us -> 3.55 us  [shards(): halo = lax.ppermute(halo, 'seq', [(s, s + 1) for s in range(1, 63, 2)])]
    pallas_call x0 -> x2, Pallas kernels: none -> 1.09 us  [the longest x1 0.86 us: across(): pl.pallas_call(across_kernel, out_shape=[out_of(NROWS, COLS, dtype=F32)]...]
  transfers between devices with their start and end apart: 18 -> 19, of which waited for: 9 -> 6; matrix products, arithmetic and copies ran while one was open for 0% -> 0% of each run, Pallas kernels for 15% -> 20%
where the time goes in v3:
time: 59.1 us; the launch traced here: 58.6 us
  starting transfers between devices  35.9 us (61%)
  Pallas kernels  16.9 us (29%)
  waiting for transfers between devices  5.33 us (9%)
    ppermute x18, starting transfers between devices, send(): return lax.ppermute(value, 'seq', moves(**shift))  32.4 us
    ppermute x18, waiting for transfers between devices, send(): return lax.ppermute(value, 'seq', moves(**shift))  5.33 us
    pallas_call x1, Pallas kernels, local(): pl.pallas_call(local_kernel, out_shape=[out_of(TOK - W0, COLS), state, st...  3.83 us
    ppermute x1, starting transfers between devices, shards(): halo = lax.ppermute(halo, 'seq', [(s, s + 1) for s in range(1, 63, 2)])  3.55 us
    pallas_call x1, Pallas kernels, extract(): pl.pallas_call(extract_kernel, out_shape=[out_of(8, DH, dtype=jnp.int32),...  3.22 us
    pallas_call x1, Pallas kernels, far(): pl.pallas_call(far_kernel, out_shape=[out_of(FROWS, SENT)] * 4, in_specs=...  2.3 us
    pallas_call x1, Pallas kernels, join(): pl.pallas_call(join_kernel, out_shape=out_of(TOK, COLS), in_specs=[VMEM]...  2.13 us
    pallas_call x1, Pallas kernels, near(): pl.pallas_call(near_kernel, out_shape=[out_of(NROWS, COLS, dtype=F32)] *...  1.84 us
  transfers between devices with their start and end apart: 19, of which 6 were waited for; matrix products, arithmetic and copies ran while one was open for 0% of the time, Pallas kernels for 20%

profile of v3, /device:TPU:1, one launch (start us, length us, event | category | flops | bytes accessed | tf_op | source)
XLA Modules:
  0.0 58.6 jit_solution(14343893021436616641)
XLA Ops:
  0.0 3.2 %extract.1 = (s32[8,128]{1,0:T(8,128)}, bf16[64,1024]{1,0:T(8,128)(2,1)}, bf16[192,1024]{1,0:T(8,128)(2,1)}, bf16[256,1024]{1,0:T(8,128)(2,1)}, bf16[256,1024]{1,0:T(8,128)(2,1)}) custom-call(s32[4]{0:T(128)} %off_hbm.1, bf16[1024,512]{1,0:T(8,128)(2,1)} %k.1, bf16[1024,512]{1,0:T(8,128)(2,1)} %v.1), custom_call_target="tpu_custom_call" | custom-call | bytes 1000 | tf_op jit(solution)/shard_map/extract/pallas_call | solution.py:150
  3.2 3.3 %collective-permute-start.5 = (bf16[256,1024]{1,0:T(8,128)(2,1)}, bf16[256,1024]{1,0:T(8,128)(2,1)S(1)}, u32[]{:S(2)}, u32[]{:S(2)}) collective-permute-start(bf16[256,1024]{1,0:T(8,128)(2,1)} %get-tuple-element.66.near), channel_id=1, source_target_pairs={{0,4},{4,0},{8,12},{12,8},{16,20},{20,16},{24,28},{28,24},{32,36},... | collective-permute-start | bytes 1572872 | tf_op jit(solution)/shard_map/ppermute | solution.py:509
  6.6 5.2 %collective-permute-start = (bf16[64,1024]{1,0:T(8,128)(2,1)}, bf16[64,1024]{1,0:T(8,128)(2,1)S(1)}, u32[]{:S(2)}, u32[]{:S(2)}) collective-permute-start(bf16[64,1024]{1,0:T(8,128)(2,1)} %get-tuple-element.50.kv_far), channel_id=1, source_target_pairs={{0,8},{4,12},{8,0},{12,4},{16,24},{20,28},{24,16},{28,20},{32,40},... | collective-permute-start | bytes 393224 | tf_op jit(solution)/shard_map/ppermute | solution.py:509
  12.1 3.5 %collective-permute-start.6 = (bf16[256,1024]{1,0:T(8,128)(2,1)}, bf16[256,1024]{1,0:T(8,128)(2,1)S(1)}, u32[]{:S(2)}, u32[]{:S(2)}) collective-permute-start(bf16[256,1024]{1,0:T(8,128)(2,1)} %get-tuple-element.67), channel_id=1, source_target_pairs={{4,8},{12,16},{20,24},{28,32},{36,40},{44,48},{52,56},{60,64},{68,... | collective-permute-start | bytes 1572872 | tf_op jit(solution)/shard_map/ppermute | solution.py:519
  15.7 1.0 %queries.1 = (bf16[1024,512]{1,0:T(8,128)(2,1)S(1)}, bf16[256,512]{1,0:T(8,128)(2,1)S(1)}, bf16[64,512]{1,0:T(8,128)(2,1)S(1)}, bf16[1024,256]{1,0:T(8,128)(2,1)S(1)}) custom-call(s32[8,128]{1,0:T(8,128)S(1)} %copy-done.5, bf16[1024,512]{1,0:T(8,128)(2,1)S(1)} %copy-done.4), custom_call_target="tpu_custom_call" | custom-call | flops 12000000000 | bytes 1000 | tf_op jit(solution)/shard_map/queries/pallas_call | solution.py:203
  16.8 3.0 %collective-permute-start.2 = (bf16[64,512]{1,0:T(8,128)(2,1)S(1)}, bf16[64,512]{1,0:T(8,128)(2,1)S(1)}, u32[]{:S(2)}, u32[]{:S(2)}) collective-permute-start(bf16[64,512]{1,0:T(8,128)(2,1)S(1)} %get-tuple-element.54.refs_0_), channel_id=1, source_target_pairs={{0,32},{4,36},{8,40},{12,44},{16,48},{20,52},{24,56},{28,60},{32,0... | collective-permute-start | bytes 196616 | tf_op jit(solution)/shard_map/ppermute | solution.py:509
  20.2 2.3 %collective-permute-start.4 = (bf16[64,512]{1,0:T(8,128)(2,1)S(1)}, bf16[64,512]{1,0:T(8,128)(2,1)S(1)}, u32[]{:S(2)}, u32[]{:S(2)}) collective-permute-start(bf16[64,512]{1,0:T(8,128)(2,1)S(1)} %get-tuple-element.54.refs_0_), channel_id=1, source_target_pairs={{0,48},{4,52},{8,56},{12,60},{16,0},{20,4},{24,8},{28,12},{32,16},... | collective-permute-start | bytes 196616 | tf_op jit(solution)/shard_map/ppermute | solution.py:509
  22.5 1.6 %collective-permute-done.3.refs_2_ = bf16[64,512]{1,0:T(8,128)(2,1)S(1)} collective-permute-done((bf16[64,512]{1,0:T(8,128)(2,1)S(1)}, bf16[64,512]{1,0:T(8,128)(2,1)S(1)}, u32[]{:S(2)}, u32[]{:S(2)}) %collective-permute-start.3) | collective-permute-done | bytes 65568 | tf_op jit(solution)/shard_map/ppermute | solution.py:509
  24.1 3.2 %collective-permute-start.7 = (bf16[128,1024]{1,0:T(8,128)(2,1)S(1)}, bf16[128,1024]{1,0:T(8,128)(2,1)S(1)}, u32[]{:S(2)}, u32[]{:S(2)}) collective-permute-start(bf16[128,1024]{1,0:T(8,128)(2,1)S(1)} %own.1.refs_4_), channel_id=1, source_target_pairs={{0,128},{4,132},{8,136},{12,140},{16,144},{20,148},{24,152},{28,15... | collective-permute-start | bytes 786440 | tf_op jit(solution)/shard_map/ppermute | solution.py:509
  27.6 2.4 %collective-permute-start.9 = (bf16[128,1024]{1,0:T(8,128)(2,1)S(1)}, bf16[128,1024]{1,0:T(8,128)(2,1)S(1)}, u32[]{:S(2)}, u32[]{:S(2)}) collective-permute-start(bf16[128,1024]{1,0:T(8,128)(2,1)S(1)} %own.1.refs_4_), channel_id=1, source_target_pairs={{0,192},{4,196},{8,200},{12,204},{16,208},{20,212},{24,216},{28,22... | collective-permute-start | bytes 786440 | tf_op jit(solution)/shard_map/ppermute | solution.py:509
  30.0 4.5 %collective-permute-start.14 = (bf16[192,1024]{1,0:T(8,128)(2,1)S(1)}, bf16[192,1024]{1,0:T(8,128)(2,1)S(1)}, u32[]{:S(2)}, u32[]{:S(2)}) collective-permute-start(bf16[192,1024]{1,0:T(8,128)(2,1)S(1)} %copy-done.6), channel_id=1, source_target_pairs={{0,8},{4,12},{8,0},{12,4},{16,24},{20,28},{24,16},{28,20},{32,40},... | collective-permute-start | bytes 1179656 | tf_op jit(solution)/shard_map/ppermute | solution.py:509
  34.5 3.8 %local.1 = (bf16[768,512]{1,0:T(8,128)(2,1)S(1)}, f32[448,512]{1,0:T(8,128)S(1)}, f32[448,512]{1,0:T(8,128)S(1)}, f32[448,512]{1,0:T(8,128)S(1)}) custom-call(bf16[1024,256]{1,0:T(8,128)(2,1)S(1)} %get-tuple-element.56.res, bf16[1024,512]{1,0:T(8,128)(2,1)S(1)} %get-tuple-element.61.q, bf16[1024,512]{1,0:T(8,128)(2,1)S(1)} %copy-done, ...), custom_call_target="tpu_custom_call" | custom-call | flops 1000000000 | bytes 1000 | tf_op jit(solution)/shard_map/local/pallas_call | solution.py:280
  38.3 1.4 %halo.1 = (bf16[256,512]{1,0:T(8,128)(2,1)S(1)}, f32[64,512]{1,0:T(8,128)S(1)}, f32[64,512]{1,0:T(8,128)S(1)}, f32[64,512]{1,0:T(8,128)S(1)}) custom-call(bf16[1024,256]{1,0:T(8,128)(2,1)S(1)} %get-tuple-element.56.res, bf16[1024,512]{1,0:T(8,128)(2,1)S(1)} %get-tuple-element.61.q, f32[448,512]{1,0:T(8,128)S(1)} %get-tuple-element.62.km, ...), custom_call_target="tpu_custom_call" | custom-call | bytes 1000 | tf_op jit(solution)/shard_map/halo/pallas_call | solution.py:318
  39.9 0.5 collective-permute-start.11
  40.9 0.5 collective-permute-done.10.refs_8_.far_zc
  42.5 2.3 %far.1 = (bf16[64,896]{1,0:T(8,128)(2,1)S(1)}, bf16[64,896]{1,0:T(8,128)(2,1)S(1)}, bf16[64,896]{1,0:T(8,128)(2,1)S(1)}, bf16[64,896]{1,0:T(8,128)(2,1)S(1)}) custom-call(bf16[64,512]{1,0:T(8,128)(2,1)S(1)} %get-tuple-element.54.refs_0_, bf16[64,512]{1,0:T(8,128)(2,1)S(1)} %collective-permute-done.2.refs_1_, ...), custom_call_target="tpu_custom_call" | custom-call | bytes 1000 | tf_op jit(solution)/shard_map/far/pallas_call | solution.py:402
  44.8 1.3 %collective-permute-start.16 = (bf16[64,896]{1,0:T(8,128)(2,1)S(1)}, bf16[64,896]{1,0:T(8,128)(2,1)S(1)}, u32[]{:S(2)}, u32[]{:S(2)}) collective-permute-start(bf16[64,896]{1,0:T(8,128)(2,1)S(1)} %get-tuple-element.89), channel_id=1, source_target_pairs={{0,32},{4,36},{8,40},{12,44},{16,48},{20,52},{24,56},{28,60},{32,0... | collective-permute-start | bytes 344072 | tf_op jit(solution)/shard_map/ppermute | solution.py:509
  46.1 3.8 %collective-permute-start.17 = (bf16[64,896]{1,0:T(8,128)(2,1)S(1)}, bf16[64,896]{1,0:T(8,128)(2,1)S(1)}, u32[]{:S(2)}, u32[]{:S(2)}) collective-permute-start(bf16[64,896]{1,0:T(8,128)(2,1)S(1)} %get-tuple-element.90), channel_id=1, source_target_pairs={{0,48},{4,52},{8,56},{12,60},{16,0},{20,4},{24,8},{28,12},{32,16},... | collective-permute-start | bytes 344072 | tf_op jit(solution)/shard_map/ppermute | solution.py:509
  49.9 0.5 collective-permute-start.18
  50.4 1.8 %near.1 = (f32[256,512]{1,0:T(8,128)S(1)}, f32[256,512]{1,0:T(8,128)S(1)}, f32[256,512]{1,0:T(8,128)S(1)}) custom-call(bf16[256,512]{1,0:T(8,128)(2,1)S(1)} %get-tuple-element.74.q, f32[448,512]{1,0:T(8,128)S(1)} %get-tuple-element.62.km, f32[448,512]{1,0:T(8,128)S(1)} %get-tuple-element.63.kl, f32[448,512]{1,0:T(8,128)S(1)} %get-tuple-element.64.ka, ...), custom_call_target="tpu_custom_call" | custom-call | bytes 1000 | tf_op jit(solution)/shard_map/near/pallas_call | solution.py:343
  52.3 0.8 %collective-permute-start.15 = (bf16[192,1024]{1,0:T(8,128)(2,1)S(1)}, bf16[192,1024]{1,0:T(8,128)(2,1)S(1)}, u32[]{:S(2)}, u32[]{:S(2)}) collective-permute-start(bf16[192,1024]{1,0:T(8,128)(2,1)S(1)} %collective-permute-done.14.rest_z), channel_id=1, source_target_pairs={{0,4},{4,0},{8,12},{12,8},{16,20},{20,16},{24,28},{28,24},{32,36},... | collective-permute-start | bytes 1179656 | tf_op jit(solution)/shard_map/ppermute | solution.py:509
  53.1 0.9 %across.1 = (f32[256,512]{1,0:T(8,128)S(1)}, f32[256,512]{1,0:T(8,128)S(1)}, f32[256,512]{1,0:T(8,128)S(1)}) custom-call(bf16[256,512]{1,0:T(8,128)(2,1)S(1)} %get-tuple-element.74.q, f32[256,512]{1,0:T(8,128)S(1)} %get-tuple-element.79.nm, f32[256,512]{1,0:T(8,128)S(1)} %get-tuple-element.80.nl, f32[256,512]{1,0:T(8,128)S(1)} %get-tuple-element.81.na, ...), custom_call_target="tpu_custom_call" | custom-call | bytes 1000 | tf_op jit(solution)/shard_map/across/pallas_call | solution.py:366
  54.0 2.0 %collective-permute-done.17.f2 = bf16[64,896]{1,0:T(8,128)(2,1)S(1)} collective-permute-done((bf16[64,896]{1,0:T(8,128)(2,1)S(1)}, bf16[64,896]{1,0:T(8,128)(2,1)S(1)}, u32[]{:S(2)}, u32[]{:S(2)}) %collective-permute-start.17) | collective-permute-done | bytes 114720 | tf_op jit(solution)/shard_map/ppermute | solution.py:509
  56.3 2.1 %join.1 = bf16[1024,512]{1,0:T(8,128)(2,1)} custom-call(bf16[64,1024]{1,0:T(8,128)(2,1)S(1)} %collective-permute-done.far_z, bf16[1024,256]{1,0:T(8,128)(2,1)S(1)} %get-tuple-element.56.res, bf16[256,512]{1,0:T(8,128)(2,1)S(1)} %get-tuple-element.74.q, f32[256,512]{1,0:T(8,128)S(1)} %get-tuple-element.85.nm, f32[256,512]{1,0:T(8,128)S(1)} %get-tuple-element.86.nl, ...), custom_call_target="tpu_custom_call" | custom-call | bytes 1000 | tf_op jit(solution)/shard_map/join/pallas_call | solution.py:482
  (38 shorter events, 3.1 us)
Async XLA Ops:
  0.0 15.7 %copy-start.4 = (bf16[1024,512]{1,0:T(8,128)(2,1)S(1)}, bf16[1024,512]{1,0:T(8,128)(2,1)}, u32[]{:S(2)}) copy-start(bf16[1024,512]{1,0:T(8,128)(2,1)} %q_hbm.1) | copy-start | bytes 3145732
  3.2 12.5 %copy-start.5 = (s32[8,128]{1,0:T(8,128)S(1)}, s32[8,128]{1,0:T(8,128)}, u32[]{:S(2)}) copy-start(s32[8,128]{1,0:T(8,128)} %get-tuple-element.51.offs) | copy-start | bytes 12292
  3.2 8.9 %collective-permute-start.5 = (bf16[256,1024]{1,0:T(8,128)(2,1)}, bf16[256,1024]{1,0:T(8,128)(2,1)S(1)}, u32[]{:S(2)}, u32[]{:S(2)}) collective-permute-start(bf16[256,1024]{1,0:T(8,128)(2,1)} %get-tuple-element.66.near), channel_id=1, source_target_pairs={{0,4},{4,0},{8,12},{12,8},{16,20},{20,16},{24,28},{28,24},{32,36},... | collective-permute-start | bytes 1572872 | tf_op jit(solution)/shard_map/ppermute | solution.py:509
  6.6 15.9 %collective-permute-start = (bf16[64,1024]{1,0:T(8,128)(2,1)}, bf16[64,1024]{1,0:T(8,128)(2,1)S(1)}, u32[]{:S(2)}, u32[]{:S(2)}) collective-permute-start(bf16[64,1024]{1,0:T(8,128)(2,1)} %get-tuple-element.50.kv_far), channel_id=1, source_target_pairs={{0,8},{4,12},{8,0},{12,4},{16,24},{20,28},{24,16},{28,20},{32,40},... | collective-permute-start | bytes 393224 | tf_op jit(solution)/shard_map/ppermute | solution.py:509
  11.8 5.0 %collective-permute-start.1 = (bf16[256,1024]{1,0:T(8,128)(2,1)}, bf16[256,1024]{1,0:T(8,128)(2,1)S(1)}, u32[]{:S(2)}, u32[]{:S(2)}) collective-permute-start(bf16[256,1024]{1,0:T(8,128)(2,1)} %get-tuple-element.67), channel_id=1, source_target_pairs={{0,4},{4,0},{8,12},{12,8},{16,20},{20,16},{24,28},{28,24},{32,36},... | collective-permute-start | bytes 1572872 | tf_op jit(solution)/shard_map/ppermute | solution.py:509
  12.1 26.2 %collective-permute-start.6 = (bf16[256,1024]{1,0:T(8,128)(2,1)}, bf16[256,1024]{1,0:T(8,128)(2,1)S(1)}, u32[]{:S(2)}, u32[]{:S(2)}) collective-permute-start(bf16[256,1024]{1,0:T(8,128)(2,1)} %get-tuple-element.67), channel_id=1, source_target_pairs={{4,8},{12,16},{20,24},{28,32},{36,40},{44,48},{52,56},{60,64},{68,... | collective-permute-start | bytes 1572872 | tf_op jit(solution)/shard_map/ppermute | solution.py:519
  15.7 18.7 %copy-start = (bf16[1024,512]{1,0:T(8,128)(2,1)S(1)}, bf16[1024,512]{1,0:T(8,128)(2,1)}, u32[]{:S(2)}) copy-start(bf16[1024,512]{1,0:T(8,128)(2,1)} %k.1) | copy-start | bytes 3145732
  15.7 18.7 %copy-start.1 = (bf16[1024,512]{1,0:T(8,128)(2,1)S(1)}, bf16[1024,512]{1,0:T(8,128)(2,1)}, u32[]{:S(2)}) copy-start(bf16[1024,512]{1,0:T(8,128)(2,1)} %v.1) | copy-start | bytes 3145732
  16.8 13.2 %copy-start.6 = (bf16[192,1024]{1,0:T(8,128)(2,1)S(1)}, bf16[192,1024]{1,0:T(8,128)(2,1)}, u32[]{:S(2)}) copy-start(bf16[192,1024]{1,0:T(8,128)(2,1)} %get-tuple-element.83) | copy-start | bytes 1179652
  16.8 5.7 %collective-permute-start.2 = (bf16[64,512]{1,0:T(8,128)(2,1)S(1)}, bf16[64,512]{1,0:T(8,128)(2,1)S(1)}, u32[]{:S(2)}, u32[]{:S(2)}) collective-permute-start(bf16[64,512]{1,0:T(8,128)(2,1)S(1)} %get-tuple-element.54.refs_0_), channel_id=1, source_target_pairs={{0,32},{4,36},{8,40},{12,44},{16,48},{20,52},{24,56},{28,60},{32,0... | collective-permute-start | bytes 196616 | tf_op jit(solution)/shard_map/ppermute | solution.py:509
  19.8 4.3 %collective-permute-start.3 = (bf16[64,512]{1,0:T(8,128)(2,1)S(1)}, bf16[64,512]{1,0:T(8,128)(2,1)S(1)}, u32[]{:S(2)}, u32[]{:S(2)}) collective-permute-start(bf16[64,512]{1,0:T(8,128)(2,1)S(1)} %get-tuple-element.54.refs_0_), channel_id=1, source_target_pairs={{0,16},{4,20},{8,24},{12,28},{16,32},{20,36},{24,40},{28,44},{32,4... | collective-permute-start | bytes 196616 | tf_op jit(solution)/shard_map/ppermute | solution.py:509
  20.2 3.9 %collective-permute-start.4 = (bf16[64,512]{1,0:T(8,128)(2,1)S(1)}, bf16[64,512]{1,0:T(8,128)(2,1)S(1)}, u32[]{:S(2)}, u32[]{:S(2)}) collective-permute-start(bf16[64,512]{1,0:T(8,128)(2,1)S(1)} %get-tuple-element.54.refs_0_), channel_id=1, source_target_pairs={{0,48},{4,52},{8,56},{12,60},{16,0},{20,4},{24,8},{28,12},{32,16},... | collective-permute-start | bytes 196616 | tf_op jit(solution)/shard_map/ppermute | solution.py:509
  24.1 15.6 %collective-permute-start.7 = (bf16[128,1024]{1,0:T(8,128)(2,1)S(1)}, bf16[128,1024]{1,0:T(8,128)(2,1)S(1)}, u32[]{:S(2)}, u32[]{:S(2)}) collective-permute-start(bf16[128,1024]{1,0:T(8,128)(2,1)S(1)} %own.1.refs_4_), channel_id=1, source_target_pairs={{0,128},{4,132},{8,136},{12,140},{16,144},{20,148},{24,152},{28,15... | collective-permute-start | bytes 786440 | tf_op jit(solution)/shard_map/ppermute | solution.py:509
  27.3 12.4 %collective-permute-start.8 = (bf16[128,1024]{1,0:T(8,128)(2,1)S(1)}, bf16[128,1024]{1,0:T(8,128)(2,1)S(1)}, u32[]{:S(2)}, u32[]{:S(2)}) collective-permute-start(bf16[128,1024]{1,0:T(8,128)(2,1)S(1)} %own.1.refs_4_), channel_id=1, source_target_pairs={{0,64},{4,68},{8,72},{12,76},{16,80},{20,84},{24,88},{28,92},{32,9... | collective-permute-start | bytes 786440 | tf_op jit(solution)/shard_map/ppermute | solution.py:509
  27.6 12.1 %collective-permute-start.9 = (bf16[128,1024]{1,0:T(8,128)(2,1)S(1)}, bf16[128,1024]{1,0:T(8,128)(2,1)S(1)}, u32[]{:S(2)}, u32[]{:S(2)}) collective-permute-start(bf16[128,1024]{1,0:T(8,128)(2,1)S(1)} %own.1.refs_4_), channel_id=1, source_target_pairs={{0,192},{4,196},{8,200},{12,204},{16,208},{20,212},{24,216},{28,22... | collective-permute-start | bytes 786440 | tf_op jit(solution)/shard_map/ppermute | solution.py:509
  30.0 22.3 %collective-permute-start.14 = (bf16[192,1024]{1,0:T(8,128)(2,1)S(1)}, bf16[192,1024]{1,0:T(8,128)(2,1)S(1)}, u32[]{:S(2)}, u32[]{:S(2)}) collective-permute-start(bf16[192,1024]{1,0:T(8,128)(2,1)S(1)} %copy-done.6), channel_id=1, source_target_pairs={{0,8},{4,12},{8,0},{12,4},{16,24},{20,28},{24,16},{28,20},{32,40},... | collective-permute-start | bytes 1179656 | tf_op jit(solution)/shard_map/ppermute | solution.py:509
  39.8 1.6 %collective-permute-start.10 = (bf16[128,1024]{1,0:T(8,128)(2,1)S(1)}, bf16[128,1024]{1,0:T(8,128)(2,1)S(1)}, u32[]{:S(2)}, u32[]{:S(2)}) collective-permute-start(bf16[128,1024]{1,0:T(8,128)(2,1)S(1)} %own.1.refs_4_), channel_id=1, source_target_pairs={{0,4},{4,0},{8,12},{12,8},{16,20},{20,16},{24,28},{28,24},{32,36},... | collective-permute-start | bytes 786440 | tf_op jit(solution)/shard_map/ppermute | solution.py:509
  39.9 1.9 %collective-permute-start.11 = (bf16[128,1024]{1,0:T(8,128)(2,1)S(1)}, bf16[128,1024]{1,0:T(8,128)(2,1)S(1)}, u32[]{:S(2)}, u32[]{:S(2)}) collective-permute-start(bf16[128,1024]{1,0:T(8,128)(2,1)S(1)} %collective-permute-done.7.refs_5_), channel_id=1, source_target_pairs={{0,4},{4,0},{8,12},{12,8},{16,20},{20,16},{24,28},{28,24},{32,36},... | collective-permute-start | bytes 786440 | tf_op jit(solution)/shard_map/ppermute | solution.py:509
  40.4 1.8 %collective-permute-start.12 = (bf16[128,1024]{1,0:T(8,128)(2,1)S(1)}, bf16[128,1024]{1,0:T(8,128)(2,1)S(1)}, u32[]{:S(2)}, u32[]{:S(2)}) collective-permute-start(bf16[128,1024]{1,0:T(8,128)(2,1)S(1)} %collective-permute-done.8.refs_6_), channel_id=1, source_target_pairs={{0,4},{4,0},{8,12},{12,8},{16,20},{20,16},{24,28},{28,24},{32,36},... | collective-permute-start | bytes 786440 | tf_op jit(solution)/shard_map/ppermute | solution.py:509
  40.5 2.0 %collective-permute-start.13 = (bf16[128,1024]{1,0:T(8,128)(2,1)S(1)}, bf16[128,1024]{1,0:T(8,128)(2,1)S(1)}, u32[]{:S(2)}, u32[]{:S(2)}) collective-permute-start(bf16[128,1024]{1,0:T(8,128)(2,1)S(1)} %collective-permute-done.9.refs_7_), channel_id=1, source_target_pairs={{0,4},{4,0},{8,12},{12,8},{16,20},{20,16},{24,28},{28,24},{32,36},... | collective-permute-start | bytes 786440 | tf_op jit(solution)/shard_map/ppermute | solution.py:509
  44.8 9.2 %collective-permute-start.16 = (bf16[64,896]{1,0:T(8,128)(2,1)S(1)}, bf16[64,896]{1,0:T(8,128)(2,1)S(1)}, u32[]{:S(2)}, u32[]{:S(2)}) collective-permute-start(bf16[64,896]{1,0:T(8,128)(2,1)S(1)} %get-tuple-element.89), channel_id=1, source_target_pairs={{0,32},{4,36},{8,40},{12,44},{16,48},{20,52},{24,56},{28,60},{32,0... | collective-permute-start | bytes 344072 | tf_op jit(solution)/shard_map/ppermute | solution.py:509
  46.1 9.9 %collective-permute-start.17 = (bf16[64,896]{1,0:T(8,128)(2,1)S(1)}, bf16[64,896]{1,0:T(8,128)(2,1)S(1)}, u32[]{:S(2)}, u32[]{:S(2)}) collective-permute-start(bf16[64,896]{1,0:T(8,128)(2,1)S(1)} %get-tuple-element.90), channel_id=1, source_target_pairs={{0,48},{4,52},{8,56},{12,60},{16,0},{20,4},{24,8},{28,12},{32,16},... | collective-permute-start | bytes 344072 | tf_op jit(solution)/shard_map/ppermute | solution.py:509
  49.9 6.1 %collective-permute-start.18 = (bf16[64,896]{1,0:T(8,128)(2,1)S(1)}, bf16[64,896]{1,0:T(8,128)(2,1)S(1)}, u32[]{:S(2)}, u32[]{:S(2)}) collective-permute-start(bf16[64,896]{1,0:T(8,128)(2,1)S(1)} %get-tuple-element.91), channel_id=1, source_target_pairs={{0,16},{4,20},{8,24},{12,28},{16,32},{20,36},{24,40},{28,44},{32,4... | collective-permute-start | bytes 344072 | tf_op jit(solution)/shard_map/ppermute | solution.py:509
  52.3 4.0 %collective-permute-start.15 = (bf16[192,1024]{1,0:T(8,128)(2,1)S(1)}, bf16[192,1024]{1,0:T(8,128)(2,1)S(1)}, u32[]{:S(2)}, u32[]{:S(2)}) collective-permute-start(bf16[192,1024]{1,0:T(8,128)(2,1)S(1)} %collective-permute-done.14.rest_z), channel_id=1, source_target_pairs={{0,4},{4,0},{8,12},{12,8},{16,20},{20,16},{24,28},{28,24},{32,36},... | collective-permute-start | bytes 1179656 | tf_op jit(solution)/shard_map/ppermute | solution.py:509
  (2 other events, 19.1 us)

commit v4 on v3

--- a/solution.py
+++ b/solution.py
@@ -22,7 +22,8 @@
 NROWS = NEAR * BLOCKS
 FROWS = FAR * BLOCKS
 KEPT = OTHER + NROWS
-SENT = COLS + 3 * DH
+HALF = COLS // 2
+SENT = HALF + DH
 SCALE2 = 128**-0.5 * 1.4426950408889634
 F32 = jnp.float32
 BF16 = jnp.bfloat16
@@ -173,7 +174,9 @@
     )(*args)
 
 
-def queries_kernel(offs, q_hbm, qp, qn, qf, res, q, sems):
+def queries_kernel(offs, q_hbm, qp, qn, q_keep, q_give, res, q, sems):
+    core = lax.axis_index("seq") & 1
+    qf = {}
     copies = []
     for b in range(BLOCKS):
         copies.append(
@@ -196,7 +199,13 @@
                 part = moved[:, i * DH : (i + 1) * DH]
                 qp[block_rows(b + i), c] = part
                 qn[(b + i) * NEAR : (b + i + 1) * NEAR, c] = part[OTHER:]
-                qf[(b + i) * FAR : (b + i + 1) * FAR, c] = part[OTHER : OTHER + FAR]
+                qf[b + i, h] = part[OTHER : OTHER + FAR]
+    for b in range(BLOCKS):
+        rows = slice(b * FAR, (b + 1) * FAR)
+        for g in range(HEADS // 2):
+            low, high = qf[b, g], qf[b, g + HEADS // 2]
+            q_keep[rows, head_cols(g)] = jnp.where(core == 0, low, high)
+            q_give[rows, head_cols(g)] = jnp.where(core == 0, high, low)
 
 
 def permute_queries(*args):
@@ -205,11 +214,12 @@
         out_shape=[
             out_of(TOK, COLS),
             out_of(NROWS, COLS),
-            out_of(FROWS, COLS),
+            out_of(FROWS, HALF),
+            out_of(FROWS, HALF),
             out_of(HEADS * W0, W0),
         ],
         in_specs=[VMEM, HBM],
-        out_specs=[VMEM] * 4,
+        out_specs=[VMEM] * 5,
         scratch_shapes=[pltpu.VMEM((TOK, COLS), BF16), pltpu.SemaphoreType.DMA((BLOCKS,))],
         compiler_params=params(16),
         cost_estimate=cost(12),
@@ -217,20 +227,67 @@
     )(*args)
 
 
-def own_kernel(kv_far, far_z, own):
-    own[:FROWS, :] = kv_far[...]
-    own[FROWS:, :] = far_z[...]
-
-
-def join_far(*args):
-    return pl.pallas_call(
-        own_kernel,
-        out_shape=out_of(2 * FROWS, 2 * COLS),
+def pick(ref, core, start):
+    return jnp.where(core == 0, ref[:, start : start + HALF], ref[:, start + HALF : start + COLS])
+
+
+def split_kernel(far_z, keep, give):
+    core = lax.axis_index("seq") & 1
+    for start in (0, COLS):
+        cols = slice(start // 2, start // 2 + HALF)
+        keep[:, cols] = pick(far_z, core, start)
+        give[:, cols] = pick(far_z, 1 - core, start)
+
+
+def split_far(*args):
+    return pl.pallas_call(
+        split_kernel,
+        out_shape=[out_of(FROWS, COLS)] * 2,
+        in_specs=[VMEM],
+        out_specs=[VMEM] * 2,
+        compiler_params=params(8),
+        cost_estimate=cost(0),
+        name="split",
+    )(*args)
+
+
+def keys_kernel(kv_far, near_c, keep, given, own):
+    core = lax.axis_index("seq") & 1
+    for i, src in enumerate((kv_far, near_c.at[:FROWS, :])):
+        rows = slice(i * FROWS, (i + 1) * FROWS)
+        own[rows, :HALF] = pick(src, core, 0)
+        own[rows, HALF:] = pick(src, core, COLS)
+    own[2 * FROWS : 3 * FROWS, :] = keep[...]
+    own[3 * FROWS :, :] = given[...]
+
+
+def pick_keys(*args):
+    return pl.pallas_call(
+        keys_kernel,
+        out_shape=out_of(4 * FROWS, COLS),
+        in_specs=[VMEM] * 4,
+        out_specs=VMEM,
+        compiler_params=params(8),
+        cost_estimate=cost(0),
+        name="keys",
+    )(*args)
+
+
+def half_kernel(keep, given, out):
+    core = lax.axis_index("seq") & 1
+    out[:FROWS, :] = jnp.where(core == 0, keep[...], given[...])
+    out[FROWS:, :] = jnp.where(core == 0, given[...], keep[...])
+
+
+def pick_queries(*args):
+    return pl.pallas_call(
+        half_kernel,
+        out_shape=out_of(2 * FROWS, HALF),
         in_specs=[VMEM] * 2,
         out_specs=VMEM,
         compiler_params=params(8),
         cost_estimate=cost(0),
-        name="own",
+        name="half",
     )(*args)
 
 
@@ -326,24 +383,25 @@
     )(*args)
 
 
-def near_kernel(q, km, kl, ka, hm, hl, ha, near, near_c, far_z, m, l, acc):
+def near_kernel(q, km, kl, ka, near, near_c, far_z, m, l, acc):
     for h in range(HEADS):
         c, d = head_cols(h), value_cols(h)
         k, v = (
             jnp.concatenate([near[:, cols], near_c[:, cols], far_z[:, cols]], 0)
             for cols in (c, d)
         )
-        state = tuple(
-            jnp.concatenate([x[:, c], y[W0:, c]], 0) for x, y in ((hm, km), (hl, kl), (ha, ka))
-        )
-        m[:, c], l[:, c], acc[:, c] = merge([state, attend(q[:, c], k, v)])
+        state = attend(q[:, c], k, v)
+        later = merge([(km[W0:, c], kl[W0:, c], ka[W0:, c]), tuple(x[NEAR:] for x in state)])
+        for ref, first, rest in zip((m, l, acc), state, later):
+            ref[:NEAR, c] = first[:NEAR]
+            ref[NEAR:, c] = rest
 
 
 def near(*args):
     return pl.pallas_call(
         near_kernel,
         out_shape=[out_of(NROWS, COLS, dtype=F32)] * 3,
-        in_specs=[VMEM] * 10,
+        in_specs=[VMEM] * 7,
         out_specs=[VMEM] * 3,
         compiler_params=params(16),
         cost_estimate=cost(0),
@@ -351,11 +409,23 @@
     )(*args)
 
 
-def across_kernel(q, nm, nl, na, far_zc, rest_z, m, l, acc):
+def across_kernel(q, nm, nl, na, given, other, rest_z, rest_zc, m, l, acc):
+    core = lax.axis_index("seq") & 1
     for h in range(HEADS):
         c, d = head_cols(h), value_cols(h)
         k, v = (
-            jnp.concatenate([far_zc[FROWS:, cols], rest_z[:, cols]], 0) for cols in (c, d)
+            jnp.concatenate(
+                [
+                    jnp.where(core == h // 2, given[:, half], other[:, half]),
+                    rest_z[:, cols],
+                    rest_zc[:, cols],
+                ],
+                0,
+            )
+            for cols, half in (
+                (c, head_cols(h % 2)),
+                (d, slice(HALF + h % 2 * DH, HALF + (h % 2 + 1) * DH)),
+            )
         )
         m[:, c], l[:, c], acc[:, c] = merge(
             [(nm[:, c], nl[:, c], na[:, c]), attend(q[:, c], k, v)]
@@ -366,7 +436,7 @@
     return pl.pallas_call(
         across_kernel,
         out_shape=[out_of(NROWS, COLS, dtype=F32)] * 3,
-        in_specs=[VMEM] * 6,
+        in_specs=[VMEM] * 8,
         out_specs=[VMEM] * 3,
         compiler_params=params(16),
         cost_estimate=cost(0),
@@ -375,11 +445,13 @@
 
 
 def far_kernel(*refs):
-    q, kv, out = refs[:4], refs[4:12], refs[12:]
+    q, kv, out = refs[:4], refs[4:8], refs[8:]
+    n = 2 * FROWS
     for part in out:
-        part[:, COLS:] = jnp.zeros((FROWS, 3 * DH), BF16)
-    for h in range(HEADS):
-        c, d = head_cols(h), value_cols(h)
+        part[:, HALF:] = jnp.zeros((n, DH), BF16)
+    for g in range(HEADS // 2):
+        c = head_cols(g)
+        d = slice(HALF + g * DH, HALF + (g + 1) * DH)
         qh = jnp.concatenate([x[:, c] for x in q], 0)
         k = jnp.concatenate([x[:, c] for x in kv], 0)
         v = jnp.concatenate([x[:, d] for x in kv], 0)
@@ -391,68 +463,75 @@
         second = left.astype(BF16)
         third = (left - second.astype(F32)).astype(BF16)
         for i, part in enumerate(out):
-            rows = slice(i * FROWS, (i + 1) * FROWS)
+            rows = slice(i * n, (i + 1) * n)
             part[:, c] = o[rows]
             for e, piece in enumerate((first, second, third)):
-                col = COLS + e * DH + h
+                col = HALF + 2 * e + g
                 part[:, col : col + 1] = piece[rows]
 
 
 def far(*args):
     return pl.pallas_call(
         far_kernel,
-        out_shape=[out_of(FROWS, SENT)] * 4,
-        in_specs=[VMEM] * 12,
+        out_shape=[out_of(2 * FROWS, SENT)] * 4,
+        in_specs=[VMEM] * 8,
         out_specs=[VMEM] * 4,
-        compiler_params=params(16),
+        compiler_params=params(24),
         cost_estimate=cost(0),
         name="far",
     )(*args)
 
 
-def fold_kernel(f0, f1, f2, f3, m, l, acc):
-    fars = (f0, f1, f2, f3)
-    lses = [
-        sum(f[:, COLS + e * DH : COLS + (e + 1) * DH].astype(F32) for e in range(3)) for f in fars
-    ]
+def fold_kernel(f0, f1, f2, f3, out):
+    for g in range(HEADS // 2):
+        c = head_cols(g)
+        states = []
+        for f in (f0, f1, f2, f3):
+            lse = sum(
+                f[:, HALF + 2 * e + g : HALF + 2 * e + g + 1].astype(F32) for e in range(3)
+            )
+            states.append((wide(lse), jnp.ones((2 * FROWS, DH), F32), f[:, c].astype(F32)))
+        m, l, acc = merge(states)
+        out[:, c] = acc * (1.0 / l)
+        out[:, HALF + g * DH : HALF + (g + 1) * DH] = m + jnp.log2(l)
+
+
+def fold(*args):
+    return pl.pallas_call(
+        fold_kernel,
+        out_shape=out_of(2 * FROWS, COLS, dtype=F32),
+        in_specs=[VMEM] * 4,
+        out_specs=VMEM,
+        compiler_params=params(8),
+        cost_estimate=cost(0),
+        name="fold",
+    )(*args)
+
+
+def join_kernel(
+    far_z, res, hm, hl, ha, nm, nl, na, done0, done, mine, mine_c, out, block, sems
+):
+    core = lax.axis_index("seq") & 1
+    restored = []
     for h in range(HEADS):
         c = head_cols(h)
-        m[:, c], l[:, c], acc[:, c] = merge(
-            [
-                (wide(x[:, h : h + 1]), jnp.ones((FROWS, DH), F32), f[:, c].astype(F32))
-                for x, f in zip(lses, fars)
-            ]
-        )
-
-
-def fold(*args):
-    return pl.pallas_call(
-        fold_kernel,
-        out_shape=[out_of(FROWS, COLS, dtype=F32)] * 3,
-        in_specs=[VMEM] * 4,
-        out_specs=[VMEM] * 3,
-        compiler_params=params(8),
-        cost_estimate=cost(5),
-        name="fold",
-    )(*args)
-
-
-def join_kernel(
-    far_z, res, q, nm, nl, na, rest_zc, done0, done, fm, fl, fa, out, block, sems
-):
-    restored = []
-    for h in range(HEADS):
-        c, d = head_cols(h), value_cols(h)
-        m, l, acc = merge(
-            [(nm[:, c], nl[:, c], na[:, c]), attend(q[:, c], rest_zc[:, c], rest_zc[:, d])]
+        m, l, acc = nm[:, c], nl[:, c], na[:, c]
+        g = h % 2
+        fo, fm = (
+            jnp.where(
+                core == h // 2,
+                jnp.where(core == 0, mine[:FROWS, cols], mine[FROWS:, cols]),
+                jnp.where(core == 0, mine_c[:FROWS, cols], mine_c[FROWS:, cols]),
+            )
+            for cols in (head_cols(g), slice(HALF + g * DH, HALF + (g + 1) * DH))
         )
         for b in range(BLOCKS):
             rows = slice(b * NEAR, (b + 1) * NEAR)
             mb, lb, ab = m[rows], l[rows], acc[rows]
+            if b == 0:
+                mb, lb, ab = merge([(hm[:, c], hl[:, c], ha[:, c]), (mb, lb, ab)])
             fr = slice(b * FAR, (b + 1) * FAR)
-            _, lf, af = merge(
-                [(mb[:FAR], lb[:FAR], ab[:FAR]), (fm[fr, c], fl[fr, c], fa[fr, c])]
-            )
+            _, lf, af = merge([(mb[:FAR], lb[:FAR], ab[:FAR]), (fm[fr], 1.0, fo[fr])])
             restored.append(
                 (
                     jnp.concatenate([af, ab[FAR:]], 0)
@@ -509,36 +588,51 @@
     return lax.ppermute(value, "seq", moves(**shift))
 
 
+def turn(value, step, keys):
+    pairs = []
+    for x in range(4):
+        for y in range(4):
+            for z in range(2):
+                for core in range(2):
+                    dx, dy = (step, 0) if (core == 0) == keys else (0, step)
+                    pairs.append((place(x, y, z, core), place(x + dx, y + dy, z, core)))
+    return lax.ppermute(value, "seq", pairs)
+
+
 def shards(q, k, v, off):
     offs, kv_far, kv_rest, kv_near, halo = extract(off, k, v)
     far_z = send(kv_far, dz=1)
     near_c = send(kv_near, dcore=1)
     halo_c = send(halo, dcore=1)
-    qp, qn, qf, res = permute_queries(offs, q)
-    halo, near_c = lax.optimization_barrier((halo, near_c))
+    kv_rest, near_c = lax.optimization_barrier((kv_rest, near_c))
+    rest_z = send(kv_rest, dz=1)
+    qp, qn, q_keep, q_give, res = permute_queries(offs, q)
+    q_give, halo_c = lax.optimization_barrier((q_give, halo_c))
+    qm = pick_queries(q_keep, send(q_give, dcore=1))
+    steps = (2, 1, -1)
+    qs = [turn(qm, s, False) for s in steps]
+    done, *kept = local(res, qp, k, v)
+    far_z, *_ = lax.optimization_barrier((far_z, done, *qs))
+    keep, give = split_far(far_z)
+    given = send(give, dcore=1)
+    own = pick_keys(kv_far, near_c, keep, given)
+    gathered = [own] + [turn(own, s, True) for s in steps]
+    halo, _ = lax.optimization_barrier((halo, own))
     halo = lax.ppermute(halo, "seq", [(s, s + 1) for s in range(1, 63, 2)])
-    qf, halo_c = lax.optimization_barrier((qf, halo_c))
-    qs = [send(qf, dy=s) for s in (2, 1, -1)]
-    far_z, *qs = lax.optimization_barrier((far_z, *qs))
-    own = join_far(kv_far, far_z)
-    kv_rest, _ = lax.optimization_barrier((kv_rest, own))
-    gathered = [send(own, dx=s) for s in (2, 1, -1)]
-    rest_z = send(kv_rest, dz=1)
-    done, *kept = local(res, qp, k, v)
+    rest_z, *_ = lax.optimization_barrier((rest_z, *gathered, done))
+    parts = far(qm, *qs, *gathered)
+    rest_zc = send(rest_z, dcore=1)
+    rest_zc, *parts = lax.optimization_barrier((rest_zc, *parts))
+    keep, *_ = lax.optimization_barrier((keep, *parts))
+    other = send(keep, dcore=1)
+    back = [parts[0]] + [turn(p, -s, False) for p, s in zip(parts[1:], steps)]
+    mine = fold(*back)
+    state = near(qn, *kept, kv_near, near_c, far_z)
+    state = across(qn, *state, given, other, rest_z, rest_zc)
     done0, *halo_state = halo_fold(res, qp, *kept, halo_c, halo)
-    own, _ = lax.optimization_barrier((own, done0))
-    own_c = send(own, dcore=1)
-    gathered, _ = lax.optimization_barrier((gathered, done0))
-    crossed = [send(x, dcore=1) for x in gathered]
-    parts = far(qf, *qs, own, *gathered, own_c, *crossed)
-    back = [parts[0]] + [send(p, dy=-s) for p, s in zip(parts[1:], (2, 1, -1))]
-    folded = fold(*back)
-    qn, _ = lax.optimization_barrier((qn, parts[0]))
-    state = near(qn, *kept, *halo_state, kv_near, near_c, far_z)
-    rest_z, _ = lax.optimization_barrier((rest_z, state[0]))
-    rest_zc = send(rest_z, dcore=1)
-    state = across(qn, *state, own_c, rest_z)
-    return join(far_z, res, qn, *state, rest_zc, done0, done, *folded)
+    mine, *_ = lax.optimization_barrier((mine, halo, state[0]))
+    mine_c = send(mine, dcore=1)
+    return join(far_z, res, *halo_state, *state, done0, done, mine, mine_c)
 
 
 def solution(mesh):

time: 59.1 us -> 55.9 us (0.946)
  waiting for transfers between devices: 5.33 us -> 2.77 us
  starting transfers between devices: 35.9 us -> 35 us
    ppermute x18 -> x9, starting transfers between devices: 32.4 us -> 12.3 us  [send(): return lax.ppermute(value, 'seq', moves(**shift))]
    ppermute x0 -> x9, starting transfers between devices: none -> 13.7 us  [turn(): return lax.ppermute(value, 'seq', pairs)]
    ppermute x1, starting transfers between devices: 3.55 us -> 9.04 us  [shards(): halo = lax.ppermute(halo, 'seq', [(s, s + 1) for s in range(1, 63, 2)])]
    ppermute x18 -> x9, waiting for transfers between devices: 5.33 us -> 2.23 us  [send(): return lax.ppermute(value, 'seq', moves(**shift))]
    pallas_call x1, Pallas kernels: 2.13 us -> 1.36 us  [join(): pl.pallas_call(join_kernel, out_shape=out_of(TOK, COLS), in_specs=[VMEM]...]
    pallas_call x3 -> x5, Pallas kernels: 2.55 us -> 3.14 us  [the longest x1 2.28 us: far(): pl.pallas_call(far_kernel, out_shape=[out_of(2 * FROWS, SENT)] * 4, in_sp...]
  transfers between devices with their start and end apart: 19 -> 19, of which waited for: 6 -> 6; matrix products, arithmetic and copies ran while one was open for 0% -> 0% of each run, Pallas kernels for 20% -> 23%
where the time goes in v4:
time: 55.9 us; the launch traced here: 55.5 us
  starting transfers between devices  35 us (63%)
  Pallas kernels  17.2 us (31%)
  waiting for transfers between devices  2.77 us (5%)
    ppermute x9, starting transfers between devices, turn(): return lax.ppermute(value, 'seq', pairs)  13.7 us
    ppermute x9, starting transfers between devices, send(): return lax.ppermute(value, 'seq', moves(**shift))  12.3 us
    ppermute x1, starting transfers between devices, shards(): halo = lax.ppermute(halo, 'seq', [(s, s + 1) for s in range(1, 63, 2)])  9.04 us
    pallas_call x1, Pallas kernels, local(): pl.pallas_call(local_kernel, out_shape=[out_of(TOK - W0, COLS), state, st...  3.82 us
    pallas_call x1, Pallas kernels, extract(): pl.pallas_call(extract_kernel, out_shape=[out_of(8, DH, dtype=jnp.int32),...  3.22 us
    pallas_call x1, Pallas kernels, far(): pl.pallas_call(far_kernel, out_shape=[out_of(2 * FROWS, SENT)] * 4, in_sp...  2.28 us
    ppermute x9, waiting for transfers between devices, send(): return lax.ppermute(value, 'seq', moves(**shift))  2.23 us
    pallas_call x1, Pallas kernels, near(): pl.pallas_call(near_kernel, out_shape=[out_of(NROWS, COLS, dtype=F32)] *...  1.84 us
  transfers between devices with their start and end apart: 19, of which 6 were waited for; matrix products, arithmetic and copies ran while one was open for 0% of the time, Pallas kernels for 23%

profile of v4, /device:TPU:1, one launch (start us, length us, event | category | flops | bytes accessed | tf_op | source)
XLA Modules:
  0.0 55.5 jit_solution(15093552262217076036)
XLA Ops:
  0.0 3.2 %extract.1 = (s32[8,128]{1,0:T(8,128)}, bf16[64,1024]{1,0:T(8,128)(2,1)}, bf16[192,1024]{1,0:T(8,128)(2,1)}, bf16[256,1024]{1,0:T(8,128)(2,1)}, bf16[256,1024]{1,0:T(8,128)(2,1)}) custom-call(s32[4]{0:T(128)} %off_hbm.1, bf16[1024,512]{1,0:T(8,128)(2,1)} %k.1, bf16[1024,512]{1,0:T(8,128)(2,1)} %v.1), custom_call_target="tpu_custom_call" | custom-call | bytes 1000 | tf_op jit(solution)/shard_map/extract/pallas_call | solution.py:151
  3.2 7.8 %collective-permute-start = (bf16[64,1024]{1,0:T(8,128)(2,1)}, bf16[64,1024]{1,0:T(8,128)(2,1)S(1)}, u32[]{:S(2)}, u32[]{:S(2)}) collective-permute-start(bf16[64,1024]{1,0:T(8,128)(2,1)} %get-tuple-element.49.kv_far), channel_id=1, source_target_pairs={{0,8},{4,12},{8,0},{12,4},{16,24},{20,28},{24,16},{28,20},{32,40},... | collective-permute-start | bytes 393224 | tf_op jit(solution)/shard_map/ppermute | solution.py:588
  11.1 1.0 %collective-permute-start.1 = (bf16[256,1024]{1,0:T(8,128)(2,1)}, bf16[256,1024]{1,0:T(8,128)(2,1)S(1)}, u32[]{:S(2)}, u32[]{:S(2)}) collective-permute-start(bf16[256,1024]{1,0:T(8,128)(2,1)} %get-tuple-element.68), channel_id=1, source_target_pairs={{0,4},{4,0},{8,12},{12,8},{16,20},{20,16},{24,28},{28,24},{32,36},... | collective-permute-start | bytes 1572872 | tf_op jit(solution)/shard_map/ppermute | solution.py:588
  12.1 1.0 %queries.1 = (bf16[1024,512]{1,0:T(8,128)(2,1)S(1)}, bf16[256,512]{1,0:T(8,128)(2,1)S(1)}, bf16[64,256]{1,0:T(8,128)(2,1)S(1)}, bf16[64,256]{1,0:T(8,128)(2,1)S(1)}, bf16[1024,256]{1,0:T(8,128)(2,1)S(1)}) custom-call(s32[8,128]{1,0:T(8,128)S(1)} %copy-done.5, bf16[1024,512]{1,0:T(8,128)(2,1)S(1)} %copy-done.4), custom_call_target="tpu_custom_call" | custom-call | flops 12000000000 | bytes 1000 | tf_op jit(solution)/shard_map/queries/pallas_call | solution.py:212
  13.1 0.7 %collective-permute-done.1.halo_c = bf16[256,1024]{1,0:T(8,128)(2,1)S(1)} collective-permute-done((bf16[256,1024]{1,0:T(8,128)(2,1)}, bf16[256,1024]{1,0:T(8,128)(2,1)S(1)}, u32[]{:S(2)}, u32[]{:S(2)}) %collective-permute-start.1) | collective-permute-done | bytes 524320 | tf_op jit(solution)/shard_map/ppermute | solution.py:588
  15.0 2.8 %collective-permute-start.3 = (bf16[128,256]{1,0:T(8,128)(2,1)S(1)}, bf16[128,256]{1,0:T(8,128)(2,1)S(1)}, u32[]{:S(2)}, u32[]{:S(2)}) collective-permute-start(bf16[128,256]{1,0:T(8,128)(2,1)S(1)} %half.1.refs_0_), channel_id=1, source_target_pairs={{0,32},{4,132},{8,40},{12,140},{16,48},{20,148},{24,56},{28,156},{... | collective-permute-start | bytes 196616 | tf_op jit(solution)/shard_map/ppermute | solution.py:599
  18.2 2.4 %collective-permute-start.5 = (bf16[128,256]{1,0:T(8,128)(2,1)S(1)}, bf16[128,256]{1,0:T(8,128)(2,1)S(1)}, u32[]{:S(2)}, u32[]{:S(2)}) collective-permute-start(bf16[128,256]{1,0:T(8,128)(2,1)S(1)} %half.1.refs_0_), channel_id=1, source_target_pairs={{0,48},{4,196},{8,56},{12,204},{16,0},{20,212},{24,8},{28,220},{32... | collective-permute-start | bytes 196616 | tf_op jit(solution)/shard_map/ppermute | solution.py:599
  20.5 3.8 %local.1 = (bf16[768,512]{1,0:T(8,128)(2,1)S(1)}, f32[448,512]{1,0:T(8,128)S(1)}, f32[448,512]{1,0:T(8,128)S(1)}, f32[448,512]{1,0:T(8,128)S(1)}) custom-call(bf16[1024,256]{1,0:T(8,128)(2,1)S(1)} %get-tuple-element.51.res, bf16[1024,512]{1,0:T(8,128)(2,1)S(1)} %get-tuple-element.52.q, bf16[1024,512]{1,0:T(8,128)(2,1)S(1)} %copy-done, ...), custom_call_target="tpu_custom_call" | custom-call | flops 1000000000 | bytes 1000 | tf_op jit(solution)/shard_map/local/pallas_call | solution.py:337
  24.4 1.4 %collective-permute-start.7 = (bf16[64,512]{1,0:T(8,128)(2,1)S(1)}, bf16[64,512]{1,0:T(8,128)(2,1)S(1)}, u32[]{:S(2)}, u32[]{:S(2)}) collective-permute-start(bf16[64,512]{1,0:T(8,128)(2,1)S(1)} %get-tuple-element.67), channel_id=1, source_target_pairs={{0,4},{4,0},{8,12},{12,8},{16,20},{20,16},{24,28},{28,24},{32,36},... | collective-permute-start | bytes 196616 | tf_op jit(solution)/shard_map/ppermute | solution.py:588
  25.9 0.9 %collective-permute-done.7.given = bf16[64,512]{1,0:T(8,128)(2,1)S(1)} collective-permute-done((bf16[64,512]{1,0:T(8,128)(2,1)S(1)}, bf16[64,512]{1,0:T(8,128)(2,1)S(1)}, u32[]{:S(2)}, u32[]{:S(2)}) %collective-permute-start.7) | collective-permute-done | bytes 65568 | tf_op jit(solution)/shard_map/ppermute | solution.py:588
  26.8 2.0 %collective-permute-start.10 = (bf16[256,512]{1,0:T(8,128)(2,1)S(1)}, bf16[256,512]{1,0:T(8,128)(2,1)S(1)}, u32[]{:S(2)}, u32[]{:S(2)}) collective-permute-start(bf16[256,512]{1,0:T(8,128)(2,1)S(1)} %keys.1.refs_4_), channel_id=1, source_target_pairs={{0,128},{4,36},{8,136},{12,44},{16,144},{20,52},{24,152},{28,60},{... | collective-permute-start | bytes 786440 | tf_op jit(solution)/shard_map/ppermute | solution.py:599
  28.8 0.4 collective-permute-start.11
  29.2 2.3 %collective-permute-start.12 = (bf16[256,512]{1,0:T(8,128)(2,1)S(1)}, bf16[256,512]{1,0:T(8,128)(2,1)S(1)}, u32[]{:S(2)}, u32[]{:S(2)}) collective-permute-start(bf16[256,512]{1,0:T(8,128)(2,1)S(1)} %keys.1.refs_4_), channel_id=1, source_target_pairs={{0,192},{4,52},{8,200},{12,60},{16,208},{20,4},{24,216},{28,12},{3... | collective-permute-start | bytes 786440 | tf_op jit(solution)/shard_map/ppermute | solution.py:599
  31.5 9.0 %collective-permute-start.8 = (bf16[256,1024]{1,0:T(8,128)(2,1)S(1)}, bf16[256,1024]{1,0:T(8,128)(2,1)S(1)}, u32[]{:S(2)}, u32[]{:S(2)}) collective-permute-start(bf16[256,1024]{1,0:T(8,128)(2,1)S(1)} %copy-done.6), channel_id=1, source_target_pairs={{4,8},{12,16},{20,24},{28,32},{36,40},{44,48},{52,56},{60,64},{68,... | collective-permute-start | bytes 1572872 | tf_op jit(solution)/shard_map/ppermute | solution.py:621
  40.7 2.3 %far.1 = (bf16[128,384]{1,0:T(8,128)(2,1)S(1)}, bf16[128,384]{1,0:T(8,128)(2,1)S(1)}, bf16[128,384]{1,0:T(8,128)(2,1)S(1)}, bf16[128,384]{1,0:T(8,128)(2,1)S(1)}) custom-call(bf16[128,256]{1,0:T(8,128)(2,1)S(1)} %half.1.refs_0_, bf16[128,256]{1,0:T(8,128)(2,1)S(1)} %collective-permute-done.3.refs_1_, bf16[128,256]{1,0:T(8,128)(2,1)S(1)} %collective-permute-done.4.refs_2_, ...), custom_call_target="tpu_custom_call" | custom-call | bytes 1000 | tf_op jit(solution)/shard_map/far/pallas_call | solution.py:474
  43.0 2.1 %collective-permute-start.15 = (bf16[128,384]{1,0:T(8,128)(2,1)S(1)}, bf16[128,384]{1,0:T(8,128)(2,1)S(1)}, u32[]{:S(2)}, u32[]{:S(2)}) collective-permute-start(bf16[128,384]{1,0:T(8,128)(2,1)S(1)} %get-tuple-element.83), channel_id=1, source_target_pairs={{0,32},{4,132},{8,40},{12,140},{16,48},{20,148},{24,56},{28,156},{... | collective-permute-start | bytes 294920 | tf_op jit(solution)/shard_map/ppermute | solution.py:599
  45.2 1.4 %collective-permute-start.17 = (bf16[128,384]{1,0:T(8,128)(2,1)S(1)}, bf16[128,384]{1,0:T(8,128)(2,1)S(1)}, u32[]{:S(2)}, u32[]{:S(2)}) collective-permute-start(bf16[128,384]{1,0:T(8,128)(2,1)S(1)} %get-tuple-element.85), channel_id=1, source_target_pairs={{0,16},{4,68},{8,24},{12,76},{16,32},{20,84},{24,40},{28,92},{32,4... | collective-permute-start | bytes 294920 | tf_op jit(solution)/shard_map/ppermute | solution.py:599
  46.7 1.8 %near.1 = (f32[256,512]{1,0:T(8,128)S(1)}, f32[256,512]{1,0:T(8,128)S(1)}, f32[256,512]{1,0:T(8,128)S(1)}) custom-call(bf16[256,512]{1,0:T(8,128)(2,1)S(1)} %get-tuple-element.72.q, f32[448,512]{1,0:T(8,128)S(1)} %get-tuple-element.59.km, f32[448,512]{1,0:T(8,128)S(1)} %get-tuple-element.60.kl, f32[448,512]{1,0:T(8,128)S(1)} %get-tuple-element.61.ka, ...), custom_call_target="tpu_custom_call" | custom-call | bytes 1000 | tf_op jit(solution)/shard_map/near/pallas_call | solution.py:401
  48.6 1.4 %across.1 = (f32[256,512]{1,0:T(8,128)S(1)}, f32[256,512]{1,0:T(8,128)S(1)}, f32[256,512]{1,0:T(8,128)S(1)}) custom-call(bf16[256,512]{1,0:T(8,128)(2,1)S(1)} %get-tuple-element.72.q, f32[256,512]{1,0:T(8,128)S(1)} %get-tuple-element.73.nm, f32[256,512]{1,0:T(8,128)S(1)} %get-tuple-element.74.nl, f32[256,512]{1,0:T(8,128)S(1)} %get-tuple-element.75.na, ...), custom_call_target="tpu_custom_call" | custom-call | bytes 1000 | tf_op jit(solution)/shard_map/across/pallas_call | solution.py:436
  50.2 0.8 %fold.1.mine = f32[128,512]{1,0:T(8,128)S(1)} custom-call(bf16[128,384]{1,0:T(8,128)(2,1)S(1)} %get-tuple-element.82.f0, bf16[128,384]{1,0:T(8,128)(2,1)S(1)} %collective-permute-done.15.f1, bf16[128,384]{1,0:T(8,128)(2,1)S(1)} %collective-permute-done.16.f2, bf16[128,384]{1,0:T(8,128)(2,1)S(1)} %collective-permute-done.17.f3), custom_call_target="tpu_custom_call" | custom-call | bytes 1000 | tf_op jit(solution)/shard_map/fold/pallas_call | solution.py:500
  51.0 0.4 collective-permute-done.8.halo
  51.4 1.2 %collective-permute-start.18 = (f32[128,512]{1,0:T(8,128)S(1)}, f32[128,512]{1,0:T(8,128)S(1)}, u32[]{:S(2)}, u32[]{:S(2)}) collective-permute-start(f32[128,512]{1,0:T(8,128)S(1)} %fold.1.mine), channel_id=1, source_target_pairs={{0,4},{4,0},{8,12},{12,8},{16,20},{20,16},{24,28},{28,24},{32,36},... | collective-permute-start | bytes 786440 | tf_op jit(solution)/shard_map/ppermute | solution.py:588
  52.5 1.4 %halo.1 = (bf16[256,512]{1,0:T(8,128)(2,1)S(1)}, f32[64,512]{1,0:T(8,128)S(1)}, f32[64,512]{1,0:T(8,128)S(1)}, f32[64,512]{1,0:T(8,128)S(1)}) custom-call(bf16[1024,256]{1,0:T(8,128)(2,1)S(1)} %get-tuple-element.51.res, bf16[1024,512]{1,0:T(8,128)(2,1)S(1)} %get-tuple-element.52.q, f32[448,512]{1,0:T(8,128)S(1)} %get-tuple-element.59.km, ...), custom_call_target="tpu_custom_call" | custom-call | bytes 1000 | tf_op jit(solution)/shard_map/halo/pallas_call | solution.py:375
  54.0 1.4 %join.1 = bf16[1024,512]{1,0:T(8,128)(2,1)} custom-call(bf16[64,1024]{1,0:T(8,128)(2,1)S(1)} %collective-permute-done.far_z, bf16[1024,256]{1,0:T(8,128)(2,1)S(1)} %get-tuple-element.51.res, f32[64,512]{1,0:T(8,128)S(1)} %get-tuple-element.69.hm, f32[64,512]{1,0:T(8,128)S(1)} %get-tuple-element.70.hl, f32[64,512]{1,0:T(8,128)S(1)} %get-tuple-element.71.ha, ...), custom_call_target="tpu_custom_call" | custom-call | bytes 1000 | tf_op jit(solution)/shard_map/join/pallas_call | solution.py:561
  (42 shorter events, 2.2 us)
Async XLA Ops:
  0.0 12.0 %copy-start.4 = (bf16[1024,512]{1,0:T(8,128)(2,1)S(1)}, bf16[1024,512]{1,0:T(8,128)(2,1)}, u32[]{:S(2)}) copy-start(bf16[1024,512]{1,0:T(8,128)(2,1)} %q_hbm.1) | copy-start | bytes 3145732
  3.2 8.8 %copy-start.5 = (s32[8,128]{1,0:T(8,128)S(1)}, s32[8,128]{1,0:T(8,128)}, u32[]{:S(2)}) copy-start(s32[8,128]{1,0:T(8,128)} %get-tuple-element.50.offs) | copy-start | bytes 12292
  3.2 21.1 %collective-permute-start = (bf16[64,1024]{1,0:T(8,128)(2,1)}, bf16[64,1024]{1,0:T(8,128)(2,1)S(1)}, u32[]{:S(2)}, u32[]{:S(2)}) collective-permute-start(bf16[64,1024]{1,0:T(8,128)(2,1)} %get-tuple-element.49.kv_far), channel_id=1, source_target_pairs={{0,8},{4,12},{8,0},{12,4},{16,24},{20,28},{24,16},{28,20},{32,40},... | collective-permute-start | bytes 393224 | tf_op jit(solution)/shard_map/ppermute | solution.py:588
  11.1 2.7 %collective-permute-start.1 = (bf16[256,1024]{1,0:T(8,128)(2,1)}, bf16[256,1024]{1,0:T(8,128)(2,1)S(1)}, u32[]{:S(2)}, u32[]{:S(2)}) collective-permute-start(bf16[256,1024]{1,0:T(8,128)(2,1)} %get-tuple-element.68), channel_id=1, source_target_pairs={{0,4},{4,0},{8,12},{12,8},{16,20},{20,16},{24,28},{28,24},{32,36},... | collective-permute-start | bytes 1572872 | tf_op jit(solution)/shard_map/ppermute | solution.py:588
  12.0 2.5 %collective-permute-start.6 = (bf16[256,1024]{1,0:T(8,128)(2,1)}, bf16[256,1024]{1,0:T(8,128)(2,1)S(1)}, u32[]{:S(2)}, u32[]{:S(2)}) collective-permute-start(bf16[256,1024]{1,0:T(8,128)(2,1)} %get-tuple-element.64.near), channel_id=1, source_target_pairs={{0,4},{4,0},{8,12},{12,8},{16,20},{20,16},{24,28},{28,24},{32,36},... | collective-permute-start | bytes 1572872 | tf_op jit(solution)/shard_map/ppermute | solution.py:588
  12.0 8.5 %copy-start = (bf16[1024,512]{1,0:T(8,128)(2,1)S(1)}, bf16[1024,512]{1,0:T(8,128)(2,1)}, u32[]{:S(2)}) copy-start(bf16[1024,512]{1,0:T(8,128)(2,1)} %k.1) | copy-start | bytes 3145732
  12.1 8.5 %copy-start.1 = (bf16[1024,512]{1,0:T(8,128)(2,1)S(1)}, bf16[1024,512]{1,0:T(8,128)(2,1)}, u32[]{:S(2)}) copy-start(bf16[1024,512]{1,0:T(8,128)(2,1)} %v.1) | copy-start | bytes 3145732
  13.8 1.2 %collective-permute-start.2 = (bf16[64,256]{1,0:T(8,128)(2,1)S(1)}, bf16[64,256]{1,0:T(8,128)(2,1)S(1)}, u32[]{:S(2)}, u32[]{:S(2)}) collective-permute-start(bf16[64,256]{1,0:T(8,128)(2,1)S(1)} %get-tuple-element.57), channel_id=1, source_target_pairs={{0,4},{4,0},{8,12},{12,8},{16,20},{20,16},{24,28},{28,24},{32,36},... | collective-permute-start | bytes 98312 | tf_op jit(solution)/shard_map/ppermute | solution.py:588
  14.5 26.0 %collective-permute-start.9 = (bf16[192,1024]{1,0:T(8,128)(2,1)S(1)}, bf16[192,1024]{1,0:T(8,128)(2,1)S(1)}, u32[]{:S(2)}, u32[]{:S(2)}) collective-permute-start(bf16[192,1024]{1,0:T(8,128)(2,1)S(1)} %copy-done.7), channel_id=1, source_target_pairs={{0,8},{4,12},{8,0},{12,4},{16,24},{20,28},{24,16},{28,20},{32,40},... | collective-permute-start | bytes 1179656 | tf_op jit(solution)/shard_map/ppermute | solution.py:588
  15.0 9.4 %collective-permute-start.3 = (bf16[128,256]{1,0:T(8,128)(2,1)S(1)}, bf16[128,256]{1,0:T(8,128)(2,1)S(1)}, u32[]{:S(2)}, u32[]{:S(2)}) collective-permute-start(bf16[128,256]{1,0:T(8,128)(2,1)S(1)} %half.1.refs_0_), channel_id=1, source_target_pairs={{0,32},{4,132},{8,40},{12,140},{16,48},{20,148},{24,56},{28,156},{... | collective-permute-start | bytes 196616 | tf_op jit(solution)/shard_map/ppermute | solution.py:599
  17.8 6.5 %collective-permute-start.4 = (bf16[128,256]{1,0:T(8,128)(2,1)S(1)}, bf16[128,256]{1,0:T(8,128)(2,1)S(1)}, u32[]{:S(2)}, u32[]{:S(2)}) collective-permute-start(bf16[128,256]{1,0:T(8,128)(2,1)S(1)} %half.1.refs_0_), channel_id=1, source_target_pairs={{0,16},{4,68},{8,24},{12,76},{16,32},{20,84},{24,40},{28,92},{32,4... | collective-permute-start | bytes 196616 | tf_op jit(solution)/shard_map/ppermute | solution.py:599
  18.2 6.2 %collective-permute-start.5 = (bf16[128,256]{1,0:T(8,128)(2,1)S(1)}, bf16[128,256]{1,0:T(8,128)(2,1)S(1)}, u32[]{:S(2)}, u32[]{:S(2)}) collective-permute-start(bf16[128,256]{1,0:T(8,128)(2,1)S(1)} %half.1.refs_0_), channel_id=1, source_target_pairs={{0,48},{4,196},{8,56},{12,204},{16,0},{20,212},{24,8},{28,220},{32... | collective-permute-start | bytes 196616 | tf_op jit(solution)/shard_map/ppermute | solution.py:599
  24.4 2.3 %collective-permute-start.7 = (bf16[64,512]{1,0:T(8,128)(2,1)S(1)}, bf16[64,512]{1,0:T(8,128)(2,1)S(1)}, u32[]{:S(2)}, u32[]{:S(2)}) collective-permute-start(bf16[64,512]{1,0:T(8,128)(2,1)S(1)} %get-tuple-element.67), channel_id=1, source_target_pairs={{0,4},{4,0},{8,12},{12,8},{16,20},{20,16},{24,28},{28,24},{32,36},... | collective-permute-start | bytes 196616 | tf_op jit(solution)/shard_map/ppermute | solution.py:588
  26.8 19.9 %copy-start.2 = (bf16[256,1024]{1,0:T(8,128)(2,1)S(1)}, bf16[256,1024]{1,0:T(8,128)(2,1)}, u32[]{:S(2)}) copy-start(bf16[256,1024]{1,0:T(8,128)(2,1)} %get-tuple-element.64.near) | copy-start | bytes 1572868
  26.8 13.7 %collective-permute-start.10 = (bf16[256,512]{1,0:T(8,128)(2,1)S(1)}, bf16[256,512]{1,0:T(8,128)(2,1)S(1)}, u32[]{:S(2)}, u32[]{:S(2)}) collective-permute-start(bf16[256,512]{1,0:T(8,128)(2,1)S(1)} %keys.1.refs_4_), channel_id=1, source_target_pairs={{0,128},{4,36},{8,136},{12,44},{16,144},{20,52},{24,152},{28,60},{... | collective-permute-start | bytes 786440 | tf_op jit(solution)/shard_map/ppermute | solution.py:599
  28.8 11.8 %collective-permute-start.11 = (bf16[256,512]{1,0:T(8,128)(2,1)S(1)}, bf16[256,512]{1,0:T(8,128)(2,1)S(1)}, u32[]{:S(2)}, u32[]{:S(2)}) collective-permute-start(bf16[256,512]{1,0:T(8,128)(2,1)S(1)} %keys.1.refs_4_), channel_id=1, source_target_pairs={{0,64},{4,20},{8,72},{12,28},{16,80},{20,36},{24,88},{28,44},{32,9... | collective-permute-start | bytes 786440 | tf_op jit(solution)/shard_map/ppermute | solution.py:599
  29.2 11.4 %collective-permute-start.12 = (bf16[256,512]{1,0:T(8,128)(2,1)S(1)}, bf16[256,512]{1,0:T(8,128)(2,1)S(1)}, u32[]{:S(2)}, u32[]{:S(2)}) collective-permute-start(bf16[256,512]{1,0:T(8,128)(2,1)S(1)} %keys.1.refs_4_), channel_id=1, source_target_pairs={{0,192},{4,52},{8,200},{12,60},{16,208},{20,4},{24,216},{28,12},{3... | collective-permute-start | bytes 786440 | tf_op jit(solution)/shard_map/ppermute | solution.py:599
  31.5 19.8 %collective-permute-start.8 = (bf16[256,1024]{1,0:T(8,128)(2,1)S(1)}, bf16[256,1024]{1,0:T(8,128)(2,1)S(1)}, u32[]{:S(2)}, u32[]{:S(2)}) collective-permute-start(bf16[256,1024]{1,0:T(8,128)(2,1)S(1)} %copy-done.6), channel_id=1, source_target_pairs={{4,8},{12,16},{20,24},{28,32},{36,40},{44,48},{52,56},{60,64},{68,... | collective-permute-start | bytes 1572872 | tf_op jit(solution)/shard_map/ppermute | solution.py:621
  40.6 2.4 %collective-permute-start.13 = (bf16[192,1024]{1,0:T(8,128)(2,1)S(1)}, bf16[192,1024]{1,0:T(8,128)(2,1)S(1)}, u32[]{:S(2)}, u32[]{:S(2)}) collective-permute-start(bf16[192,1024]{1,0:T(8,128)(2,1)S(1)} %collective-permute-done.9.rest_z), channel_id=1, source_target_pairs={{0,4},{4,0},{8,12},{12,8},{16,20},{20,16},{24,28},{28,24},{32,36},... | collective-permute-start | bytes 1179656 | tf_op jit(solution)/shard_map/ppermute | solution.py:588
  43.0 7.0 %collective-permute-start.15 = (bf16[128,384]{1,0:T(8,128)(2,1)S(1)}, bf16[128,384]{1,0:T(8,128)(2,1)S(1)}, u32[]{:S(2)}, u32[]{:S(2)}) collective-permute-start(bf16[128,384]{1,0:T(8,128)(2,1)S(1)} %get-tuple-element.83), channel_id=1, source_target_pairs={{0,32},{4,132},{8,40},{12,140},{16,48},{20,148},{24,56},{28,156},{... | collective-permute-start | bytes 294920 | tf_op jit(solution)/shard_map/ppermute | solution.py:599
  45.1 4.9 %collective-permute-start.16 = (bf16[128,384]{1,0:T(8,128)(2,1)S(1)}, bf16[128,384]{1,0:T(8,128)(2,1)S(1)}, u32[]{:S(2)}, u32[]{:S(2)}) collective-permute-start(bf16[128,384]{1,0:T(8,128)(2,1)S(1)} %get-tuple-element.84), channel_id=1, source_target_pairs={{0,48},{4,196},{8,56},{12,204},{16,0},{20,212},{24,8},{28,220},{32... | collective-permute-start | bytes 294920 | tf_op jit(solution)/shard_map/ppermute | solution.py:599
  45.2 5.0 %collective-permute-start.17 = (bf16[128,384]{1,0:T(8,128)(2,1)S(1)}, bf16[128,384]{1,0:T(8,128)(2,1)S(1)}, u32[]{:S(2)}, u32[]{:S(2)}) collective-permute-start(bf16[128,384]{1,0:T(8,128)(2,1)S(1)} %get-tuple-element.85), channel_id=1, source_target_pairs={{0,16},{4,68},{8,24},{12,76},{16,32},{20,84},{24,40},{28,92},{32,4... | collective-permute-start | bytes 294920 | tf_op jit(solution)/shard_map/ppermute | solution.py:599
  46.5 2.0 %collective-permute-start.14 = (bf16[64,512]{1,0:T(8,128)(2,1)S(1)}, bf16[64,512]{1,0:T(8,128)(2,1)S(1)}, u32[]{:S(2)}, u32[]{:S(2)}) collective-permute-start(bf16[64,512]{1,0:T(8,128)(2,1)S(1)} %get-tuple-element.86.keep), channel_id=1, source_target_pairs={{0,4},{4,0},{8,12},{12,8},{16,20},{20,16},{24,28},{28,24},{32,36},... | collective-permute-start | bytes 196616 | tf_op jit(solution)/shard_map/ppermute | solution.py:588
  51.4 2.6 %collective-permute-start.18 = (f32[128,512]{1,0:T(8,128)S(1)}, f32[128,512]{1,0:T(8,128)S(1)}, u32[]{:S(2)}, u32[]{:S(2)}) collective-permute-start(f32[128,512]{1,0:T(8,128)S(1)} %fold.1.mine), channel_id=1, source_target_pairs={{0,4},{4,0},{8,12},{12,8},{16,20},{20,16},{24,28},{28,24},{32,36},... | collective-permute-start | bytes 786440 | tf_op jit(solution)/shard_map/ppermute | solution.py:588
  (3 other events, 9.6 us)

commit v5 on v4

--- a/solution.py
+++ b/solution.py
@@ -74,8 +74,15 @@
     return jnp.broadcast_to(column, (column.shape[0], DH))
 
 
-def attend(q, k, v):
-    s = dot_nt(q, k) * SCALE2
+def staged(first, second):
+    ready = first(0)
+    for h in range(HEADS):
+        later = first(h + 1) if h + 1 < HEADS else None
+        second(h, ready)
+        ready = later
+
+
+def weigh(s, v):
     m = jnp.max(s, axis=1, keepdims=True)
     p = jnp.exp2(s - m)
     l = jnp.sum(p, axis=1, keepdims=True)
@@ -292,7 +299,7 @@
 
 
 def local_kernel(res, q, k, v, done, km, kl, ka):
-    for h in range(HEADS):
+    def first(h):
         c = head_cols(h)
         qs = [q[block_rows(b), c] for b in range(BLOCKS)]
         scores = [[] for _ in range(BLOCKS)]
@@ -301,6 +308,10 @@
             s = dot_nt(jnp.concatenate(users, 0), k[block_rows(j), c]) * SCALE2
             for i in range(len(users)):
                 scores[j + i].append(s[i * W0 : (i + 1) * W0])
+        return scores
+
+    def second(h, scores):
+        c = head_cols(h)
         ms, ls, ps = [], [], []
         for b in range(BLOCKS):
             m = functools.reduce(
@@ -331,6 +342,8 @@
         done[W0 : 2 * W0, c] = pair[:, DH:]
         done[2 * W0 :, c] = dot(restore, rest[2]).astype(BF16)
 
+    staged(first, second)
+
 
 def local(*args):
     state = out_of(KEPT, COLS, dtype=F32)
@@ -354,12 +367,16 @@
     position = lax.axis_index("seq")
     from_core = (position & 1) == 1
     has_halo = position > 0
-    for h in range(HEADS):
+
+    def first(h):
+        c = head_cols(h)
+        hk = jnp.where(from_core, halo_c[:, c], halo[:, c])
+        return jnp.where(has_halo, dot_nt(q[:W0, c], hk) * SCALE2, -jnp.inf)
+
+    def second(h, s):
         c, d = head_cols(h), value_cols(h)
-        hk = jnp.where(from_core, halo_c[:, c], halo[:, c])
         hv = jnp.where(from_core, halo_c[:, d], halo[:, d])
         m = km[:W0, c]
-        s = jnp.where(has_halo, dot_nt(q[:W0, c], hk) * SCALE2, -jnp.inf)
         m_new = jnp.maximum(m, wide(jnp.max(s, axis=1, keepdims=True)))
         p = jnp.exp2(s - jnp.concatenate([m_new, m_new], 1))
         scale = jnp.exp2(m - m_new)
@@ -369,6 +386,8 @@
         rest = (acc[:OTHER] * (1.0 / l[:OTHER])).astype(BF16)
         done[:, c] = dot(res[block_rows(h), :OTHER], rest).astype(BF16)
 
+    staged(first, second)
+
 
 def halo_fold(*args):
     state = out_of(NEAR, COLS, dtype=F32)
@@ -384,17 +403,21 @@
 
 
 def near_kernel(q, km, kl, ka, near, near_c, far_z, m, l, acc):
-    for h in range(HEADS):
-        c, d = head_cols(h), value_cols(h)
-        k, v = (
-            jnp.concatenate([near[:, cols], near_c[:, cols], far_z[:, cols]], 0)
-            for cols in (c, d)
-        )
-        state = attend(q[:, c], k, v)
+    def keys(cols):
+        return jnp.concatenate([near[:, cols], near_c[:, cols], far_z[:, cols]], 0)
+
+    def first(h):
+        return dot_nt(q[:, head_cols(h)], keys(head_cols(h))) * SCALE2
+
+    def second(h, s):
+        c = head_cols(h)
+        state = weigh(s, keys(value_cols(h)))
         later = merge([(km[W0:, c], kl[W0:, c], ka[W0:, c]), tuple(x[NEAR:] for x in state)])
-        for ref, first, rest in zip((m, l, acc), state, later):
-            ref[:NEAR, c] = first[:NEAR]
+        for ref, start, rest in zip((m, l, acc), state, later):
+            ref[:NEAR, c] = start[:NEAR]
             ref[NEAR:, c] = rest
+
+    staged(first, second)
 
 
 def near(*args):
@@ -411,25 +434,23 @@
 
 def across_kernel(q, nm, nl, na, given, other, rest_z, rest_zc, m, l, acc):
     core = lax.axis_index("seq") & 1
-    for h in range(HEADS):
-        c, d = head_cols(h), value_cols(h)
-        k, v = (
-            jnp.concatenate(
-                [
-                    jnp.where(core == h // 2, given[:, half], other[:, half]),
-                    rest_z[:, cols],
-                    rest_zc[:, cols],
-                ],
-                0,
-            )
-            for cols, half in (
-                (c, head_cols(h % 2)),
-                (d, slice(HALF + h % 2 * DH, HALF + (h % 2 + 1) * DH)),
-            )
+
+    def keys(h, start):
+        half = slice(start // 2 + h % 2 * DH, start // 2 + (h % 2 + 1) * DH)
+        cols = slice(start + h * DH, start + (h + 1) * DH)
+        far = jnp.where(core == h // 2, given[:, half], other[:, half])
+        return jnp.concatenate([far, rest_z[:, cols], rest_zc[:, cols]], 0)
+
+    def first(h):
+        return dot_nt(q[:, head_cols(h)], keys(h, 0)) * SCALE2
+
+    def second(h, s):
+        c = head_cols(h)
+        m[:, c], l[:, c], acc[:, c] = merge(
+            [(nm[:, c], nl[:, c], na[:, c]), weigh(s, keys(h, COLS))]
         )
-        m[:, c], l[:, c], acc[:, c] = merge(
-            [(nm[:, c], nl[:, c], na[:, c]), attend(q[:, c], k, v)]
-        )
+
+    staged(first, second)
 
 
 def across(*args):
@@ -447,27 +468,33 @@
 def far_kernel(*refs):
     q, kv, out = refs[:4], refs[4:8], refs[8:]
     n = 2 * FROWS
-    for part in out:
-        part[:, HALF:] = jnp.zeros((n, DH), BF16)
-    for g in range(HEADS // 2):
+    lane = lax.broadcasted_iota(jnp.int32, (4 * n, DH), 1)
+    heads = range(HEADS // 2)
+    scores = []
+    for g in heads:
+        c = head_cols(g)
+        qh = jnp.concatenate([x[:, c] for x in q], 0)
+        k = jnp.concatenate([x[:, c] for x in kv], 0)
+        scores.append(dot_nt(qh, k) * SCALE2)
+    tail = jnp.zeros((4 * n, DH), F32)
+    for g in heads:
         c = head_cols(g)
         d = slice(HALF + g * DH, HALF + (g + 1) * DH)
-        qh = jnp.concatenate([x[:, c] for x in q], 0)
-        k = jnp.concatenate([x[:, c] for x in kv], 0)
         v = jnp.concatenate([x[:, d] for x in kv], 0)
-        m, l, o = attend(qh, k, v)
-        o = (o * (1.0 / l)).astype(BF16)
-        lse = (m + jnp.log2(l))[:, :1]
-        first = lse.astype(BF16)
-        left = lse - first.astype(F32)
-        second = left.astype(BF16)
-        third = (left - second.astype(F32)).astype(BF16)
+        m = jnp.max(scores[g], axis=1, keepdims=True)
+        p = jnp.exp2(scores[g] - m)
+        l = wide(jnp.sum(p, axis=1, keepdims=True))
+        o = (dot(p.astype(BF16), v) * (1.0 / l)).astype(BF16)
+        left = wide(m) + jnp.log2(l)
+        for e in range(3):
+            piece = left.astype(BF16).astype(F32)
+            tail = jnp.where(lane == 2 * e + g, piece, tail)
+            left = left - piece
         for i, part in enumerate(out):
-            rows = slice(i * n, (i + 1) * n)
-            part[:, c] = o[rows]
-            for e, piece in enumerate((first, second, third)):
-                col = HALF + 2 * e + g
-                part[:, col : col + 1] = piece[rows]
+            part[:, c] = o[i * n : (i + 1) * n]
+    tail = tail.astype(BF16)
+    for i, part in enumerate(out):
+        part[:, HALF:] = tail[i * n : (i + 1) * n]
 
 
 def far(*args):
@@ -483,14 +510,17 @@
 
 
 def fold_kernel(f0, f1, f2, f3, out):
+    fars = (f0, f1, f2, f3)
+    n = 2 * FROWS
+    tails = jnp.concatenate([f[:, HALF:] for f in fars], 0)
+    row = lax.broadcasted_iota(jnp.int32, (DH, DH), 0)
     for g in range(HEADS // 2):
         c = head_cols(g)
-        states = []
-        for f in (f0, f1, f2, f3):
-            lse = sum(
-                f[:, HALF + 2 * e + g : HALF + 2 * e + g + 1].astype(F32) for e in range(3)
-            )
-            states.append((wide(lse), jnp.ones((2 * FROWS, DH), F32), f[:, c].astype(F32)))
+        gather = jnp.where((row < 6) & ((row & 1) == g), 1.0, 0.0).astype(BF16)
+        lse = dot(tails, gather)
+        states = [
+            (lse[i * n : (i + 1) * n], 1.0, f[:, c].astype(F32)) for i, f in enumerate(fars)
+        ]
         m, l, acc = merge(states)
         out[:, c] = acc * (1.0 / l)
         out[:, HALF + g * DH : HALF + (g + 1) * DH] = m + jnp.log2(l)

time: 55.9 us -> 55.2 us (0.987)
  Pallas kernels: 17.2 us -> 15 us
  waiting for transfers between devices: 2.77 us -> 3.87 us
    ppermute x9, waiting for transfers between devices: 0.15 us -> 1.64 us  [turn(): return lax.ppermute(value, 'seq', pairs)]
  transfers between devices with their start and end apart: 19 -> 19, of which waited for: 6 -> 5; matrix products, arithmetic and copies ran while one was open for 0% -> 0% of each run, Pallas kernels for 23% -> 19%
where the time goes in v5:
time: 55.2 us; the launch traced here: 54.5 us
  starting transfers between devices  35.1 us (64%)
  Pallas kernels  15 us (27%)
  waiting for transfers between devices  3.87 us (7%)
    ppermute x9, starting transfers between devices, turn(): return lax.ppermute(value, 'seq', pairs)  14.3 us
    ppermute x9, starting transfers between devices, send(): return lax.ppermute(value, 'seq', moves(**shift))  11.8 us
    ppermute x1, starting transfers between devices, shards(): halo = lax.ppermute(halo, 'seq', [(s, s + 1) for s in range(1, 63, 2)])  9.04 us
    pallas_call x1, Pallas kernels, local(): pl.pallas_call(local_kernel, out_shape=[out_of(TOK - W0, COLS), state, st...  3.33 us
    pallas_call x1, Pallas kernels, extract(): pl.pallas_call(extract_kernel, out_shape=[out_of(8, DH, dtype=jnp.int32),...  3.22 us
    ppermute x9, waiting for transfers between devices, send(): return lax.ppermute(value, 'seq', moves(**shift))  2.23 us
    pallas_call x1, Pallas kernels, far(): pl.pallas_call(far_kernel, out_shape=[out_of(2 * FROWS, SENT)] * 4, in_sp...  1.96 us
    ppermute x9, waiting for transfers between devices, turn(): return lax.ppermute(value, 'seq', pairs)  1.64 us
  transfers between devices with their start and end apart: 19, of which 5 were waited for; matrix products, arithmetic and copies ran while one was open for 0% of the time, Pallas kernels for 19%

profile of v5, /device:TPU:1, one launch (start us, length us, event | category | flops | bytes accessed | tf_op | source)
XLA Modules:
  0.0 54.5 jit_solution(413646624942125149)
XLA Ops:
  0.0 3.2 %extract.1 = (s32[8,128]{1,0:T(8,128)}, bf16[64,1024]{1,0:T(8,128)(2,1)}, bf16[192,1024]{1,0:T(8,128)(2,1)}, bf16[256,1024]{1,0:T(8,128)(2,1)}, bf16[256,1024]{1,0:T(8,128)(2,1)}) custom-call(s32[4]{0:T(128)} %off_hbm.1, bf16[1024,512]{1,0:T(8,128)(2,1)} %k.1, bf16[1024,512]{1,0:T(8,128)(2,1)} %v.1), custom_call_target="tpu_custom_call" | custom-call | bytes 1000 | tf_op jit(solution)/shard_map/extract/pallas_call | solution.py:158
  3.2 7.8 %collective-permute-start = (bf16[64,1024]{1,0:T(8,128)(2,1)}, bf16[64,1024]{1,0:T(8,128)(2,1)S(1)}, u32[]{:S(2)}, u32[]{:S(2)}) collective-permute-start(bf16[64,1024]{1,0:T(8,128)(2,1)} %get-tuple-element.49.kv_far), channel_id=1, source_target_pairs={{0,8},{4,12},{8,0},{12,4},{16,24},{20,28},{24,16},{28,20},{32,40},... | collective-permute-start | bytes 393224 | tf_op jit(solution)/shard_map/ppermute | solution.py:618
  11.1 1.0 %collective-permute-start.1 = (bf16[256,1024]{1,0:T(8,128)(2,1)}, bf16[256,1024]{1,0:T(8,128)(2,1)S(1)}, u32[]{:S(2)}, u32[]{:S(2)}) collective-permute-start(bf16[256,1024]{1,0:T(8,128)(2,1)} %get-tuple-element.68), channel_id=1, source_target_pairs={{0,4},{4,0},{8,12},{12,8},{16,20},{20,16},{24,28},{28,24},{32,36},... | collective-permute-start | bytes 1572872 | tf_op jit(solution)/shard_map/ppermute | solution.py:618
  12.1 1.0 %queries.1 = (bf16[1024,512]{1,0:T(8,128)(2,1)S(1)}, bf16[256,512]{1,0:T(8,128)(2,1)S(1)}, bf16[64,256]{1,0:T(8,128)(2,1)S(1)}, bf16[64,256]{1,0:T(8,128)(2,1)S(1)}, bf16[1024,256]{1,0:T(8,128)(2,1)S(1)}) custom-call(s32[8,128]{1,0:T(8,128)S(1)} %copy-done.5, bf16[1024,512]{1,0:T(8,128)(2,1)S(1)} %copy-done.4), custom_call_target="tpu_custom_call" | custom-call | flops 12000000000 | bytes 1000 | tf_op jit(solution)/shard_map/queries/pallas_call | solution.py:219
  13.1 0.7 %collective-permute-done.1.halo_c = bf16[256,1024]{1,0:T(8,128)(2,1)S(1)} collective-permute-done((bf16[256,1024]{1,0:T(8,128)(2,1)}, bf16[256,1024]{1,0:T(8,128)(2,1)S(1)}, u32[]{:S(2)}, u32[]{:S(2)}) %collective-permute-start.1) | collective-permute-done | bytes 524320 | tf_op jit(solution)/shard_map/ppermute | solution.py:618
  15.0 2.8 %collective-permute-start.3 = (bf16[128,256]{1,0:T(8,128)(2,1)S(1)}, bf16[128,256]{1,0:T(8,128)(2,1)S(1)}, u32[]{:S(2)}, u32[]{:S(2)}) collective-permute-start(bf16[128,256]{1,0:T(8,128)(2,1)S(1)} %half.1.refs_0_), channel_id=1, source_target_pairs={{0,32},{4,132},{8,40},{12,140},{16,48},{20,148},{24,56},{28,156},{... | collective-permute-start | bytes 196616 | tf_op jit(solution)/shard_map/ppermute | solution.py:629
  18.2 2.4 %collective-permute-start.5 = (bf16[128,256]{1,0:T(8,128)(2,1)S(1)}, bf16[128,256]{1,0:T(8,128)(2,1)S(1)}, u32[]{:S(2)}, u32[]{:S(2)}) collective-permute-start(bf16[128,256]{1,0:T(8,128)(2,1)S(1)} %half.1.refs_0_), channel_id=1, source_target_pairs={{0,48},{4,196},{8,56},{12,204},{16,0},{20,212},{24,8},{28,220},{32... | collective-permute-start | bytes 196616 | tf_op jit(solution)/shard_map/ppermute | solution.py:629
  20.5 3.3 %local.1 = (bf16[768,512]{1,0:T(8,128)(2,1)S(1)}, f32[448,512]{1,0:T(8,128)S(1)}, f32[448,512]{1,0:T(8,128)S(1)}, f32[448,512]{1,0:T(8,128)S(1)}) custom-call(bf16[1024,256]{1,0:T(8,128)(2,1)S(1)} %get-tuple-element.51.res, bf16[1024,512]{1,0:T(8,128)(2,1)S(1)} %get-tuple-element.52.q, bf16[1024,512]{1,0:T(8,128)(2,1)S(1)} %copy-done, ...), custom_call_target="tpu_custom_call" | custom-call | flops 1000000000 | bytes 1000 | tf_op jit(solution)/shard_map/local/pallas_call | solution.py:350
  24.0 1.4 %collective-permute-start.7 = (bf16[64,512]{1,0:T(8,128)(2,1)S(1)}, bf16[64,512]{1,0:T(8,128)(2,1)S(1)}, u32[]{:S(2)}, u32[]{:S(2)}) collective-permute-start(bf16[64,512]{1,0:T(8,128)(2,1)S(1)} %get-tuple-element.67), channel_id=1, source_target_pairs={{0,4},{4,0},{8,12},{12,8},{16,20},{20,16},{24,28},{28,24},{32,36},... | collective-permute-start | bytes 196616 | tf_op jit(solution)/shard_map/ppermute | solution.py:618
  25.4 0.9 %collective-permute-done.7.given = bf16[64,512]{1,0:T(8,128)(2,1)S(1)} collective-permute-done((bf16[64,512]{1,0:T(8,128)(2,1)S(1)}, bf16[64,512]{1,0:T(8,128)(2,1)S(1)}, u32[]{:S(2)}, u32[]{:S(2)}) %collective-permute-start.7) | collective-permute-done | bytes 65568 | tf_op jit(solution)/shard_map/ppermute | solution.py:618
  26.3 2.0 %collective-permute-start.10 = (bf16[256,512]{1,0:T(8,128)(2,1)S(1)}, bf16[256,512]{1,0:T(8,128)(2,1)S(1)}, u32[]{:S(2)}, u32[]{:S(2)}) collective-permute-start(bf16[256,512]{1,0:T(8,128)(2,1)S(1)} %keys.1.refs_4_), channel_id=1, source_target_pairs={{0,128},{4,36},{8,136},{12,44},{16,144},{20,52},{24,152},{28,60},{... | collective-permute-start | bytes 786440 | tf_op jit(solution)/shard_map/ppermute | solution.py:629
  28.3 0.5 collective-permute-start.11
  28.8 2.2 %collective-permute-start.12 = (bf16[256,512]{1,0:T(8,128)(2,1)S(1)}, bf16[256,512]{1,0:T(8,128)(2,1)S(1)}, u32[]{:S(2)}, u32[]{:S(2)}) collective-permute-start(bf16[256,512]{1,0:T(8,128)(2,1)S(1)} %keys.1.refs_4_), channel_id=1, source_target_pairs={{0,192},{4,52},{8,200},{12,60},{16,208},{20,4},{24,216},{28,12},{3... | collective-permute-start | bytes 786440 | tf_op jit(solution)/shard_map/ppermute | solution.py:629
  31.0 9.0 %collective-permute-start.8 = (bf16[256,1024]{1,0:T(8,128)(2,1)S(1)}, bf16[256,1024]{1,0:T(8,128)(2,1)S(1)}, u32[]{:S(2)}, u32[]{:S(2)}) collective-permute-start(bf16[256,1024]{1,0:T(8,128)(2,1)S(1)} %copy-done.6), channel_id=1, source_target_pairs={{4,8},{12,16},{20,24},{28,32},{36,40},{44,48},{52,56},{60,64},{68,... | collective-permute-start | bytes 1572872 | tf_op jit(solution)/shard_map/ppermute | solution.py:651
  40.2 2.0 %far.1 = (bf16[128,384]{1,0:T(8,128)(2,1)S(1)}, bf16[128,384]{1,0:T(8,128)(2,1)S(1)}, bf16[128,384]{1,0:T(8,128)(2,1)S(1)}, bf16[128,384]{1,0:T(8,128)(2,1)S(1)}) custom-call(bf16[128,256]{1,0:T(8,128)(2,1)S(1)} %half.1.refs_0_, bf16[128,256]{1,0:T(8,128)(2,1)S(1)} %collective-permute-done.3.refs_1_, bf16[128,256]{1,0:T(8,128)(2,1)S(1)} %collective-permute-done.4.refs_2_, ...), custom_call_target="tpu_custom_call" | custom-call | bytes 1000 | tf_op jit(solution)/shard_map/far/pallas_call | solution.py:501
  42.2 2.6 %collective-permute-start.15 = (bf16[128,384]{1,0:T(8,128)(2,1)S(1)}, bf16[128,384]{1,0:T(8,128)(2,1)S(1)}, u32[]{:S(2)}, u32[]{:S(2)}) collective-permute-start(bf16[128,384]{1,0:T(8,128)(2,1)S(1)} %get-tuple-element.83), channel_id=1, source_target_pairs={{0,32},{4,132},{8,40},{12,140},{16,48},{20,148},{24,56},{28,156},{... | collective-permute-start | bytes 294920 | tf_op jit(solution)/shard_map/ppermute | solution.py:629
  44.8 0.8 %collective-permute-start.16 = (bf16[128,384]{1,0:T(8,128)(2,1)S(1)}, bf16[128,384]{1,0:T(8,128)(2,1)S(1)}, u32[]{:S(2)}, u32[]{:S(2)}) collective-permute-start(bf16[128,384]{1,0:T(8,128)(2,1)S(1)} %get-tuple-element.84), channel_id=1, source_target_pairs={{0,48},{4,196},{8,56},{12,204},{16,0},{20,212},{24,8},{28,220},{32... | collective-permute-start | bytes 294920 | tf_op jit(solution)/shard_map/ppermute | solution.py:629
  45.6 0.7 %collective-permute-start.17 = (bf16[128,384]{1,0:T(8,128)(2,1)S(1)}, bf16[128,384]{1,0:T(8,128)(2,1)S(1)}, u32[]{:S(2)}, u32[]{:S(2)}) collective-permute-start(bf16[128,384]{1,0:T(8,128)(2,1)S(1)} %get-tuple-element.85), channel_id=1, source_target_pairs={{0,16},{4,68},{8,24},{12,76},{16,32},{20,84},{24,40},{28,92},{32,4... | collective-permute-start | bytes 294920 | tf_op jit(solution)/shard_map/ppermute | solution.py:629
  46.4 1.4 %near.1 = (f32[256,512]{1,0:T(8,128)S(1)}, f32[256,512]{1,0:T(8,128)S(1)}, f32[256,512]{1,0:T(8,128)S(1)}) custom-call(bf16[256,512]{1,0:T(8,128)(2,1)S(1)} %get-tuple-element.72.q, f32[448,512]{1,0:T(8,128)S(1)} %get-tuple-element.59.km, f32[448,512]{1,0:T(8,128)S(1)} %get-tuple-element.60.kl, f32[448,512]{1,0:T(8,128)S(1)} %get-tuple-element.61.ka, ...), custom_call_target="tpu_custom_call" | custom-call | bytes 1000 | tf_op jit(solution)/shard_map/near/pallas_call | solution.py:424
  47.8 1.1 %across.1 = (f32[256,512]{1,0:T(8,128)S(1)}, f32[256,512]{1,0:T(8,128)S(1)}, f32[256,512]{1,0:T(8,128)S(1)}) custom-call(bf16[256,512]{1,0:T(8,128)(2,1)S(1)} %get-tuple-element.72.q, f32[256,512]{1,0:T(8,128)S(1)} %get-tuple-element.73.nm, f32[256,512]{1,0:T(8,128)S(1)} %get-tuple-element.74.nl, f32[256,512]{1,0:T(8,128)S(1)} %get-tuple-element.75.na, ...), custom_call_target="tpu_custom_call" | custom-call | bytes 1000 | tf_op jit(solution)/shard_map/across/pallas_call | solution.py:457
  49.0 1.6 %collective-permute-done.17.f3 = bf16[128,384]{1,0:T(8,128)(2,1)S(1)} collective-permute-done((bf16[128,384]{1,0:T(8,128)(2,1)S(1)}, bf16[128,384]{1,0:T(8,128)(2,1)S(1)}, u32[]{:S(2)}, u32[]{:S(2)}) %collective-permute-start.17) | collective-permute-done | bytes 98336 | tf_op jit(solution)/shard_map/ppermute | solution.py:629
  50.9 0.8 %collective-permute-start.18 = (f32[128,512]{1,0:T(8,128)S(1)}, f32[128,512]{1,0:T(8,128)S(1)}, u32[]{:S(2)}, u32[]{:S(2)}) collective-permute-start(f32[128,512]{1,0:T(8,128)S(1)} %fold.1.mine), channel_id=1, source_target_pairs={{0,4},{4,0},{8,12},{12,8},{16,20},{20,16},{24,28},{28,24},{32,36},... | collective-permute-start | bytes 786440 | tf_op jit(solution)/shard_map/ppermute | solution.py:618
  51.8 1.2 %halo.1 = (bf16[256,512]{1,0:T(8,128)(2,1)S(1)}, f32[64,512]{1,0:T(8,128)S(1)}, f32[64,512]{1,0:T(8,128)S(1)}, f32[64,512]{1,0:T(8,128)S(1)}) custom-call(bf16[1024,256]{1,0:T(8,128)(2,1)S(1)} %get-tuple-element.51.res, bf16[1024,512]{1,0:T(8,128)(2,1)S(1)} %get-tuple-element.52.q, f32[448,512]{1,0:T(8,128)S(1)} %get-tuple-element.59.km, ...), custom_call_target="tpu_custom_call" | custom-call | bytes 1000 | tf_op jit(solution)/shard_map/halo/pallas_call | solution.py:394
  53.0 1.4 %join.1 = bf16[1024,512]{1,0:T(8,128)(2,1)} custom-call(bf16[64,1024]{1,0:T(8,128)(2,1)S(1)} %collective-permute-done.far_z, bf16[1024,256]{1,0:T(8,128)(2,1)S(1)} %get-tuple-element.51.res, f32[64,512]{1,0:T(8,128)S(1)} %get-tuple-element.69.hm, f32[64,512]{1,0:T(8,128)S(1)} %get-tuple-element.70.hl, f32[64,512]{1,0:T(8,128)S(1)} %get-tuple-element.71.ha, ...), custom_call_target="tpu_custom_call" | custom-call | bytes 1000 | tf_op jit(solution)/shard_map/join/pallas_call | solution.py:591
  (42 shorter events, 2.2 us)
Async XLA Ops:
  0.0 12.0 %copy-start.4 = (bf16[1024,512]{1,0:T(8,128)(2,1)S(1)}, bf16[1024,512]{1,0:T(8,128)(2,1)}, u32[]{:S(2)}) copy-start(bf16[1024,512]{1,0:T(8,128)(2,1)} %q_hbm.1) | copy-start | bytes 3145732
  3.2 8.8 %copy-start.5 = (s32[8,128]{1,0:T(8,128)S(1)}, s32[8,128]{1,0:T(8,128)}, u32[]{:S(2)}) copy-start(s32[8,128]{1,0:T(8,128)} %get-tuple-element.50.offs) | copy-start | bytes 12292
  3.2 20.6 %collective-permute-start = (bf16[64,1024]{1,0:T(8,128)(2,1)}, bf16[64,1024]{1,0:T(8,128)(2,1)S(1)}, u32[]{:S(2)}, u32[]{:S(2)}) collective-permute-start(bf16[64,1024]{1,0:T(8,128)(2,1)} %get-tuple-element.49.kv_far), channel_id=1, source_target_pairs={{0,8},{4,12},{8,0},{12,4},{16,24},{20,28},{24,16},{28,20},{32,40},... | collective-permute-start | bytes 393224 | tf_op jit(solution)/shard_map/ppermute | solution.py:618
  11.1 2.7 %collective-permute-start.1 = (bf16[256,1024]{1,0:T(8,128)(2,1)}, bf16[256,1024]{1,0:T(8,128)(2,1)S(1)}, u32[]{:S(2)}, u32[]{:S(2)}) collective-permute-start(bf16[256,1024]{1,0:T(8,128)(2,1)} %get-tuple-element.68), channel_id=1, source_target_pairs={{0,4},{4,0},{8,12},{12,8},{16,20},{20,16},{24,28},{28,24},{32,36},... | collective-permute-start | bytes 1572872 | tf_op jit(solution)/shard_map/ppermute | solution.py:618
  12.0 2.5 %collective-permute-start.6 = (bf16[256,1024]{1,0:T(8,128)(2,1)}, bf16[256,1024]{1,0:T(8,128)(2,1)S(1)}, u32[]{:S(2)}, u32[]{:S(2)}) collective-permute-start(bf16[256,1024]{1,0:T(8,128)(2,1)} %get-tuple-element.64.near), channel_id=1, source_target_pairs={{0,4},{4,0},{8,12},{12,8},{16,20},{20,16},{24,28},{28,24},{32,36},... | collective-permute-start | bytes 1572872 | tf_op jit(solution)/shard_map/ppermute | solution.py:618
  12.0 8.5 %copy-start = (bf16[1024,512]{1,0:T(8,128)(2,1)S(1)}, bf16[1024,512]{1,0:T(8,128)(2,1)}, u32[]{:S(2)}) copy-start(bf16[1024,512]{1,0:T(8,128)(2,1)} %k.1) | copy-start | bytes 3145732
  12.1 8.5 %copy-start.1 = (bf16[1024,512]{1,0:T(8,128)(2,1)S(1)}, bf16[1024,512]{1,0:T(8,128)(2,1)}, u32[]{:S(2)}) copy-start(bf16[1024,512]{1,0:T(8,128)(2,1)} %v.1) | copy-start | bytes 3145732
  13.8 1.2 %collective-permute-start.2 = (bf16[64,256]{1,0:T(8,128)(2,1)S(1)}, bf16[64,256]{1,0:T(8,128)(2,1)S(1)}, u32[]{:S(2)}, u32[]{:S(2)}) collective-permute-start(bf16[64,256]{1,0:T(8,128)(2,1)S(1)} %get-tuple-element.57), channel_id=1, source_target_pairs={{0,4},{4,0},{8,12},{12,8},{16,20},{20,16},{24,28},{28,24},{32,36},... | collective-permute-start | bytes 98312 | tf_op jit(solution)/shard_map/ppermute | solution.py:618
  14.5 25.5 %collective-permute-start.9 = (bf16[192,1024]{1,0:T(8,128)(2,1)S(1)}, bf16[192,1024]{1,0:T(8,128)(2,1)S(1)}, u32[]{:S(2)}, u32[]{:S(2)}) collective-permute-start(bf16[192,1024]{1,0:T(8,128)(2,1)S(1)} %copy-done.7), channel_id=1, source_target_pairs={{0,8},{4,12},{8,0},{12,4},{16,24},{20,28},{24,16},{28,20},{32,40},... | collective-permute-start | bytes 1179656 | tf_op jit(solution)/shard_map/ppermute | solution.py:618
  15.0 8.9 %collective-permute-start.3 = (bf16[128,256]{1,0:T(8,128)(2,1)S(1)}, bf16[128,256]{1,0:T(8,128)(2,1)S(1)}, u32[]{:S(2)}, u32[]{:S(2)}) collective-permute-start(bf16[128,256]{1,0:T(8,128)(2,1)S(1)} %half.1.refs_0_), channel_id=1, source_target_pairs={{0,32},{4,132},{8,40},{12,140},{16,48},{20,148},{24,56},{28,156},{... | collective-permute-start | bytes 196616 | tf_op jit(solution)/shard_map/ppermute | solution.py:629
  17.8 6.1 %collective-permute-start.4 = (bf16[128,256]{1,0:T(8,128)(2,1)S(1)}, bf16[128,256]{1,0:T(8,128)(2,1)S(1)}, u32[]{:S(2)}, u32[]{:S(2)}) collective-permute-start(bf16[128,256]{1,0:T(8,128)(2,1)S(1)} %half.1.refs_0_), channel_id=1, source_target_pairs={{0,16},{4,68},{8,24},{12,76},{16,32},{20,84},{24,40},{28,92},{32,4... | collective-permute-start | bytes 196616 | tf_op jit(solution)/shard_map/ppermute | solution.py:629
  18.2 5.7 %collective-permute-start.5 = (bf16[128,256]{1,0:T(8,128)(2,1)S(1)}, bf16[128,256]{1,0:T(8,128)(2,1)S(1)}, u32[]{:S(2)}, u32[]{:S(2)}) collective-permute-start(bf16[128,256]{1,0:T(8,128)(2,1)S(1)} %half.1.refs_0_), channel_id=1, source_target_pairs={{0,48},{4,196},{8,56},{12,204},{16,0},{20,212},{24,8},{28,220},{32... | collective-permute-start | bytes 196616 | tf_op jit(solution)/shard_map/ppermute | solution.py:629
  24.0 2.3 %collective-permute-start.7 = (bf16[64,512]{1,0:T(8,128)(2,1)S(1)}, bf16[64,512]{1,0:T(8,128)(2,1)S(1)}, u32[]{:S(2)}, u32[]{:S(2)}) collective-permute-start(bf16[64,512]{1,0:T(8,128)(2,1)S(1)} %get-tuple-element.67), channel_id=1, source_target_pairs={{0,4},{4,0},{8,12},{12,8},{16,20},{20,16},{24,28},{28,24},{32,36},... | collective-permute-start | bytes 196616 | tf_op jit(solution)/shard_map/ppermute | solution.py:618
  26.3 20.1 %copy-start.2 = (bf16[256,1024]{1,0:T(8,128)(2,1)S(1)}, bf16[256,1024]{1,0:T(8,128)(2,1)}, u32[]{:S(2)}) copy-start(bf16[256,1024]{1,0:T(8,128)(2,1)} %get-tuple-element.64.near) | copy-start | bytes 1572868
  26.3 13.7 %collective-permute-start.10 = (bf16[256,512]{1,0:T(8,128)(2,1)S(1)}, bf16[256,512]{1,0:T(8,128)(2,1)S(1)}, u32[]{:S(2)}, u32[]{:S(2)}) collective-permute-start(bf16[256,512]{1,0:T(8,128)(2,1)S(1)} %keys.1.refs_4_), channel_id=1, source_target_pairs={{0,128},{4,36},{8,136},{12,44},{16,144},{20,52},{24,152},{28,60},{... | collective-permute-start | bytes 786440 | tf_op jit(solution)/shard_map/ppermute | solution.py:629
  28.3 11.7 %collective-permute-start.11 = (bf16[256,512]{1,0:T(8,128)(2,1)S(1)}, bf16[256,512]{1,0:T(8,128)(2,1)S(1)}, u32[]{:S(2)}, u32[]{:S(2)}) collective-permute-start(bf16[256,512]{1,0:T(8,128)(2,1)S(1)} %keys.1.refs_4_), channel_id=1, source_target_pairs={{0,64},{4,20},{8,72},{12,28},{16,80},{20,36},{24,88},{28,44},{32,9... | collective-permute-start | bytes 786440 | tf_op jit(solution)/shard_map/ppermute | solution.py:629
  28.8 11.3 %collective-permute-start.12 = (bf16[256,512]{1,0:T(8,128)(2,1)S(1)}, bf16[256,512]{1,0:T(8,128)(2,1)S(1)}, u32[]{:S(2)}, u32[]{:S(2)}) collective-permute-start(bf16[256,512]{1,0:T(8,128)(2,1)S(1)} %keys.1.refs_4_), channel_id=1, source_target_pairs={{0,192},{4,52},{8,200},{12,60},{16,208},{20,4},{24,216},{28,12},{3... | collective-permute-start | bytes 786440 | tf_op jit(solution)/shard_map/ppermute | solution.py:629
  31.0 19.9 %collective-permute-start.8 = (bf16[256,1024]{1,0:T(8,128)(2,1)S(1)}, bf16[256,1024]{1,0:T(8,128)(2,1)S(1)}, u32[]{:S(2)}, u32[]{:S(2)}) collective-permute-start(bf16[256,1024]{1,0:T(8,128)(2,1)S(1)} %copy-done.6), channel_id=1, source_target_pairs={{4,8},{12,16},{20,24},{28,32},{36,40},{44,48},{52,56},{60,64},{68,... | collective-permute-start | bytes 1572872 | tf_op jit(solution)/shard_map/ppermute | solution.py:651
  40.1 2.1 %collective-permute-start.13 = (bf16[192,1024]{1,0:T(8,128)(2,1)S(1)}, bf16[192,1024]{1,0:T(8,128)(2,1)S(1)}, u32[]{:S(2)}, u32[]{:S(2)}) collective-permute-start(bf16[192,1024]{1,0:T(8,128)(2,1)S(1)} %collective-permute-done.9.rest_z), channel_id=1, source_target_pairs={{0,4},{4,0},{8,12},{12,8},{16,20},{20,16},{24,28},{28,24},{32,36},... | collective-permute-start | bytes 1179656 | tf_op jit(solution)/shard_map/ppermute | solution.py:618
  42.2 6.8 %collective-permute-start.15 = (bf16[128,384]{1,0:T(8,128)(2,1)S(1)}, bf16[128,384]{1,0:T(8,128)(2,1)S(1)}, u32[]{:S(2)}, u32[]{:S(2)}) collective-permute-start(bf16[128,384]{1,0:T(8,128)(2,1)S(1)} %get-tuple-element.83), channel_id=1, source_target_pairs={{0,32},{4,132},{8,40},{12,140},{16,48},{20,148},{24,56},{28,156},{... | collective-permute-start | bytes 294920 | tf_op jit(solution)/shard_map/ppermute | solution.py:629
  44.8 4.2 %collective-permute-start.16 = (bf16[128,384]{1,0:T(8,128)(2,1)S(1)}, bf16[128,384]{1,0:T(8,128)(2,1)S(1)}, u32[]{:S(2)}, u32[]{:S(2)}) collective-permute-start(bf16[128,384]{1,0:T(8,128)(2,1)S(1)} %get-tuple-element.84), channel_id=1, source_target_pairs={{0,48},{4,196},{8,56},{12,204},{16,0},{20,212},{24,8},{28,220},{32... | collective-permute-start | bytes 294920 | tf_op jit(solution)/shard_map/ppermute | solution.py:629
  45.6 5.0 %collective-permute-start.17 = (bf16[128,384]{1,0:T(8,128)(2,1)S(1)}, bf16[128,384]{1,0:T(8,128)(2,1)S(1)}, u32[]{:S(2)}, u32[]{:S(2)}) collective-permute-start(bf16[128,384]{1,0:T(8,128)(2,1)S(1)} %get-tuple-element.85), channel_id=1, source_target_pairs={{0,16},{4,68},{8,24},{12,76},{16,32},{20,84},{24,40},{28,92},{32,4... | collective-permute-start | bytes 294920 | tf_op jit(solution)/shard_map/ppermute | solution.py:629
  46.3 1.5 %collective-permute-start.14 = (bf16[64,512]{1,0:T(8,128)(2,1)S(1)}, bf16[64,512]{1,0:T(8,128)(2,1)S(1)}, u32[]{:S(2)}, u32[]{:S(2)}) collective-permute-start(bf16[64,512]{1,0:T(8,128)(2,1)S(1)} %get-tuple-element.86.keep), channel_id=1, source_target_pairs={{0,4},{4,0},{8,12},{12,8},{16,20},{20,16},{24,28},{28,24},{32,36},... | collective-permute-start | bytes 196616 | tf_op jit(solution)/shard_map/ppermute | solution.py:618
  50.9 2.0 %collective-permute-start.18 = (f32[128,512]{1,0:T(8,128)S(1)}, f32[128,512]{1,0:T(8,128)S(1)}, u32[]{:S(2)}, u32[]{:S(2)}) collective-permute-start(f32[128,512]{1,0:T(8,128)S(1)} %fold.1.mine), channel_id=1, source_target_pairs={{0,4},{4,0},{8,12},{12,8},{16,20},{20,16},{24,28},{28,24},{32,36},... | collective-permute-start | bytes 786440 | tf_op jit(solution)/shard_map/ppermute | solution.py:618
  (3 other events, 9.6 us)

commit v6 on v5

--- a/solution.py
+++ b/solution.py
@@ -170,8 +170,8 @@
             pltpu.SMEM((HEADS,), jnp.int32),
             pltpu.VMEM((TOK, COLS), BF16),
             pltpu.VMEM((TOK, COLS), BF16),
-            pltpu.VMEM((HEADS, TOK, DH), F32),
-            pltpu.VMEM((HEADS, TOK, DH), F32),
+            pltpu.VMEM((HEADS, TOK + R2, DH), F32),
+            pltpu.VMEM((HEADS, TOK + R2, DH), F32),
             pltpu.SemaphoreType.DMA,
             pltpu.SemaphoreType.DMA((2, BLOCKS + 1)),
         ],
@@ -181,23 +181,15 @@
     )(*args)
 
 
-def queries_kernel(offs, q_hbm, qp, qn, q_keep, q_give, res, q, sems):
+def queries_kernel(offs, q, qp, qn, q_keep, q_give, res):
     core = lax.axis_index("seq") & 1
     qf = {}
-    copies = []
-    for b in range(BLOCKS):
-        copies.append(
-            pltpu.make_async_copy(q_hbm.at[block_rows(b), :], q.at[block_rows(b), :], sems.at[b])
-        )
-        copies[-1].start()
     sels = []
     for h in range(HEADS):
         offset = offset_rows(offs, h, W0)
         sels.append(select_matrix(offset, 0, W0))
         res[block_rows(h), :] = restore_matrix(offset, 0, W0)
     for b in range(0, BLOCKS, 2):
-        copies[b].wait()
-        copies[b + 1].wait()
         for h in range(HEADS):
             c = head_cols(h)
             pair = jnp.concatenate([q[block_rows(b), c], q[block_rows(b + 1), c]], 1)
@@ -225,9 +217,8 @@
             out_of(FROWS, HALF),
             out_of(HEADS * W0, W0),
         ],
-        in_specs=[VMEM, HBM],
+        in_specs=[VMEM] * 2,
         out_specs=[VMEM] * 5,
-        scratch_shapes=[pltpu.VMEM((TOK, COLS), BF16), pltpu.SemaphoreType.DMA((BLOCKS,))],
         compiler_params=params(16),
         cost_estimate=cost(12),
         name="queries",

time: 55.2 us -> 55.2 us (level)
  transfers between devices with their start and end apart: 19 -> 19, of which waited for: 5 -> 5; matrix products, arithmetic and copies ran while one was open for 0% -> 0% of each run, Pallas kernels for 19% -> 18%
where the time goes in v6:
time: 55.2 us; the launch traced here: 54.5 us
  starting transfers between devices  35.1 us (64%)
  Pallas kernels  14.6 us (26%)
  waiting for transfers between devices  4.29 us (8%)
    ppermute x9, starting transfers between devices, turn(): return lax.ppermute(value, 'seq', pairs)  14.3 us
    ppermute x9, starting transfers between devices, send(): return lax.ppermute(value, 'seq', moves(**shift))  11.8 us
    ppermute x1, starting transfers between devices, shards(): halo = lax.ppermute(halo, 'seq', [(s, s + 1) for s in range(1, 63, 2)])  9.04 us
    pallas_call x1, Pallas kernels, local(): pl.pallas_call(local_kernel, out_shape=[out_of(TOK - W0, COLS), state, st...  3.33 us
    pallas_call x1, Pallas kernels, extract(): pl.pallas_call(extract_kernel, out_shape=[out_of(8, DH, dtype=jnp.int32),...  3.22 us
    ppermute x9, waiting for transfers between devices, send(): return lax.ppermute(value, 'seq', moves(**shift))  2.65 us
    pallas_call x1, Pallas kernels, far(): pl.pallas_call(far_kernel, out_shape=[out_of(2 * FROWS, SENT)] * 4, in_sp...  1.96 us
    ppermute x9, waiting for transfers between devices, turn(): return lax.ppermute(value, 'seq', pairs)  1.64 us
  transfers between devices with their start and end apart: 19, of which 5 were waited for; matrix products, arithmetic and copies ran while one was open for 0% of the time, Pallas kernels for 18%

profile of v6, /device:TPU:1, one launch (start us, length us, event | category | flops | bytes accessed | tf_op | source)
XLA Modules:
  0.0 54.5 jit_solution(17939246554276409267)
XLA Ops:
  0.0 3.2 %extract.1 = (s32[8,128]{1,0:T(8,128)}, bf16[64,1024]{1,0:T(8,128)(2,1)}, bf16[192,1024]{1,0:T(8,128)(2,1)}, bf16[256,1024]{1,0:T(8,128)(2,1)}, bf16[256,1024]{1,0:T(8,128)(2,1)}) custom-call(s32[4]{0:T(128)} %off_hbm.1, bf16[1024,512]{1,0:T(8,128)(2,1)} %k.1, bf16[1024,512]{1,0:T(8,128)(2,1)} %v.1), custom_call_target="tpu_custom_call" | custom-call | bytes 1000 | tf_op jit(solution)/shard_map/extract/pallas_call | solution.py:158
  3.2 7.8 %collective-permute-start = (bf16[64,1024]{1,0:T(8,128)(2,1)}, bf16[64,1024]{1,0:T(8,128)(2,1)S(1)}, u32[]{:S(2)}, u32[]{:S(2)}) collective-permute-start(bf16[64,1024]{1,0:T(8,128)(2,1)} %get-tuple-element.49.kv_far), channel_id=1, source_target_pairs={{0,8},{4,12},{8,0},{12,4},{16,24},{20,28},{24,16},{28,20},{32,40},... | collective-permute-start | bytes 393224 | tf_op jit(solution)/shard_map/ppermute | solution.py:609
  11.1 1.0 %collective-permute-start.1 = (bf16[256,1024]{1,0:T(8,128)(2,1)}, bf16[256,1024]{1,0:T(8,128)(2,1)S(1)}, u32[]{:S(2)}, u32[]{:S(2)}) collective-permute-start(bf16[256,1024]{1,0:T(8,128)(2,1)} %get-tuple-element.68), channel_id=1, source_target_pairs={{0,4},{4,0},{8,12},{12,8},{16,20},{20,16},{24,28},{28,24},{32,36},... | collective-permute-start | bytes 1572872 | tf_op jit(solution)/shard_map/ppermute | solution.py:609
  12.1 0.6 %queries.1 = (bf16[1024,512]{1,0:T(8,128)(2,1)S(1)}, bf16[256,512]{1,0:T(8,128)(2,1)S(1)}, bf16[64,256]{1,0:T(8,128)(2,1)S(1)}, bf16[64,256]{1,0:T(8,128)(2,1)S(1)}, bf16[1024,256]{1,0:T(8,128)(2,1)S(1)}) custom-call(s32[8,128]{1,0:T(8,128)S(1)} %copy-done.5, bf16[1024,512]{1,0:T(8,128)(2,1)S(1)} %copy-done.4), custom_call_target="tpu_custom_call" | custom-call | flops 12000000000 | bytes 1000 | tf_op jit(solution)/shard_map/queries/pallas_call | solution.py:211
  12.7 1.1 %collective-permute-done.1.halo_c = bf16[256,1024]{1,0:T(8,128)(2,1)S(1)} collective-permute-done((bf16[256,1024]{1,0:T(8,128)(2,1)}, bf16[256,1024]{1,0:T(8,128)(2,1)S(1)}, u32[]{:S(2)}, u32[]{:S(2)}) %collective-permute-start.1) | collective-permute-done | bytes 524320 | tf_op jit(solution)/shard_map/ppermute | solution.py:609
  15.0 2.8 %collective-permute-start.3 = (bf16[128,256]{1,0:T(8,128)(2,1)S(1)}, bf16[128,256]{1,0:T(8,128)(2,1)S(1)}, u32[]{:S(2)}, u32[]{:S(2)}) collective-permute-start(bf16[128,256]{1,0:T(8,128)(2,1)S(1)} %half.1.refs_0_), channel_id=1, source_target_pairs={{0,32},{4,132},{8,40},{12,140},{16,48},{20,148},{24,56},{28,156},{... | collective-permute-start | bytes 196616 | tf_op jit(solution)/shard_map/ppermute | solution.py:620
  18.2 2.4 %collective-permute-start.5 = (bf16[128,256]{1,0:T(8,128)(2,1)S(1)}, bf16[128,256]{1,0:T(8,128)(2,1)S(1)}, u32[]{:S(2)}, u32[]{:S(2)}) collective-permute-start(bf16[128,256]{1,0:T(8,128)(2,1)S(1)} %half.1.refs_0_), channel_id=1, source_target_pairs={{0,48},{4,196},{8,56},{12,204},{16,0},{20,212},{24,8},{28,220},{32... | collective-permute-start | bytes 196616 | tf_op jit(solution)/shard_map/ppermute | solution.py:620
  20.5 3.3 %local.1 = (bf16[768,512]{1,0:T(8,128)(2,1)S(1)}, f32[448,512]{1,0:T(8,128)S(1)}, f32[448,512]{1,0:T(8,128)S(1)}, f32[448,512]{1,0:T(8,128)S(1)}) custom-call(bf16[1024,256]{1,0:T(8,128)(2,1)S(1)} %get-tuple-element.51.res, bf16[1024,512]{1,0:T(8,128)(2,1)S(1)} %get-tuple-element.52.q, bf16[1024,512]{1,0:T(8,128)(2,1)S(1)} %copy-done, ...), custom_call_target="tpu_custom_call" | custom-call | flops 1000000000 | bytes 1000 | tf_op jit(solution)/shard_map/local/pallas_call | solution.py:341
  24.0 1.4 %collective-permute-start.7 = (bf16[64,512]{1,0:T(8,128)(2,1)S(1)}, bf16[64,512]{1,0:T(8,128)(2,1)S(1)}, u32[]{:S(2)}, u32[]{:S(2)}) collective-permute-start(bf16[64,512]{1,0:T(8,128)(2,1)S(1)} %get-tuple-element.67), channel_id=1, source_target_pairs={{0,4},{4,0},{8,12},{12,8},{16,20},{20,16},{24,28},{28,24},{32,36},... | collective-permute-start | bytes 196616 | tf_op jit(solution)/shard_map/ppermute | solution.py:609
  25.4 0.9 %collective-permute-done.7.given = bf16[64,512]{1,0:T(8,128)(2,1)S(1)} collective-permute-done((bf16[64,512]{1,0:T(8,128)(2,1)S(1)}, bf16[64,512]{1,0:T(8,128)(2,1)S(1)}, u32[]{:S(2)}, u32[]{:S(2)}) %collective-permute-start.7) | collective-permute-done | bytes 65568 | tf_op jit(solution)/shard_map/ppermute | solution.py:609
  26.3 2.0 %collective-permute-start.10 = (bf16[256,512]{1,0:T(8,128)(2,1)S(1)}, bf16[256,512]{1,0:T(8,128)(2,1)S(1)}, u32[]{:S(2)}, u32[]{:S(2)}) collective-permute-start(bf16[256,512]{1,0:T(8,128)(2,1)S(1)} %keys.1.refs_4_), channel_id=1, source_target_pairs={{0,128},{4,36},{8,136},{12,44},{16,144},{20,52},{24,152},{28,60},{... | collective-permute-start | bytes 786440 | tf_op jit(solution)/shard_map/ppermute | solution.py:620
  28.3 0.5 collective-permute-start.11
  28.8 2.2 %collective-permute-start.12 = (bf16[256,512]{1,0:T(8,128)(2,1)S(1)}, bf16[256,512]{1,0:T(8,128)(2,1)S(1)}, u32[]{:S(2)}, u32[]{:S(2)}) collective-permute-start(bf16[256,512]{1,0:T(8,128)(2,1)S(1)} %keys.1.refs_4_), channel_id=1, source_target_pairs={{0,192},{4,52},{8,200},{12,60},{16,208},{20,4},{24,216},{28,12},{3... | collective-permute-start | bytes 786440 | tf_op jit(solution)/shard_map/ppermute | solution.py:620
  31.0 9.0 %collective-permute-start.8 = (bf16[256,1024]{1,0:T(8,128)(2,1)S(1)}, bf16[256,1024]{1,0:T(8,128)(2,1)S(1)}, u32[]{:S(2)}, u32[]{:S(2)}) collective-permute-start(bf16[256,1024]{1,0:T(8,128)(2,1)S(1)} %copy-done.6), channel_id=1, source_target_pairs={{4,8},{12,16},{20,24},{28,32},{36,40},{44,48},{52,56},{60,64},{68,... | collective-permute-start | bytes 1572872 | tf_op jit(solution)/shard_map/ppermute | solution.py:642
  40.2 2.0 %far.1 = (bf16[128,384]{1,0:T(8,128)(2,1)S(1)}, bf16[128,384]{1,0:T(8,128)(2,1)S(1)}, bf16[128,384]{1,0:T(8,128)(2,1)S(1)}, bf16[128,384]{1,0:T(8,128)(2,1)S(1)}) custom-call(bf16[128,256]{1,0:T(8,128)(2,1)S(1)} %half.1.refs_0_, bf16[128,256]{1,0:T(8,128)(2,1)S(1)} %collective-permute-done.3.refs_1_, bf16[128,256]{1,0:T(8,128)(2,1)S(1)} %collective-permute-done.4.refs_2_, ...), custom_call_target="tpu_custom_call" | custom-call | bytes 1000 | tf_op jit(solution)/shard_map/far/pallas_call | solution.py:492
  42.2 2.6 %collective-permute-start.15 = (bf16[128,384]{1,0:T(8,128)(2,1)S(1)}, bf16[128,384]{1,0:T(8,128)(2,1)S(1)}, u32[]{:S(2)}, u32[]{:S(2)}) collective-permute-start(bf16[128,384]{1,0:T(8,128)(2,1)S(1)} %get-tuple-element.83), channel_id=1, source_target_pairs={{0,32},{4,132},{8,40},{12,140},{16,48},{20,148},{24,56},{28,156},{... | collective-permute-start | bytes 294920 | tf_op jit(solution)/shard_map/ppermute | solution.py:620
  44.8 0.8 %collective-permute-start.16 = (bf16[128,384]{1,0:T(8,128)(2,1)S(1)}, bf16[128,384]{1,0:T(8,128)(2,1)S(1)}, u32[]{:S(2)}, u32[]{:S(2)}) collective-permute-start(bf16[128,384]{1,0:T(8,128)(2,1)S(1)} %get-tuple-element.84), channel_id=1, source_target_pairs={{0,48},{4,196},{8,56},{12,204},{16,0},{20,212},{24,8},{28,220},{32... | collective-permute-start | bytes 294920 | tf_op jit(solution)/shard_map/ppermute | solution.py:620
  45.6 0.7 %collective-permute-start.17 = (bf16[128,384]{1,0:T(8,128)(2,1)S(1)}, bf16[128,384]{1,0:T(8,128)(2,1)S(1)}, u32[]{:S(2)}, u32[]{:S(2)}) collective-permute-start(bf16[128,384]{1,0:T(8,128)(2,1)S(1)} %get-tuple-element.85), channel_id=1, source_target_pairs={{0,16},{4,68},{8,24},{12,76},{16,32},{20,84},{24,40},{28,92},{32,4... | collective-permute-start | bytes 294920 | tf_op jit(solution)/shard_map/ppermute | solution.py:620
  46.4 1.4 %near.1 = (f32[256,512]{1,0:T(8,128)S(1)}, f32[256,512]{1,0:T(8,128)S(1)}, f32[256,512]{1,0:T(8,128)S(1)}) custom-call(bf16[256,512]{1,0:T(8,128)(2,1)S(1)} %get-tuple-element.72.q, f32[448,512]{1,0:T(8,128)S(1)} %get-tuple-element.59.km, f32[448,512]{1,0:T(8,128)S(1)} %get-tuple-element.60.kl, f32[448,512]{1,0:T(8,128)S(1)} %get-tuple-element.61.ka, ...), custom_call_target="tpu_custom_call" | custom-call | bytes 1000 | tf_op jit(solution)/shard_map/near/pallas_call | solution.py:415
  47.8 1.1 %across.1 = (f32[256,512]{1,0:T(8,128)S(1)}, f32[256,512]{1,0:T(8,128)S(1)}, f32[256,512]{1,0:T(8,128)S(1)}) custom-call(bf16[256,512]{1,0:T(8,128)(2,1)S(1)} %get-tuple-element.72.q, f32[256,512]{1,0:T(8,128)S(1)} %get-tuple-element.73.nm, f32[256,512]{1,0:T(8,128)S(1)} %get-tuple-element.74.nl, f32[256,512]{1,0:T(8,128)S(1)} %get-tuple-element.75.na, ...), custom_call_target="tpu_custom_call" | custom-call | bytes 1000 | tf_op jit(solution)/shard_map/across/pallas_call | solution.py:448
  49.0 1.6 %collective-permute-done.17.f3 = bf16[128,384]{1,0:T(8,128)(2,1)S(1)} collective-permute-done((bf16[128,384]{1,0:T(8,128)(2,1)S(1)}, bf16[128,384]{1,0:T(8,128)(2,1)S(1)}, u32[]{:S(2)}, u32[]{:S(2)}) %collective-permute-start.17) | collective-permute-done | bytes 98336 | tf_op jit(solution)/shard_map/ppermute | solution.py:620
  50.9 0.8 %collective-permute-start.18 = (f32[128,512]{1,0:T(8,128)S(1)}, f32[128,512]{1,0:T(8,128)S(1)}, u32[]{:S(2)}, u32[]{:S(2)}) collective-permute-start(f32[128,512]{1,0:T(8,128)S(1)} %fold.1.mine), channel_id=1, source_target_pairs={{0,4},{4,0},{8,12},{12,8},{16,20},{20,16},{24,28},{28,24},{32,36},... | collective-permute-start | bytes 786440 | tf_op jit(solution)/shard_map/ppermute | solution.py:609
  51.8 1.2 %halo.1 = (bf16[256,512]{1,0:T(8,128)(2,1)S(1)}, f32[64,512]{1,0:T(8,128)S(1)}, f32[64,512]{1,0:T(8,128)S(1)}, f32[64,512]{1,0:T(8,128)S(1)}) custom-call(bf16[1024,256]{1,0:T(8,128)(2,1)S(1)} %get-tuple-element.51.res, bf16[1024,512]{1,0:T(8,128)(2,1)S(1)} %get-tuple-element.52.q, f32[448,512]{1,0:T(8,128)S(1)} %get-tuple-element.59.km, ...), custom_call_target="tpu_custom_call" | custom-call | bytes 1000 | tf_op jit(solution)/shard_map/halo/pallas_call | solution.py:385
  53.0 1.4 %join.1 = bf16[1024,512]{1,0:T(8,128)(2,1)} custom-call(bf16[64,1024]{1,0:T(8,128)(2,1)S(1)} %collective-permute-done.far_z, bf16[1024,256]{1,0:T(8,128)(2,1)S(1)} %get-tuple-element.51.res, f32[64,512]{1,0:T(8,128)S(1)} %get-tuple-element.69.hm, f32[64,512]{1,0:T(8,128)S(1)} %get-tuple-element.70.hl, f32[64,512]{1,0:T(8,128)S(1)} %get-tuple-element.71.ha, ...), custom_call_target="tpu_custom_call" | custom-call | bytes 1000 | tf_op jit(solution)/shard_map/join/pallas_call | solution.py:582
  (42 shorter events, 2.2 us)
Async XLA Ops:
  0.0 12.0 %copy-start.4 = (bf16[1024,512]{1,0:T(8,128)(2,1)S(1)}, bf16[1024,512]{1,0:T(8,128)(2,1)}, u32[]{:S(2)}) copy-start(bf16[1024,512]{1,0:T(8,128)(2,1)} %q.1) | copy-start | bytes 3145732
  3.2 8.8 %copy-start.5 = (s32[8,128]{1,0:T(8,128)S(1)}, s32[8,128]{1,0:T(8,128)}, u32[]{:S(2)}) copy-start(s32[8,128]{1,0:T(8,128)} %get-tuple-element.50.offs) | copy-start | bytes 12292
  3.2 20.6 %collective-permute-start = (bf16[64,1024]{1,0:T(8,128)(2,1)}, bf16[64,1024]{1,0:T(8,128)(2,1)S(1)}, u32[]{:S(2)}, u32[]{:S(2)}) collective-permute-start(bf16[64,1024]{1,0:T(8,128)(2,1)} %get-tuple-element.49.kv_far), channel_id=1, source_target_pairs={{0,8},{4,12},{8,0},{12,4},{16,24},{20,28},{24,16},{28,20},{32,40},... | collective-permute-start | bytes 393224 | tf_op jit(solution)/shard_map/ppermute | solution.py:609
  11.1 2.7 %collective-permute-start.1 = (bf16[256,1024]{1,0:T(8,128)(2,1)}, bf16[256,1024]{1,0:T(8,128)(2,1)S(1)}, u32[]{:S(2)}, u32[]{:S(2)}) collective-permute-start(bf16[256,1024]{1,0:T(8,128)(2,1)} %get-tuple-element.68), channel_id=1, source_target_pairs={{0,4},{4,0},{8,12},{12,8},{16,20},{20,16},{24,28},{28,24},{32,36},... | collective-permute-start | bytes 1572872 | tf_op jit(solution)/shard_map/ppermute | solution.py:609
  12.0 2.5 %collective-permute-start.6 = (bf16[256,1024]{1,0:T(8,128)(2,1)}, bf16[256,1024]{1,0:T(8,128)(2,1)S(1)}, u32[]{:S(2)}, u32[]{:S(2)}) collective-permute-start(bf16[256,1024]{1,0:T(8,128)(2,1)} %get-tuple-element.64.near), channel_id=1, source_target_pairs={{0,4},{4,0},{8,12},{12,8},{16,20},{20,16},{24,28},{28,24},{32,36},... | collective-permute-start | bytes 1572872 | tf_op jit(solution)/shard_map/ppermute | solution.py:609
  12.0 8.5 %copy-start = (bf16[1024,512]{1,0:T(8,128)(2,1)S(1)}, bf16[1024,512]{1,0:T(8,128)(2,1)}, u32[]{:S(2)}) copy-start(bf16[1024,512]{1,0:T(8,128)(2,1)} %k.1) | copy-start | bytes 3145732
  12.1 8.5 %copy-start.1 = (bf16[1024,512]{1,0:T(8,128)(2,1)S(1)}, bf16[1024,512]{1,0:T(8,128)(2,1)}, u32[]{:S(2)}) copy-start(bf16[1024,512]{1,0:T(8,128)(2,1)} %v.1) | copy-start | bytes 3145732
  13.8 1.2 %collective-permute-start.2 = (bf16[64,256]{1,0:T(8,128)(2,1)S(1)}, bf16[64,256]{1,0:T(8,128)(2,1)S(1)}, u32[]{:S(2)}, u32[]{:S(2)}) collective-permute-start(bf16[64,256]{1,0:T(8,128)(2,1)S(1)} %get-tuple-element.57), channel_id=1, source_target_pairs={{0,4},{4,0},{8,12},{12,8},{16,20},{20,16},{24,28},{28,24},{32,36},... | collective-permute-start | bytes 98312 | tf_op jit(solution)/shard_map/ppermute | solution.py:609
  14.5 25.5 %collective-permute-start.9 = (bf16[192,1024]{1,0:T(8,128)(2,1)S(1)}, bf16[192,1024]{1,0:T(8,128)(2,1)S(1)}, u32[]{:S(2)}, u32[]{:S(2)}) collective-permute-start(bf16[192,1024]{1,0:T(8,128)(2,1)S(1)} %copy-done.7), channel_id=1, source_target_pairs={{0,8},{4,12},{8,0},{12,4},{16,24},{20,28},{24,16},{28,20},{32,40},... | collective-permute-start | bytes 1179656 | tf_op jit(solution)/shard_map/ppermute | solution.py:609
  15.0 8.9 %collective-permute-start.3 = (bf16[128,256]{1,0:T(8,128)(2,1)S(1)}, bf16[128,256]{1,0:T(8,128)(2,1)S(1)}, u32[]{:S(2)}, u32[]{:S(2)}) collective-permute-start(bf16[128,256]{1,0:T(8,128)(2,1)S(1)} %half.1.refs_0_), channel_id=1, source_target_pairs={{0,32},{4,132},{8,40},{12,140},{16,48},{20,148},{24,56},{28,156},{... | collective-permute-start | bytes 196616 | tf_op jit(solution)/shard_map/ppermute | solution.py:620
  17.8 6.1 %collective-permute-start.4 = (bf16[128,256]{1,0:T(8,128)(2,1)S(1)}, bf16[128,256]{1,0:T(8,128)(2,1)S(1)}, u32[]{:S(2)}, u32[]{:S(2)}) collective-permute-start(bf16[128,256]{1,0:T(8,128)(2,1)S(1)} %half.1.refs_0_), channel_id=1, source_target_pairs={{0,16},{4,68},{8,24},{12,76},{16,32},{20,84},{24,40},{28,92},{32,4... | collective-permute-start | bytes 196616 | tf_op jit(solution)/shard_map/ppermute | solution.py:620
  18.2 5.7 %collective-permute-start.5 = (bf16[128,256]{1,0:T(8,128)(2,1)S(1)}, bf16[128,256]{1,0:T(8,128)(2,1)S(1)}, u32[]{:S(2)}, u32[]{:S(2)}) collective-permute-start(bf16[128,256]{1,0:T(8,128)(2,1)S(1)} %half.1.refs_0_), channel_id=1, source_target_pairs={{0,48},{4,196},{8,56},{12,204},{16,0},{20,212},{24,8},{28,220},{32... | collective-permute-start | bytes 196616 | tf_op jit(solution)/shard_map/ppermute | solution.py:620
  24.0 2.3 %collective-permute-start.7 = (bf16[64,512]{1,0:T(8,128)(2,1)S(1)}, bf16[64,512]{1,0:T(8,128)(2,1)S(1)}, u32[]{:S(2)}, u32[]{:S(2)}) collective-permute-start(bf16[64,512]{1,0:T(8,128)(2,1)S(1)} %get-tuple-element.67), channel_id=1, source_target_pairs={{0,4},{4,0},{8,12},{12,8},{16,20},{20,16},{24,28},{28,24},{32,36},... | collective-permute-start | bytes 196616 | tf_op jit(solution)/shard_map/ppermute | solution.py:609
  26.3 20.1 %copy-start.2 = (bf16[256,1024]{1,0:T(8,128)(2,1)S(1)}, bf16[256,1024]{1,0:T(8,128)(2,1)}, u32[]{:S(2)}) copy-start(bf16[256,1024]{1,0:T(8,128)(2,1)} %get-tuple-element.64.near) | copy-start | bytes 1572868
  26.3 13.7 %collective-permute-start.10 = (bf16[256,512]{1,0:T(8,128)(2,1)S(1)}, bf16[256,512]{1,0:T(8,128)(2,1)S(1)}, u32[]{:S(2)}, u32[]{:S(2)}) collective-permute-start(bf16[256,512]{1,0:T(8,128)(2,1)S(1)} %keys.1.refs_4_), channel_id=1, source_target_pairs={{0,128},{4,36},{8,136},{12,44},{16,144},{20,52},{24,152},{28,60},{... | collective-permute-start | bytes 786440 | tf_op jit(solution)/shard_map/ppermute | solution.py:620
  28.3 11.7 %collective-permute-start.11 = (bf16[256,512]{1,0:T(8,128)(2,1)S(1)}, bf16[256,512]{1,0:T(8,128)(2,1)S(1)}, u32[]{:S(2)}, u32[]{:S(2)}) collective-permute-start(bf16[256,512]{1,0:T(8,128)(2,1)S(1)} %keys.1.refs_4_), channel_id=1, source_target_pairs={{0,64},{4,20},{8,72},{12,28},{16,80},{20,36},{24,88},{28,44},{32,9... | collective-permute-start | bytes 786440 | tf_op jit(solution)/shard_map/ppermute | solution.py:620
  28.8 11.3 %collective-permute-start.12 = (bf16[256,512]{1,0:T(8,128)(2,1)S(1)}, bf16[256,512]{1,0:T(8,128)(2,1)S(1)}, u32[]{:S(2)}, u32[]{:S(2)}) collective-permute-start(bf16[256,512]{1,0:T(8,128)(2,1)S(1)} %keys.1.refs_4_), channel_id=1, source_target_pairs={{0,192},{4,52},{8,200},{12,60},{16,208},{20,4},{24,216},{28,12},{3... | collective-permute-start | bytes 786440 | tf_op jit(solution)/shard_map/ppermute | solution.py:620
  31.0 19.9 %collective-permute-start.8 = (bf16[256,1024]{1,0:T(8,128)(2,1)S(1)}, bf16[256,1024]{1,0:T(8,128)(2,1)S(1)}, u32[]{:S(2)}, u32[]{:S(2)}) collective-permute-start(bf16[256,1024]{1,0:T(8,128)(2,1)S(1)} %copy-done.6), channel_id=1, source_target_pairs={{4,8},{12,16},{20,24},{28,32},{36,40},{44,48},{52,56},{60,64},{68,... | collective-permute-start | bytes 1572872 | tf_op jit(solution)/shard_map/ppermute | solution.py:642
  40.1 2.1 %collective-permute-start.13 = (bf16[192,1024]{1,0:T(8,128)(2,1)S(1)}, bf16[192,1024]{1,0:T(8,128)(2,1)S(1)}, u32[]{:S(2)}, u32[]{:S(2)}) collective-permute-start(bf16[192,1024]{1,0:T(8,128)(2,1)S(1)} %collective-permute-done.9.rest_z), channel_id=1, source_target_pairs={{0,4},{4,0},{8,12},{12,8},{16,20},{20,16},{24,28},{28,24},{32,36},... | collective-permute-start | bytes 1179656 | tf_op jit(solution)/shard_map/ppermute | solution.py:609
  42.2 6.8 %collective-permute-start.15 = (bf16[128,384]{1,0:T(8,128)(2,1)S(1)}, bf16[128,384]{1,0:T(8,128)(2,1)S(1)}, u32[]{:S(2)}, u32[]{:S(2)}) collective-permute-start(bf16[128,384]{1,0:T(8,128)(2,1)S(1)} %get-tuple-element.83), channel_id=1, source_target_pairs={{0,32},{4,132},{8,40},{12,140},{16,48},{20,148},{24,56},{28,156},{... | collective-permute-start | bytes 294920 | tf_op jit(solution)/shard_map/ppermute | solution.py:620
  44.8 4.2 %collective-permute-start.16 = (bf16[128,384]{1,0:T(8,128)(2,1)S(1)}, bf16[128,384]{1,0:T(8,128)(2,1)S(1)}, u32[]{:S(2)}, u32[]{:S(2)}) collective-permute-start(bf16[128,384]{1,0:T(8,128)(2,1)S(1)} %get-tuple-element.84), channel_id=1, source_target_pairs={{0,48},{4,196},{8,56},{12,204},{16,0},{20,212},{24,8},{28,220},{32... | collective-permute-start | bytes 294920 | tf_op jit(solution)/shard_map/ppermute | solution.py:620
  45.6 5.0 %collective-permute-start.17 = (bf16[128,384]{1,0:T(8,128)(2,1)S(1)}, bf16[128,384]{1,0:T(8,128)(2,1)S(1)}, u32[]{:S(2)}, u32[]{:S(2)}) collective-permute-start(bf16[128,384]{1,0:T(8,128)(2,1)S(1)} %get-tuple-element.85), channel_id=1, source_target_pairs={{0,16},{4,68},{8,24},{12,76},{16,32},{20,84},{24,40},{28,92},{32,4... | collective-permute-start | bytes 294920 | tf_op jit(solution)/shard_map/ppermute | solution.py:620
  46.3 1.5 %collective-permute-start.14 = (bf16[64,512]{1,0:T(8,128)(2,1)S(1)}, bf16[64,512]{1,0:T(8,128)(2,1)S(1)}, u32[]{:S(2)}, u32[]{:S(2)}) collective-permute-start(bf16[64,512]{1,0:T(8,128)(2,1)S(1)} %get-tuple-element.86.keep), channel_id=1, source_target_pairs={{0,4},{4,0},{8,12},{12,8},{16,20},{20,16},{24,28},{28,24},{32,36},... | collective-permute-start | bytes 196616 | tf_op jit(solution)/shard_map/ppermute | solution.py:609
  50.9 2.0 %collective-permute-start.18 = (f32[128,512]{1,0:T(8,128)S(1)}, f32[128,512]{1,0:T(8,128)S(1)}, u32[]{:S(2)}, u32[]{:S(2)}) collective-permute-start(f32[128,512]{1,0:T(8,128)S(1)} %fold.1.mine), channel_id=1, source_target_pairs={{0,4},{4,0},{8,12},{12,8},{16,20},{20,16},{24,28},{28,24},{32,36},... | collective-permute-start | bytes 786440 | tf_op jit(solution)/shard_map/ppermute | solution.py:609
  (3 other events, 9.6 us)

commit v7 on v5

--- a/solution.py
+++ b/solution.py
@@ -170,8 +170,8 @@
             pltpu.SMEM((HEADS,), jnp.int32),
             pltpu.VMEM((TOK, COLS), BF16),
             pltpu.VMEM((TOK, COLS), BF16),
-            pltpu.VMEM((HEADS, TOK, DH), F32),
-            pltpu.VMEM((HEADS, TOK, DH), F32),
+            pltpu.VMEM((HEADS, TOK + R2, DH), F32),
+            pltpu.VMEM((HEADS, TOK + R2, DH), F32),
             pltpu.SemaphoreType.DMA,
             pltpu.SemaphoreType.DMA((2, BLOCKS + 1)),
         ],
@@ -228,7 +228,7 @@
         in_specs=[VMEM, HBM],
         out_specs=[VMEM] * 5,
         scratch_shapes=[pltpu.VMEM((TOK, COLS), BF16), pltpu.SemaphoreType.DMA((BLOCKS,))],
-        compiler_params=params(16),
+        compiler_params=params(58),
         cost_estimate=cost(12),
         name="queries",
     )(*args)

time: 55.2 us -> 60.7 us (1.100)
  the two profiles are of different devices: /device:TPU:1 before, /device:TPU:35 now
where the time goes in v7:
time: 60.7 us; the launch traced here: 60.4 us
  starting transfers between devices  34.6 us (57%)
  Pallas kernels  17.7 us (29%)
  waiting for transfers between devices  4.65 us (8%)
  local copies, waits for them, and re-layouts  3.06 us (5%)
    ppermute x9, starting transfers between devices, send(): return lax.ppermute(value, 'seq', moves(**shift))  16.7 us
    ppermute x9, starting transfers between devices, turn(): return lax.ppermute(value, 'seq', pairs)  9.97 us
    ppermute x1, starting transfers between devices, shards(): halo = lax.ppermute(halo, 'seq', [(s, s + 1) for s in range(1, 63, 2)])  7.91 us
    pallas_call x1, Pallas kernels, permute_queries(): pl.pallas_call(queries_kernel, out_shape=[out_of(TOK, COLS), out_of(NROWS...  3.75 us
    pallas_call x1, Pallas kernels, local(): pl.pallas_call(local_kernel, out_shape=[out_of(TOK - W0, COLS), state, st...  3.33 us
    pallas_call x1, Pallas kernels, extract(): pl.pallas_call(extract_kernel, out_shape=[out_of(8, DH, dtype=jnp.int32),...  3.16 us
    unnamed x24, local copies, waits for them, and re-layouts  3.06 us
    ppermute x1, waiting for transfers between devices, shards(): halo = lax.ppermute(halo, 'seq', [(s, s + 1) for s in range(1, 63, 2)])  2.57 us
  transfers between devices with their start and end apart: 19, of which 4 were waited for; matrix products, arithmetic and copies ran while one was open for 0% of the time, Pallas kernels for 22%

profile of v7, /device:TPU:35, one launch (start us, length us, event | category | flops | bytes accessed | tf_op | source)
XLA Modules:
  0.0 60.4 jit_solution(3086822979938451419)
XLA Ops:
  0.0 3.2 %extract.1 = (s32[8,128]{1,0:T(8,128)}, bf16[64,1024]{1,0:T(8,128)(2,1)}, bf16[192,1024]{1,0:T(8,128)(2,1)}, bf16[256,1024]{1,0:T(8,128)(2,1)}, bf16[256,1024]{1,0:T(8,128)(2,1)}) custom-call(s32[4]{0:T(128)} %off_hbm.1, bf16[1024,512]{1,0:T(8,128)(2,1)} %k.1, bf16[1024,512]{1,0:T(8,128)(2,1)} %v.1), custom_call_target="tpu_custom_call" | custom-call | bytes 1000 | tf_op jit(solution)/shard_map/extract/pallas_call | solution.py:158
  3.2 6.1 %collective-permute-start = (bf16[64,1024]{1,0:T(8,128)(2,1)}, bf16[64,1024]{1,0:T(8,128)(2,1)S(1)}, u32[]{:S(2)}, u32[]{:S(2)}) collective-permute-start(bf16[64,1024]{1,0:T(8,128)(2,1)} %get-tuple-element.49.kv_far), channel_id=1, source_target_pairs={{0,8},{4,12},{8,0},{12,4},{16,24},{20,28},{24,16},{28,20},{32,40},... | collective-permute-start | bytes 393224 | tf_op jit(solution)/shard_map/ppermute | solution.py:618
  9.3 1.0 %collective-permute-start.1 = (bf16[256,1024]{1,0:T(8,128)(2,1)}, bf16[256,1024]{1,0:T(8,128)(2,1)S(1)}, u32[]{:S(2)}, u32[]{:S(2)}) collective-permute-start(bf16[256,1024]{1,0:T(8,128)(2,1)} %get-tuple-element.68), channel_id=1, source_target_pairs={{0,4},{4,0},{8,12},{12,8},{16,20},{20,16},{24,28},{28,24},{32,36},... | collective-permute-start | bytes 1572872 | tf_op jit(solution)/shard_map/ppermute | solution.py:618
  10.2 3.7 %queries.1 = (bf16[1024,512]{1,0:T(8,128)(2,1)}, bf16[256,512]{1,0:T(8,128)(2,1)}, bf16[64,256]{1,0:T(8,128)(2,1)}, bf16[64,256]{1,0:T(8,128)(2,1)}, bf16[1024,256]{1,0:T(8,128)(2,1)}) custom-call(s32[8,128]{1,0:T(8,128)} %get-tuple-element.50.offs, bf16[1024,512]{1,0:T(8,128)(2,1)} %q_hbm.1), custom_call_target="tpu_custom_call" | custom-call | flops 12000000000 | bytes 1000 | tf_op jit(solution)/shard_map/queries/pallas_call | solution.py:219
  14.6 1.1 %collective-permute-done.2.given = bf16[64,256]{1,0:T(8,128)(2,1)S(1)} collective-permute-done((bf16[64,256]{1,0:T(8,128)(2,1)}, bf16[64,256]{1,0:T(8,128)(2,1)S(1)}, u32[]{:S(2)}, u32[]{:S(2)}) %collective-permute-start.2) | collective-permute-done | bytes 32800 | tf_op jit(solution)/shard_map/ppermute | solution.py:618
  15.7 0.8 %copy-done.9 = bf16[64,256]{1,0:T(8,128)(2,1)S(1)} copy-done((bf16[64,256]{1,0:T(8,128)(2,1)S(1)}, bf16[64,256]{1,0:T(8,128)(2,1)}, u32[]{:S(2)}) %copy-start.9) | copy-done | bytes 32792
  16.4 1.9 %collective-permute-start.3 = (bf16[128,256]{1,0:T(8,128)(2,1)S(1)}, bf16[128,256]{1,0:T(8,128)(2,1)S(1)}, u32[]{:S(2)}, u32[]{:S(2)}) collective-permute-start(bf16[128,256]{1,0:T(8,128)(2,1)S(1)} %half.1.refs_0_), channel_id=1, source_target_pairs={{0,32},{4,132},{8,40},{12,140},{16,48},{20,148},{24,56},{28,156},{... | collective-permute-start | bytes 196616 | tf_op jit(solution)/shard_map/ppermute | solution.py:629
  18.4 1.5 %collective-permute-start.5 = (bf16[128,256]{1,0:T(8,128)(2,1)S(1)}, bf16[128,256]{1,0:T(8,128)(2,1)S(1)}, u32[]{:S(2)}, u32[]{:S(2)}) collective-permute-start(bf16[128,256]{1,0:T(8,128)(2,1)S(1)} %half.1.refs_0_), channel_id=1, source_target_pairs={{0,48},{4,196},{8,56},{12,204},{16,0},{20,212},{24,8},{28,220},{32... | collective-permute-start | bytes 196616 | tf_op jit(solution)/shard_map/ppermute | solution.py:629
  19.8 1.0 %copy-done = bf16[1024,256]{1,0:T(8,128)(2,1)S(1)} copy-done((bf16[1024,256]{1,0:T(8,128)(2,1)S(1)}, bf16[1024,256]{1,0:T(8,128)(2,1)}, u32[]{:S(2)}) %copy-start) | copy-done | bytes 524312
  20.9 1.2 %copy-done.4 = bf16[1024,512]{1,0:T(8,128)(2,1)S(1)} copy-done((bf16[1024,512]{1,0:T(8,128)(2,1)S(1)}, bf16[1024,512]{1,0:T(8,128)(2,1)}, u32[]{:S(2)}) %copy-start.4) | copy-done | bytes 1048600
  22.1 3.3 %local.1 = (bf16[768,512]{1,0:T(8,128)(2,1)S(1)}, f32[448,512]{1,0:T(8,128)S(1)}, f32[448,512]{1,0:T(8,128)S(1)}, f32[448,512]{1,0:T(8,128)S(1)}) custom-call(bf16[1024,256]{1,0:T(8,128)(2,1)S(1)} %copy-done, bf16[1024,512]{1,0:T(8,128)(2,1)S(1)} %copy-done.4, bf16[1024,512]{1,0:T(8,128)(2,1)S(1)} %copy-done.2, bf16[1024,512]{1,0:T(8,128)(2,1)S(1)} %copy-done.3), custom_call_target="tpu_custom_call" | custom-call | flops 1000000000 | bytes 1000 | tf_op jit(solution)/shard_map/local/pallas_call | solution.py:350
  25.5 3.6 %collective-permute-start.7 = (bf16[64,512]{1,0:T(8,128)(2,1)S(1)}, bf16[64,512]{1,0:T(8,128)(2,1)S(1)}, u32[]{:S(2)}, u32[]{:S(2)}) collective-permute-start(bf16[64,512]{1,0:T(8,128)(2,1)S(1)} %get-tuple-element.67), channel_id=1, source_target_pairs={{0,4},{4,0},{8,12},{12,8},{16,20},{20,16},{24,28},{28,24},{32,36},... | collective-permute-start | bytes 196616 | tf_op jit(solution)/shard_map/ppermute | solution.py:618
  29.1 0.9 %collective-permute-done.7.given = bf16[64,512]{1,0:T(8,128)(2,1)S(1)} collective-permute-done((bf16[64,512]{1,0:T(8,128)(2,1)S(1)}, bf16[64,512]{1,0:T(8,128)(2,1)S(1)}, u32[]{:S(2)}, u32[]{:S(2)}) %collective-permute-start.7) | collective-permute-done | bytes 65568 | tf_op jit(solution)/shard_map/ppermute | solution.py:618
  30.4 2.5 %collective-permute-start.12 = (bf16[256,512]{1,0:T(8,128)(2,1)S(1)}, bf16[256,512]{1,0:T(8,128)(2,1)S(1)}, u32[]{:S(2)}, u32[]{:S(2)}) collective-permute-start(bf16[256,512]{1,0:T(8,128)(2,1)S(1)} %keys.1.refs_4_), channel_id=1, source_target_pairs={{0,192},{4,52},{8,200},{12,60},{16,208},{20,4},{24,216},{28,12},{3... | collective-permute-start | bytes 786440 | tf_op jit(solution)/shard_map/ppermute | solution.py:629
  32.9 7.9 %collective-permute-start.8 = (bf16[256,1024]{1,0:T(8,128)(2,1)S(1)}, bf16[256,1024]{1,0:T(8,128)(2,1)S(1)}, u32[]{:S(2)}, u32[]{:S(2)}) collective-permute-start(bf16[256,1024]{1,0:T(8,128)(2,1)S(1)} %copy-done.10), channel_id=1, source_target_pairs={{4,8},{12,16},{20,24},{28,32},{36,40},{44,48},{52,56},{60,64},{68,... | collective-permute-start | bytes 1572872 | tf_op jit(solution)/shard_map/ppermute | solution.py:651
  41.2 1.9 %far.1 = (bf16[128,384]{1,0:T(8,128)(2,1)S(1)}, bf16[128,384]{1,0:T(8,128)(2,1)S(1)}, bf16[128,384]{1,0:T(8,128)(2,1)S(1)}, bf16[128,384]{1,0:T(8,128)(2,1)S(1)}) custom-call(bf16[128,256]{1,0:T(8,128)(2,1)S(1)} %half.1.refs_0_, bf16[128,256]{1,0:T(8,128)(2,1)S(1)} %collective-permute-done.3.refs_1_, bf16[128,256]{1,0:T(8,128)(2,1)S(1)} %collective-permute-done.4.refs_2_, ...), custom_call_target="tpu_custom_call" | custom-call | bytes 1000 | tf_op jit(solution)/shard_map/far/pallas_call | solution.py:501
  43.2 2.3 %collective-permute-start.15 = (bf16[128,384]{1,0:T(8,128)(2,1)S(1)}, bf16[128,384]{1,0:T(8,128)(2,1)S(1)}, u32[]{:S(2)}, u32[]{:S(2)}) collective-permute-start(bf16[128,384]{1,0:T(8,128)(2,1)S(1)} %get-tuple-element.83), channel_id=1, source_target_pairs={{0,32},{4,132},{8,40},{12,140},{16,48},{20,148},{24,56},{28,156},{... | collective-permute-start | bytes 294920 | tf_op jit(solution)/shard_map/ppermute | solution.py:629
  45.5 1.5 %collective-permute-start.17 = (bf16[128,384]{1,0:T(8,128)(2,1)S(1)}, bf16[128,384]{1,0:T(8,128)(2,1)S(1)}, u32[]{:S(2)}, u32[]{:S(2)}) collective-permute-start(bf16[128,384]{1,0:T(8,128)(2,1)S(1)} %get-tuple-element.85), channel_id=1, source_target_pairs={{0,16},{4,68},{8,24},{12,76},{16,32},{20,84},{24,40},{28,92},{32,4... | collective-permute-start | bytes 294920 | tf_op jit(solution)/shard_map/ppermute | solution.py:629
  46.9 1.4 %near.1 = (f32[256,512]{1,0:T(8,128)S(1)}, f32[256,512]{1,0:T(8,128)S(1)}, f32[256,512]{1,0:T(8,128)S(1)}) custom-call(bf16[256,512]{1,0:T(8,128)(2,1)S(1)} %copy-done.6, f32[448,512]{1,0:T(8,128)S(1)} %get-tuple-element.59.km, f32[448,512]{1,0:T(8,128)S(1)} %get-tuple-element.60.kl, f32[448,512]{1,0:T(8,128)S(1)} %get-tuple-element.61.ka, ...), custom_call_target="tpu_custom_call" | custom-call | bytes 1000 | tf_op jit(solution)/shard_map/near/pallas_call | solution.py:424
  48.4 1.1 %across.1 = (f32[256,512]{1,0:T(8,128)S(1)}, f32[256,512]{1,0:T(8,128)S(1)}, f32[256,512]{1,0:T(8,128)S(1)}) custom-call(bf16[256,512]{1,0:T(8,128)(2,1)S(1)} %copy-done.6, f32[256,512]{1,0:T(8,128)S(1)} %get-tuple-element.73.nm, f32[256,512]{1,0:T(8,128)S(1)} %get-tuple-element.74.nl, f32[256,512]{1,0:T(8,128)S(1)} %get-tuple-element.75.na, ...), custom_call_target="tpu_custom_call" | custom-call | bytes 1000 | tf_op jit(solution)/shard_map/across/pallas_call | solution.py:457
  49.9 2.6 %collective-permute-done.8.halo = bf16[256,1024]{1,0:T(8,128)(2,1)S(1)} collective-permute-done((bf16[256,1024]{1,0:T(8,128)(2,1)S(1)}, bf16[256,1024]{1,0:T(8,128)(2,1)S(1)}, u32[]{:S(2)}, u32[]{:S(2)}) %collective-permute-start.8) | collective-permute-done | bytes 524320 | tf_op jit(solution)/shard_map/ppermute | solution.py:651
  52.5 5.2 %collective-permute-start.18 = (f32[128,512]{1,0:T(8,128)S(1)}, f32[128,512]{1,0:T(8,128)S(1)}, u32[]{:S(2)}, u32[]{:S(2)}) collective-permute-start(f32[128,512]{1,0:T(8,128)S(1)} %fold.1.mine), channel_id=1, source_target_pairs={{0,4},{4,0},{8,12},{12,8},{16,20},{20,16},{24,28},{28,24},{32,36},... | collective-permute-start | bytes 786440 | tf_op jit(solution)/shard_map/ppermute | solution.py:618
  57.7 1.2 %halo.1 = (bf16[256,512]{1,0:T(8,128)(2,1)S(1)}, f32[64,512]{1,0:T(8,128)S(1)}, f32[64,512]{1,0:T(8,128)S(1)}, f32[64,512]{1,0:T(8,128)S(1)}) custom-call(bf16[1024,256]{1,0:T(8,128)(2,1)S(1)} %copy-done.1, bf16[1024,512]{1,0:T(8,128)(2,1)S(1)} %copy-done.5, f32[448,512]{1,0:T(8,128)S(1)} %get-tuple-element.59.km, f32[448,512]{1,0:T(8,128)S(1)} %get-tuple-element.60.kl, ...), custom_call_target="tpu_custom_call" | custom-call | bytes 1000 | tf_op jit(solution)/shard_map/halo/pallas_call | solution.py:394
  58.9 1.4 %join.1 = bf16[1024,512]{1,0:T(8,128)(2,1)} custom-call(bf16[64,1024]{1,0:T(8,128)(2,1)S(1)} %collective-permute-done.far_z, bf16[1024,256]{1,0:T(8,128)(2,1)S(1)} %copy-done.1, f32[64,512]{1,0:T(8,128)S(1)} %get-tuple-element.69.hm, f32[64,512]{1,0:T(8,128)S(1)} %get-tuple-element.70.hl, f32[64,512]{1,0:T(8,128)S(1)} %get-tuple-element.71.ha, ...), custom_call_target="tpu_custom_call" | custom-call | bytes 1000 | tf_op jit(solution)/shard_map/join/pallas_call | solution.py:591
  (50 shorter events, 1.9 us)
Async XLA Ops:
  3.2 22.3 %collective-permute-start = (bf16[64,1024]{1,0:T(8,128)(2,1)}, bf16[64,1024]{1,0:T(8,128)(2,1)S(1)}, u32[]{:S(2)}, u32[]{:S(2)}) collective-permute-start(bf16[64,1024]{1,0:T(8,128)(2,1)} %get-tuple-element.49.kv_far), channel_id=1, source_target_pairs={{0,8},{4,12},{8,0},{12,4},{16,24},{20,28},{24,16},{28,20},{32,40},... | collective-permute-start | bytes 393224 | tf_op jit(solution)/shard_map/ppermute | solution.py:618
  9.3 4.7 %collective-permute-start.1 = (bf16[256,1024]{1,0:T(8,128)(2,1)}, bf16[256,1024]{1,0:T(8,128)(2,1)S(1)}, u32[]{:S(2)}, u32[]{:S(2)}) collective-permute-start(bf16[256,1024]{1,0:T(8,128)(2,1)} %get-tuple-element.68), channel_id=1, source_target_pairs={{0,4},{4,0},{8,12},{12,8},{16,20},{20,16},{24,28},{28,24},{32,36},... | collective-permute-start | bytes 1572872 | tf_op jit(solution)/shard_map/ppermute | solution.py:618
  10.2 4.4 %collective-permute-start.6 = (bf16[256,1024]{1,0:T(8,128)(2,1)}, bf16[256,1024]{1,0:T(8,128)(2,1)S(1)}, u32[]{:S(2)}, u32[]{:S(2)}) collective-permute-start(bf16[256,1024]{1,0:T(8,128)(2,1)} %get-tuple-element.64.near), channel_id=1, source_target_pairs={{0,4},{4,0},{8,12},{12,8},{16,20},{20,16},{24,28},{28,24},{32,36},... | collective-permute-start | bytes 1572872 | tf_op jit(solution)/shard_map/ppermute | solution.py:618
  10.2 9.6 %copy-start.2 = (bf16[1024,512]{1,0:T(8,128)(2,1)S(1)}, bf16[1024,512]{1,0:T(8,128)(2,1)}, u32[]{:S(2)}) copy-start(bf16[1024,512]{1,0:T(8,128)(2,1)} %k.1) | copy-start | bytes 3145732
  10.2 9.6 %copy-start.3 = (bf16[1024,512]{1,0:T(8,128)(2,1)S(1)}, bf16[1024,512]{1,0:T(8,128)(2,1)}, u32[]{:S(2)}) copy-start(bf16[1024,512]{1,0:T(8,128)(2,1)} %v.1) | copy-start | bytes 3145732
  14.0 1.7 %collective-permute-start.2 = (bf16[64,256]{1,0:T(8,128)(2,1)}, bf16[64,256]{1,0:T(8,128)(2,1)S(1)}, u32[]{:S(2)}, u32[]{:S(2)}) collective-permute-start(bf16[64,256]{1,0:T(8,128)(2,1)} %get-tuple-element.57), channel_id=1, source_target_pairs={{0,4},{4,0},{8,12},{12,8},{16,20},{20,16},{24,28},{28,24},{32,36},... | collective-permute-start | bytes 98312 | tf_op jit(solution)/shard_map/ppermute | solution.py:618
  14.6 26.2 %collective-permute-start.9 = (bf16[192,1024]{1,0:T(8,128)(2,1)S(1)}, bf16[192,1024]{1,0:T(8,128)(2,1)S(1)}, u32[]{:S(2)}, u32[]{:S(2)}) collective-permute-start(bf16[192,1024]{1,0:T(8,128)(2,1)S(1)} %copy-done.11), channel_id=1, source_target_pairs={{0,8},{4,12},{8,0},{12,4},{16,24},{20,28},{24,16},{28,20},{32,40},... | collective-permute-start | bytes 1179656 | tf_op jit(solution)/shard_map/ppermute | solution.py:618
  16.4 9.0 %collective-permute-start.3 = (bf16[128,256]{1,0:T(8,128)(2,1)S(1)}, bf16[128,256]{1,0:T(8,128)(2,1)S(1)}, u32[]{:S(2)}, u32[]{:S(2)}) collective-permute-start(bf16[128,256]{1,0:T(8,128)(2,1)S(1)} %half.1.refs_0_), channel_id=1, source_target_pairs={{0,32},{4,132},{8,40},{12,140},{16,48},{20,148},{24,56},{28,156},{... | collective-permute-start | bytes 196616 | tf_op jit(solution)/shard_map/ppermute | solution.py:629
  18.4 7.1 %collective-permute-start.4 = (bf16[128,256]{1,0:T(8,128)(2,1)S(1)}, bf16[128,256]{1,0:T(8,128)(2,1)S(1)}, u32[]{:S(2)}, u32[]{:S(2)}) collective-permute-start(bf16[128,256]{1,0:T(8,128)(2,1)S(1)} %half.1.refs_0_), channel_id=1, source_target_pairs={{0,16},{4,68},{8,24},{12,76},{16,32},{20,84},{24,40},{28,92},{32,4... | collective-permute-start | bytes 196616 | tf_op jit(solution)/shard_map/ppermute | solution.py:629
  18.4 7.1 %collective-permute-start.5 = (bf16[128,256]{1,0:T(8,128)(2,1)S(1)}, bf16[128,256]{1,0:T(8,128)(2,1)S(1)}, u32[]{:S(2)}, u32[]{:S(2)}) collective-permute-start(bf16[128,256]{1,0:T(8,128)(2,1)S(1)} %half.1.refs_0_), channel_id=1, source_target_pairs={{0,48},{4,196},{8,56},{12,204},{16,0},{20,212},{24,8},{28,220},{32... | collective-permute-start | bytes 196616 | tf_op jit(solution)/shard_map/ppermute | solution.py:629
  25.5 4.5 %collective-permute-start.7 = (bf16[64,512]{1,0:T(8,128)(2,1)S(1)}, bf16[64,512]{1,0:T(8,128)(2,1)S(1)}, u32[]{:S(2)}, u32[]{:S(2)}) collective-permute-start(bf16[64,512]{1,0:T(8,128)(2,1)S(1)} %get-tuple-element.67), channel_id=1, source_target_pairs={{0,4},{4,0},{8,12},{12,8},{16,20},{20,16},{24,28},{28,24},{32,36},... | collective-permute-start | bytes 196616 | tf_op jit(solution)/shard_map/ppermute | solution.py:618
  30.0 16.9 %copy-start.6 = (bf16[256,512]{1,0:T(8,128)(2,1)S(1)}, bf16[256,512]{1,0:T(8,128)(2,1)}, u32[]{:S(2)}) copy-start(bf16[256,512]{1,0:T(8,128)(2,1)} %get-tuple-element.72.q) | copy-start | bytes 786436
  30.0 16.9 %copy-start.7 = (bf16[256,1024]{1,0:T(8,128)(2,1)S(1)}, bf16[256,1024]{1,0:T(8,128)(2,1)}, u32[]{:S(2)}) copy-start(bf16[256,1024]{1,0:T(8,128)(2,1)} %get-tuple-element.64.near) | copy-start | bytes 1572868
  30.0 10.8 %collective-permute-start.10 = (bf16[256,512]{1,0:T(8,128)(2,1)S(1)}, bf16[256,512]{1,0:T(8,128)(2,1)S(1)}, u32[]{:S(2)}, u32[]{:S(2)}) collective-permute-start(bf16[256,512]{1,0:T(8,128)(2,1)S(1)} %keys.1.refs_4_), channel_id=1, source_target_pairs={{0,128},{4,36},{8,136},{12,44},{16,144},{20,52},{24,152},{28,60},{... | collective-permute-start | bytes 786440 | tf_op jit(solution)/shard_map/ppermute | solution.py:629
  30.1 10.7 %collective-permute-start.11 = (bf16[256,512]{1,0:T(8,128)(2,1)S(1)}, bf16[256,512]{1,0:T(8,128)(2,1)S(1)}, u32[]{:S(2)}, u32[]{:S(2)}) collective-permute-start(bf16[256,512]{1,0:T(8,128)(2,1)S(1)} %keys.1.refs_4_), channel_id=1, source_target_pairs={{0,64},{4,20},{8,72},{12,28},{16,80},{20,36},{24,88},{28,44},{32,9... | collective-permute-start | bytes 786440 | tf_op jit(solution)/shard_map/ppermute | solution.py:629
  30.4 10.4 %collective-permute-start.12 = (bf16[256,512]{1,0:T(8,128)(2,1)S(1)}, bf16[256,512]{1,0:T(8,128)(2,1)S(1)}, u32[]{:S(2)}, u32[]{:S(2)}) collective-permute-start(bf16[256,512]{1,0:T(8,128)(2,1)S(1)} %keys.1.refs_4_), channel_id=1, source_target_pairs={{0,192},{4,52},{8,200},{12,60},{16,208},{20,4},{24,216},{28,12},{3... | collective-permute-start | bytes 786440 | tf_op jit(solution)/shard_map/ppermute | solution.py:629
  32.9 19.6 %collective-permute-start.8 = (bf16[256,1024]{1,0:T(8,128)(2,1)S(1)}, bf16[256,1024]{1,0:T(8,128)(2,1)S(1)}, u32[]{:S(2)}, u32[]{:S(2)}) collective-permute-start(bf16[256,1024]{1,0:T(8,128)(2,1)S(1)} %copy-done.10), channel_id=1, source_target_pairs={{4,8},{12,16},{20,24},{28,32},{36,40},{44,48},{52,56},{60,64},{68,... | collective-permute-start | bytes 1572872 | tf_op jit(solution)/shard_map/ppermute | solution.py:651
  40.8 2.3 %collective-permute-start.13 = (bf16[192,1024]{1,0:T(8,128)(2,1)S(1)}, bf16[192,1024]{1,0:T(8,128)(2,1)S(1)}, u32[]{:S(2)}, u32[]{:S(2)}) collective-permute-start(bf16[192,1024]{1,0:T(8,128)(2,1)S(1)} %collective-permute-done.9.rest_z), channel_id=1, source_target_pairs={{0,4},{4,0},{8,12},{12,8},{16,20},{20,16},{24,28},{28,24},{32,36},... | collective-permute-start | bytes 1179656 | tf_op jit(solution)/shard_map/ppermute | solution.py:618
  43.2 6.3 %collective-permute-start.15 = (bf16[128,384]{1,0:T(8,128)(2,1)S(1)}, bf16[128,384]{1,0:T(8,128)(2,1)S(1)}, u32[]{:S(2)}, u32[]{:S(2)}) collective-permute-start(bf16[128,384]{1,0:T(8,128)(2,1)S(1)} %get-tuple-element.83), channel_id=1, source_target_pairs={{0,32},{4,132},{8,40},{12,140},{16,48},{20,148},{24,56},{28,156},{... | collective-permute-start | bytes 294920 | tf_op jit(solution)/shard_map/ppermute | solution.py:629
  45.5 4.2 %collective-permute-start.16 = (bf16[128,384]{1,0:T(8,128)(2,1)S(1)}, bf16[128,384]{1,0:T(8,128)(2,1)S(1)}, u32[]{:S(2)}, u32[]{:S(2)}) collective-permute-start(bf16[128,384]{1,0:T(8,128)(2,1)S(1)} %get-tuple-element.84), channel_id=1, source_target_pairs={{0,48},{4,196},{8,56},{12,204},{16,0},{20,212},{24,8},{28,220},{32... | collective-permute-start | bytes 294920 | tf_op jit(solution)/shard_map/ppermute | solution.py:629
  45.5 4.1 %collective-permute-start.17 = (bf16[128,384]{1,0:T(8,128)(2,1)S(1)}, bf16[128,384]{1,0:T(8,128)(2,1)S(1)}, u32[]{:S(2)}, u32[]{:S(2)}) collective-permute-start(bf16[128,384]{1,0:T(8,128)(2,1)S(1)} %get-tuple-element.85), channel_id=1, source_target_pairs={{0,16},{4,68},{8,24},{12,76},{16,32},{20,84},{24,40},{28,92},{32,4... | collective-permute-start | bytes 294920 | tf_op jit(solution)/shard_map/ppermute | solution.py:629
  46.9 1.4 %collective-permute-start.14 = (bf16[64,512]{1,0:T(8,128)(2,1)S(1)}, bf16[64,512]{1,0:T(8,128)(2,1)S(1)}, u32[]{:S(2)}, u32[]{:S(2)}) collective-permute-start(bf16[64,512]{1,0:T(8,128)(2,1)S(1)} %get-tuple-element.86.keep), channel_id=1, source_target_pairs={{0,4},{4,0},{8,12},{12,8},{16,20},{20,16},{24,28},{28,24},{32,36},... | collective-permute-start | bytes 196616 | tf_op jit(solution)/shard_map/ppermute | solution.py:618
  48.4 9.3 %copy-start.5 = (bf16[1024,512]{1,0:T(8,128)(2,1)S(1)}, bf16[1024,512]{1,0:T(8,128)(2,1)}, u32[]{:S(2)}) copy-start(bf16[1024,512]{1,0:T(8,128)(2,1)} %get-tuple-element.52.q) | copy-start | bytes 3145732
  52.5 6.4 %collective-permute-start.18 = (f32[128,512]{1,0:T(8,128)S(1)}, f32[128,512]{1,0:T(8,128)S(1)}, u32[]{:S(2)}, u32[]{:S(2)}) collective-permute-start(f32[128,512]{1,0:T(8,128)S(1)} %fold.1.mine), channel_id=1, source_target_pairs={{0,4},{4,0},{8,12},{12,8},{16,20},{20,16},{24,28},{28,24},{32,36},... | collective-permute-start | bytes 786440 | tf_op jit(solution)/shard_map/ppermute | solution.py:618
  (7 other events, 23.0 us)
